TPU v7x, 32 devices: a whole 2x2x4 slice. The times are simulated.
32 devices in a mesh: grp: 2 (over x), tm: 8 (over z, y), head: 2 (over core).
Axes of the slice: x: 2, y: 2, z: 4, core: 2. Of those that a mesh axis runs over, the one named last changes fastest.
Arguments:
- queries: bfloat16 [2048, 6144], P(('grp', 'tm'), 'head'), parts along dimension 0, may hold values from -130 to 130
- keys: bfloat16 [2048, 1024], P(('grp', 'tm'), 'head'), parts along dimension 0, may hold values from -7 to 7
- values: bfloat16 [2048, 1024], P(('grp', 'tm'), 'head'), parts along dimension 0, may hold values from -6 to 6
- span_mask: int32 [8, 4], P('grp'), parts along dimension 0, may hold values from 0 to 1, as said below
- section: int32 [8], P('grp'), parts along dimension 0, may hold values from 0 to 3
- section_gate: float32 [4, 6144], P(None, 'head'), may hold values from 0.1 to 1.9
Outputs:
- mixed: bfloat16 [2048, 6144], P(('grp', 'tm'), 'head'), parts along dimension 0
- log_total: float32 [48, 2048], P('head', ('grp', 'tm')), parts along dimension 1
There are 2 independent parts, one for each index of `grp`. A program takes and returns all parts, laid end to end along the dimension named above; an argument that names none is the same for every part. Nothing has to cross between parts.
Inputs may be any that keep to these rules, and one draw needn't show every extreme that they name: `span_mask`: the first column and the diagonal are 1 and everything above the diagonal is 0.
All inputs are finite; a program needn't handle non-finite values.
Results may differ from a plain program's by a relative error of at most 0.006.
Values may be sent and summed in bfloat16 or wider, within the bound.
No kernel may reach another device: no remote copies, remote signals or barrier semaphores. Data moves between devices by JAX's collectives and lax.ppermute only.
A program may use at most 64 MiB of HBM per device.

v0:
```python
import math

import jax
import jax.numpy as jnp
from jax import lax
from jax.experimental import pallas as pl
from jax.experimental.pallas import tpu as pltpu
from jax.sharding import PartitionSpec as P

HEAD_SIZE = 128
CH = 256
LOG2E = math.log2(math.e)
LN2 = math.log(2.0)
FAR = 1e30
SCALE = LOG2E / math.sqrt(HEAD_SIZE)
HBM = pl.BlockSpec(memory_space=pltpu.HBM)
VMEM = pl.BlockSpec(memory_space=pltpu.VMEM)


def head_columns(h):
    return slice(h * HEAD_SIZE, (h + 1) * HEAD_SIZE)


def scores_of(k, queries):
    return SCALE * lax.dot_general(k, queries, (((1,), (1,)), ((), ())), preferred_element_type=jnp.float32)


def times_values(v, weight):
    return lax.dot_general(v, weight, (((0,), (0,)), ((), ())), preferred_element_type=jnp.float32)


def floor_kernel(floor):
    floor[...] = jnp.full(floor.shape, -FAR, jnp.float32)


def own_kernel(floor, q_hbm, k_hbm, v_hbm, stacked, acc, stat, q, k, v, sems):
    copies = [
        pltpu.make_async_copy(src, dst, sems.at[i])
        for i, (src, dst) in enumerate([(q_hbm, q), (k_hbm, k), (v_hbm, v)])
    ]
    for copy in copies:
        copy.start()
    for copy in copies:
        copy.wait()
    rows = q.shape[0]
    group = stacked.shape[1] // rows
    for h in range(stacked.shape[0]):
        for g in range(group):
            stacked[h, g * rows : (g + 1) * rows, :] = q[:, head_columns(h * group + g)]
    for h in range(stacked.shape[0]):
        score = scores_of(k[:, head_columns(h)], stacked[h])
        top = jnp.maximum(floor[0:1, :], jnp.max(score, axis=0, keepdims=True))
        weight = jnp.exp2(score - top)
        stat[h, 0:1, :] = top
        stat[h, 1:2, :] = jnp.sum(weight, axis=0, keepdims=True)
        acc[h] = times_values(v[:, head_columns(h)], weight.astype(jnp.bfloat16))


def flag_kernel(per_span, mask, section, gate, seen, gate_row):
    span = lax.axis_index("tm") // per_span
    for distance in range(seen.shape[0]):
        allowed = jnp.logical_and(span >= distance, mask[span, jnp.maximum(span - distance, 0)] > 0)
        seen[distance : distance + 1, :] = jnp.full((1, seen.shape[1]), allowed.astype(jnp.int32), jnp.int32)
    gate_row[...] = gate[pl.ds(section[span], 1), :]


def weigh(h, distances, stacked, seen, stat, key_refs):
    scores = [scores_of(k[:, head_columns(h)], stacked[h]) for k in key_refs]
    flags = [seen[d : d + 1, :] > 0 for d in distances]
    old = stat[h, 0:1, :]
    top = old
    for score, flag in zip(scores, flags):
        top = jnp.maximum(top, jnp.where(flag, jnp.max(score, axis=0, keepdims=True), -FAR))
    weights = [jnp.exp2(score - jnp.where(flag, top, FAR)) for score, flag in zip(scores, flags)]
    factor = jnp.exp2(old - top)
    total = stat[h, 1:2, :] * factor
    for weight in weights:
        total += jnp.sum(weight, axis=0, keepdims=True)
    return weights, top, total, factor


def step_kernel(distances, stacked, seen, acc_in, stat_in, *refs):
    count = len(distances)
    key_refs, value_refs, (acc, stat) = refs[:count], refs[count : 2 * count], refs[2 * count :]
    for h in range(stacked.shape[0]):
        weights, top, total, factor = weigh(h, distances, stacked, seen, stat_in, key_refs)
        stat[h, 0:1, :] = top
        stat[h, 1:2, :] = total
        acc[h] = acc_in[h] * factor + times_values(
            jnp.concatenate([v[:, head_columns(h)] for v in value_refs], axis=0),
            jnp.concatenate([weight.astype(jnp.bfloat16) for weight in weights], axis=0),
        )


def close_kernel(distances, stacked, seen, gate_row, acc_in, stat_in, *refs):
    key_refs, (part, last_weight, log_ref) = refs[: len(distances)], refs[len(distances) :]
    rows = log_ref.shape[1]
    group = stacked.shape[1] // rows
    for h in range(stacked.shape[0]):
        weights, top, total, factor = weigh(h, distances, stacked, seen, stat_in, key_refs)
        inverse = 1.0 / total
        log_total = top * LN2 + jnp.log(total)
        turned = (acc_in[h] * (factor * inverse)).T
        for at, weight in enumerate(weights):
            last_weight[h, :, head_columns(at)] = (weight * inverse).T.astype(jnp.bfloat16)
        for g in range(group):
            head = h * group + g
            inside = slice(g * rows, (g + 1) * rows)
            part[h, inside, :] = turned[inside, :] * gate_row[:, head_columns(head)]
            log_ref[head : head + 1, :] = log_total[:, inside]


def mix_kernel(gate_row, part, last_weight, *refs):
    value_refs, (mixed_hbm, mixed, sems) = refs[:-3], refs[-3:]
    kv_heads, width = part.shape[0], part.shape[1]
    rows = mixed.shape[0]
    group = width // rows
    copies = []
    for h in range(kv_heads):
        values = jnp.concatenate([v[:, head_columns(h)] for v in value_refs], axis=0)
        rest = jnp.dot(last_weight[h], values, preferred_element_type=jnp.float32)
        for g in range(group):
            inside = slice(g * rows, (g + 1) * rows)
            columns = head_columns(h * group + g)
            mixed[:, columns] = (part[h, inside, :] + gate_row[:, columns] * rest[inside, :]).astype(jnp.bfloat16)
        columns = pl.ds(h * group * HEAD_SIZE, group * HEAD_SIZE)
        copies.append(pltpu.make_async_copy(mixed.at[:, columns], mixed_hbm.at[:, columns], sems.at[h]))
        copies[-1].start()
    for copy in copies:
        copy.wait()


def on_device(queries, keys, values, span_mask, section, section_gate):
    rows, wide = queries.shape
    heads, kv_heads = wide // HEAD_SIZE, keys.shape[1] // HEAD_SIZE
    width = heads // kv_heads * rows
    count = lax.axis_size("tm")
    per_span = CH // rows
    spans = count // per_span
    params = pltpu.CompilerParams(vmem_limit_bytes=24 * 1024 * 1024)
    acc_shape = jax.ShapeDtypeStruct((kv_heads, HEAD_SIZE, width), jnp.float32)
    stat_shape = jax.ShapeDtypeStruct((kv_heads, 8, width), jnp.float32)

    def cost(blocks, times=2):
        return pl.CostEstimate(
            flops=4 * times * blocks * rows * rows * wide, bytes_accessed=rows * wide * 8, transcendentals=blocks * rows * rows * heads
        )

    cores = lax.axis_size("head")

    def send(value, target):
        pairs = []
        for i in range(count):
            for core in range(cores):
                if target(i) is None:
                    goal = i * cores + (core + 1) % cores if cores > 1 else i
                else:
                    goal = target(i) * cores + core
                pairs.append((i * cores + core, goal))
        return lax.ppermute(value, ("tm", "head"), pairs)

    def onward(value, distance):
        first = (distance - 1) * per_span

        def target(i):
            if i < first:
                return None
            return i + per_span if i + per_span < count else first + i % per_span

        return send(value, target)

    def around(value, distance, turn):
        return send(
            value, lambda i: i - i % per_span + (i + turn) % per_span if i >= distance * per_span else None
        )

    def travel(held, distance, turned_before):
        onwards = [onward(x, distance + 1) for x in held] if distance + 1 < spans else []
        turned = [[around(x, distance, turn) for turn in range(1, per_span)] for x in held]
        if not onwards and turned_before:
            turned[1] = [onward(v, distance) for _, v in turned_before]
        return list(zip(*turned)), onwards

    floor = pl.pallas_call(
        floor_kernel,
        out_shape=jax.ShapeDtypeStruct((8, width), jnp.float32),
        out_specs=VMEM,
        compiler_params=params,
        cost_estimate=cost(4, 10),
        name="floor",
    )()
    held = [onward(x, 1) for x in (keys, values)] if spans > 1 else []
    near_keys, near_values, floor = lax.optimization_barrier((keys, values, floor))
    turned = list(zip(*[[around(x, 0, turn) for turn in range(1, per_span)] for x in (near_keys, near_values)]))
    stacked, acc, stat = pl.pallas_call(
        own_kernel,
        out_shape=(jax.ShapeDtypeStruct((kv_heads, width, HEAD_SIZE), jnp.bfloat16), acc_shape, stat_shape),
        in_specs=[VMEM] + [HBM] * 3,
        out_specs=(VMEM,) * 3,
        scratch_shapes=[
            pltpu.VMEM(queries.shape, queries.dtype),
            pltpu.VMEM(keys.shape, keys.dtype),
            pltpu.VMEM(values.shape, values.dtype),
            pltpu.SemaphoreType.DMA((3,)),
        ],
        compiler_params=params,
        cost_estimate=cost(1, 10),
        name="own",
    )(floor, queries, keys, values)
    for distance in range(1, spans):
        waiting = [(distance - 1, t) for t in turned] + [(distance, tuple(held))]
        forward = []
        for x in held:
            x, stat = lax.optimization_barrier((x, stat))
            forward.append(x)
        held = forward
        waiting[-1] = (distance, tuple(held))
        turned, held = travel(held, distance, turned)
        distances = [d for d, _ in waiting]

        count_in = 2 * len(waiting)
        blocks = [k for _, (k, _) in waiting] + [v for _, (_, v) in waiting]
        if distance == 1:

            def first_step(mask, section, gate, stacked, acc, stat, *refs, distances=distances):
                flag_kernel(per_span, mask, section, gate, *refs[-2:])
                step_kernel(distances, stacked, refs[-2], acc, stat, *refs[:-2])

            acc, stat, seen, gate_row = pl.pallas_call(
                first_step,
                out_shape=(
                    acc_shape, stat_shape, jax.ShapeDtypeStruct((spans, width), jnp.int32),
                    jax.ShapeDtypeStruct((1, wide), jnp.float32),
                ),
                in_specs=[pl.BlockSpec(memory_space=pltpu.SMEM)] * 2 + [VMEM] * (4 + count_in),
                out_specs=(VMEM,) * 4,
                compiler_params=params,
                cost_estimate=cost(len(waiting)),
                name="step_1",
            )(span_mask, section, section_gate, stacked, acc, stat, *blocks)
        else:

            def step(*refs, distances=distances):
                step_kernel(distances, *refs)

            acc, stat = pl.pallas_call(
                step,
                out_shape=(acc_shape, stat_shape),
                in_specs=[VMEM] * (4 + count_in),
                out_specs=(VMEM,) * 2,
                compiler_params=params,
                cost_estimate=cost(len(waiting)),
                name="step_%d" % distance,
            )(stacked, seen, acc, stat, *blocks)

    distances = [spans - 1] * len(turned)

    def close(*refs):
        close_kernel(distances, *refs)

    part, last_weight, log_total = pl.pallas_call(
        close,
        out_shape=(
            jax.ShapeDtypeStruct((kv_heads, width, HEAD_SIZE), jnp.float32),
            jax.ShapeDtypeStruct((kv_heads, width, len(turned) * rows), jnp.bfloat16),
            jax.ShapeDtypeStruct((heads, rows), jnp.float32),
        ),
        in_specs=[VMEM] * (5 + len(turned)),
        out_specs=(VMEM,) * 3,
        compiler_params=params,
        cost_estimate=cost(1),
        name="close",
    )(stacked, seen, gate_row, acc, stat, *[k for k, _ in turned])
    mixed = pl.pallas_call(
        mix_kernel,
        out_shape=jax.ShapeDtypeStruct((rows, wide), jnp.bfloat16),
        in_specs=[VMEM] * (3 + len(turned)),
        out_specs=HBM,
        scratch_shapes=[pltpu.VMEM((rows, wide), jnp.bfloat16), pltpu.SemaphoreType.DMA((kv_heads,))],
        compiler_params=params,
        cost_estimate=cost(1),
        name="mix",
    )(gate_row, part, last_weight, *[v for _, v in turned])
    return mixed, log_total


def solution(mesh):
    placed = (
        P(("grp", "tm"), "head"),
        P(("grp", "tm"), "head"),
        P(("grp", "tm"), "head"),
        P("grp", None),
        P("grp"),
        P(None, "head"),
    )
    return jax.shard_map(
        on_device,
        mesh=mesh,
        in_specs=placed,
        out_specs=(P(("grp", "tm"), "head"), P("head", ("grp", "tm"))),
        check_vma=False,
    )
```

profile of v0, /device:TPU:16, one launch (start us, length us, event | category | flops | bytes accessed | tf_op | source)
XLA Modules:
  0.0 29.4 jit_solution(9498177748718662758)
XLA Ops:
  0.6 0.0 copy-start.4
  0.6 0.0 copy-start.5
  0.6 0.0 copy-start.3
  0.7 1.6 %collective-permute-start.1 = (bf16[128,512]{1,0:T(8,128)(2,1)}, bf16[128,512]{1,0:T(8,128)(2,1)S(1)}, u32[]{:S(2)}, u32[]{:S(2)}) collective-permute-start(bf16[128,512]{1,0:T(8,128)(2,1)} %k_hbm.1), channel_id=1, source_target_pairs={{0,4},{1,5},{2,6},{3,7},{4,8},{5,9},{6,10},{7,11},{8,12},{9,13},{1... | collective-permute-start | bytes 393224 | tf_op jit(solution)/shard_map/ppermute | solution.py:160
  2.3 0.1 collective-permute-start
  2.4 0.0 copy-done.4
  2.4 0.0 copy-start
  2.4 0.0 copy-start.1
  2.4 0.0 copy-start.2
  2.4 1.7 %collective-permute-start.2 = (bf16[128,512]{1,0:T(8,128)(2,1)S(1)}, bf16[128,512]{1,0:T(8,128)(2,1)S(1)}, u32[]{:S(2)}, u32[]{:S(2)}) collective-permute-start(bf16[128,512]{1,0:T(8,128)(2,1)S(1)} %copy-done.4), channel_id=1, source_target_pairs={{0,2},{1,3},{2,0},{3,1},{4,6},{5,7},{6,4},{7,5},{8,10},{9,11},{10,... | collective-permute-start | bytes 393224 | tf_op jit(solution)/shard_map/ppermute | solution.py:160
  4.1 0.0 copy-done.5
  4.1 0.3 %collective-permute-start.3 = (bf16[128,512]{1,0:T(8,128)(2,1)S(1)}, bf16[128,512]{1,0:T(8,128)(2,1)S(1)}, u32[]{:S(2)}, u32[]{:S(2)}) collective-permute-start(bf16[128,512]{1,0:T(8,128)(2,1)S(1)} %copy-done.5), channel_id=1, source_target_pairs={{0,2},{1,3},{2,0},{3,1},{4,6},{5,7},{6,4},{7,5},{8,10},{9,11},{10,... | collective-permute-start | bytes 393224 | tf_op jit(solution)/shard_map/ppermute | solution.py:160
  4.5 0.0 copy-done.3
  4.5 1.9 %own.1 = (bf16[4,768,128]{2,1,0:T(8,128)(2,1)S(1)}, f32[4,128,768]{2,1,0:T(8,128)S(1)}, f32[4,8,768]{2,1,0:T(8,128)S(1)}) custom-call(f32[8,768]{1,0:T(8,128)S(1)} %floor.1, bf16[128,3072]{1,0:T(8,128)(2,1)S(1)} %copy-done.3, bf16[128,512]{1,0:T(8,128)(2,1)S(1)} %copy-done.4, bf16[128,512]{1,0:T(8,128)(2,1)S(1)} %copy-done.5), custom_call_target="tpu_custom_call" | custom-call | flops 2013265920 | bytes 3145728 | tf_op jit(solution)/shard_map/own/pallas_call | solution.py:195
  6.3 1.0 %collective-permute-done.1.refs_1_ = bf16[128,512]{1,0:T(8,128)(2,1)S(1)} collective-permute-done((bf16[128,512]{1,0:T(8,128)(2,1)}, bf16[128,512]{1,0:T(8,128)(2,1)S(1)}, u32[]{:S(2)}, u32[]{:S(2)}) %collective-permute-start.1) | collective-permute-done | bytes 131104 | tf_op jit(solution)/shard_map/ppermute | solution.py:160
  7.3 1.6 %collective-permute-start.5 = (bf16[128,512]{1,0:T(8,128)(2,1)S(1)}, bf16[128,512]{1,0:T(8,128)(2,1)S(1)}, u32[]{:S(2)}, u32[]{:S(2)}) collective-permute-start(bf16[128,512]{1,0:T(8,128)(2,1)S(1)} %collective-permute-done.1.refs_1_), channel_id=1, source_target_pairs={{0,1},{1,0},{2,3},{3,2},{4,8},{5,9},{6,10},{7,11},{8,12},{9,13},{1... | collective-permute-start | bytes 393224 | tf_op jit(solution)/shard_map/ppermute | solution.py:160
  8.9 1.0 %collective-permute-done.refs_3_ = bf16[128,512]{1,0:T(8,128)(2,1)S(1)} collective-permute-done((bf16[128,512]{1,0:T(8,128)(2,1)}, bf16[128,512]{1,0:T(8,128)(2,1)S(1)}, u32[]{:S(2)}, u32[]{:S(2)}) %collective-permute-start) | collective-permute-done | bytes 131104 | tf_op jit(solution)/shard_map/ppermute | solution.py:160
  9.9 1.7 %collective-permute-start.4 = (bf16[128,512]{1,0:T(8,128)(2,1)S(1)}, bf16[128,512]{1,0:T(8,128)(2,1)S(1)}, u32[]{:S(2)}, u32[]{:S(2)}) collective-permute-start(bf16[128,512]{1,0:T(8,128)(2,1)S(1)} %collective-permute-done.refs_3_), channel_id=1, source_target_pairs={{0,1},{1,0},{2,3},{3,2},{4,8},{5,9},{6,10},{7,11},{8,12},{9,13},{1... | collective-permute-start | bytes 393224 | tf_op jit(solution)/shard_map/ppermute | solution.py:160
  11.6 1.5 %collective-permute-start.7 = (bf16[128,512]{1,0:T(8,128)(2,1)S(1)}, bf16[128,512]{1,0:T(8,128)(2,1)S(1)}, u32[]{:S(2)}, u32[]{:S(2)}) collective-permute-start(bf16[128,512]{1,0:T(8,128)(2,1)S(1)} %collective-permute-done.refs_3_), channel_id=1, source_target_pairs={{0,1},{1,0},{2,3},{3,2},{4,6},{5,7},{6,4},{7,5},{8,10},{9,11},{10,... | collective-permute-start | bytes 393224 | tf_op jit(solution)/shard_map/ppermute | solution.py:160
  13.1 0.0 collective-permute-done.2.refs_0_
  13.1 0.5 %collective-permute-start.6 = (bf16[128,512]{1,0:T(8,128)(2,1)S(1)}, bf16[128,512]{1,0:T(8,128)(2,1)S(1)}, u32[]{:S(2)}, u32[]{:S(2)}) collective-permute-start(bf16[128,512]{1,0:T(8,128)(2,1)S(1)} %collective-permute-done.1.refs_1_), channel_id=1, source_target_pairs={{0,1},{1,0},{2,3},{3,2},{4,6},{5,7},{6,4},{7,5},{8,10},{9,11},{10,... | collective-permute-start | bytes 393224 | tf_op jit(solution)/shard_map/ppermute | solution.py:160
  13.6 0.0 collective-permute-done.3.refs_2_
  13.6 0.0 copy-done
  13.6 0.0 copy-done.1
  13.6 0.0 copy-done.2
  13.6 2.4 %step_1.1 = (f32[4,128,768]{2,1,0:T(8,128)S(1)}, f32[4,8,768]{2,1,0:T(8,128)S(1)}, s32[4,768]{1,0:T(4,128)S(1)}, f32[1,3072]{1,0:T(1,128)S(1)}) custom-call(s32[4,4]{1,0:T(4,128)S(1)} %copy-done.1, s32[4]{0:T(128)S(1)} %copy-done.2, f32[4,3072]{1,0:T(4,128)S(1)} %copy-done, bf16[4,768,128]{2,1,0:T(8,128)(2,1)S(1)} %get-tuple-element.32.stacked.refs_0_, ...), custom_call_target="tpu_custom_call" | custom-call | flops 805306368 | bytes 3145728 | tf_op jit(solution)/shard_map/step_1/pallas_call | solution.py:229
  16.1 0.0 collective-permute-done.5.refs_5_
  16.1 0.1 collective-permute-start.9
  16.2 0.0 collective-permute-done.4.refs_7_
  16.2 1.6 %collective-permute-start.11 = (bf16[128,512]{1,0:T(8,128)(2,1)S(1)}, bf16[128,512]{1,0:T(8,128)(2,1)S(1)}, u32[]{:S(2)}, u32[]{:S(2)}) collective-permute-start(bf16[128,512]{1,0:T(8,128)(2,1)S(1)} %collective-permute-done.4.refs_7_), channel_id=1, source_target_pairs={{0,1},{1,0},{2,3},{3,2},{4,5},{5,4},{6,7},{7,6},{8,10},{9,11},{10,... | collective-permute-start | bytes 393224 | tf_op jit(solution)/shard_map/ppermute | solution.py:160
  17.8 1.9 %collective-permute-start.8 = (bf16[128,512]{1,0:T(8,128)(2,1)S(1)}, bf16[128,512]{1,0:T(8,128)(2,1)S(1)}, u32[]{:S(2)}, u32[]{:S(2)}) collective-permute-start(bf16[128,512]{1,0:T(8,128)(2,1)S(1)} %collective-permute-done.4.refs_7_), channel_id=1, source_target_pairs={{0,1},{1,0},{2,3},{3,2},{4,5},{5,4},{6,7},{7,6},{8,12},{9,13},{10,... | collective-permute-start | bytes 393224 | tf_op jit(solution)/shard_map/ppermute | solution.py:160
  19.7 0.0 collective-permute-done.7.refs_6_
  19.7 0.5 %collective-permute-start.10 = (bf16[128,512]{1,0:T(8,128)(2,1)S(1)}, bf16[128,512]{1,0:T(8,128)(2,1)S(1)}, u32[]{:S(2)}, u32[]{:S(2)}) collective-permute-start(bf16[128,512]{1,0:T(8,128)(2,1)S(1)} %collective-permute-done.5.refs_5_), channel_id=1, source_target_pairs={{0,1},{1,0},{2,3},{3,2},{4,5},{5,4},{6,7},{7,6},{8,10},{9,11},{10,... | collective-permute-start | bytes 393224 | tf_op jit(solution)/shard_map/ppermute | solution.py:160
  20.2 0.0 collective-permute-done.6.refs_4_
  20.2 1.9 %step_2.1 = (f32[4,128,768]{2,1,0:T(8,128)S(1)}, f32[4,8,768]{2,1,0:T(8,128)S(1)}) custom-call(bf16[4,768,128]{2,1,0:T(8,128)(2,1)S(1)} %get-tuple-element.32.stacked.refs_0_, s32[4,768]{1,0:T(4,128)S(1)} %get-tuple-element.42.refs_1_, f32[4,128,768]{2,1,0:T(8,128)S(1)} %get-tuple-element.43.refs_2_, f32[4,8,768]{2,1,0:T(8,128)S(1)} %get-tuple-element.46.refs_3_, ...), custom_call_target="tpu_custom_call" | custom-call | flops 805306368 | bytes 3145728 | tf_op jit(solution)/shard_map/step_2/pallas_call | solution.py:246
  22.1 0.0 collective-permute-done.9.refs_5_
  22.1 0.1 collective-permute-start.12
  22.2 0.0 collective-permute-done.11.refs_6_
  22.2 1.7 %collective-permute-start.13 = (bf16[128,512]{1,0:T(8,128)(2,1)S(1)}, bf16[128,512]{1,0:T(8,128)(2,1)S(1)}, u32[]{:S(2)}, u32[]{:S(2)}) collective-permute-start(bf16[128,512]{1,0:T(8,128)(2,1)S(1)} %collective-permute-done.11.refs_6_), channel_id=1, source_target_pairs={{0,1},{1,0},{2,3},{3,2},{4,5},{5,4},{6,7},{7,6},{8,12},{9,13},{10,... | collective-permute-start | bytes 393224 | tf_op jit(solution)/shard_map/ppermute | solution.py:160
  23.9 0.0 collective-permute-done.8.refs_7_
  23.9 0.8 %collective-permute-done.10.refs_4_ = bf16[128,512]{1,0:T(8,128)(2,1)S(1)} collective-permute-done((bf16[128,512]{1,0:T(8,128)(2,1)S(1)}, bf16[128,512]{1,0:T(8,128)(2,1)S(1)}, u32[]{:S(2)}, u32[]{:S(2)}) %collective-permute-start.10) | collective-permute-done | bytes 131104 | tf_op jit(solution)/shard_map/ppermute | solution.py:160
  24.7 1.9 %step_3.1 = (f32[4,128,768]{2,1,0:T(8,128)S(1)}, f32[4,8,768]{2,1,0:T(8,128)S(1)}) custom-call(bf16[4,768,128]{2,1,0:T(8,128)(2,1)S(1)} %get-tuple-element.32.stacked.refs_0_, s32[4,768]{1,0:T(4,128)S(1)} %get-tuple-element.42.refs_1_, f32[4,128,768]{2,1,0:T(8,128)S(1)} %get-tuple-element.49.refs_2_, f32[4,8,768]{2,1,0:T(8,128)S(1)} %get-tuple-element.52.refs_3_, ...), custom_call_target="tpu_custom_call" | custom-call | flops 805306368 | bytes 3145728 | tf_op jit(solution)/shard_map/step_3/pallas_call | solution.py:246
  26.6 0.0 collective-permute-done.12.refs_5_
  26.6 1.7 %close.1 = (f32[4,768,128]{2,1,0:T(8,128)S(1)}, bf16[4,768,128]{2,1,0:T(8,128)(2,1)S(1)}, f32[24,128]{1,0:T(8,128)}) custom-call(bf16[4,768,128]{2,1,0:T(8,128)(2,1)S(1)} %get-tuple-element.32.stacked.refs_0_, s32[4,768]{1,0:T(4,128)S(1)} %get-tuple-element.42.refs_1_, f32[1,3072]{1,0:T(1,128)S(1)} %get-tuple-element.41.refs_2_.gate_row, ...), custom_call_target="tpu_custom_call" | custom-call | flops 402653184 | bytes 3145728 | tf_op jit(solution)/shard_map/close/pallas_call | solution.py:261
  28.3 0.0 collective-permute-done.13.refs_0_
  28.3 1.2 %mix.1 = bf16[128,3072]{1,0:T(8,128)(2,1)} custom-call(f32[1,3072]{1,0:T(1,128)S(1)} %get-tuple-element.41.refs_2_.gate_row, f32[4,768,128]{2,1,0:T(8,128)S(1)} %get-tuple-element.57.part, bf16[4,768,128]{2,1,0:T(8,128)(2,1)S(1)} %get-tuple-element.58.last_weight, bf16[128,512]{1,0:T(8,128)(2,1)S(1)} %collective-permute-done.13.refs_0_), custom_call_target="tpu_custom_call" | custom-call | flops 402653184 | bytes 3145728 | tf_op jit(solution)/shard_map/mix/pallas_call | solution.py:274
  (1 shorter events, 0.0 us)
Async XLA Ops:
  0.6 1.7 %copy-start.4 = (bf16[128,512]{1,0:T(8,128)(2,1)S(1)}, bf16[128,512]{1,0:T(8,128)(2,1)}, u32[]{:S(2)}) copy-start(bf16[128,512]{1,0:T(8,128)(2,1)} %k_hbm.1) | copy-start | bytes 393220
  0.6 3.5 %copy-start.5 = (bf16[128,512]{1,0:T(8,128)(2,1)S(1)}, bf16[128,512]{1,0:T(8,128)(2,1)}, u32[]{:S(2)}) copy-start(bf16[128,512]{1,0:T(8,128)(2,1)} %v_hbm.1) | copy-start | bytes 393220
  0.6 3.8 %copy-start.3 = (bf16[128,3072]{1,0:T(8,128)(2,1)S(1)}, bf16[128,3072]{1,0:T(8,128)(2,1)}, u32[]{:S(2)}) copy-start(bf16[128,3072]{1,0:T(8,128)(2,1)} %q_hbm.1) | copy-start | bytes 2359300
  0.7 6.6 %collective-permute-start.1 = (bf16[128,512]{1,0:T(8,128)(2,1)}, bf16[128,512]{1,0:T(8,128)(2,1)S(1)}, u32[]{:S(2)}, u32[]{:S(2)}) collective-permute-start(bf16[128,512]{1,0:T(8,128)(2,1)} %k_hbm.1), channel_id=1, source_target_pairs={{0,4},{1,5},{2,6},{3,7},{4,8},{5,9},{6,10},{7,11},{8,12},{9,13},{1... | collective-permute-start | bytes 393224 | tf_op jit(solution)/shard_map/ppermute | solution.py:160
  2.3 7.6 %collective-permute-start = (bf16[128,512]{1,0:T(8,128)(2,1)}, bf16[128,512]{1,0:T(8,128)(2,1)S(1)}, u32[]{:S(2)}, u32[]{:S(2)}) collective-permute-start(bf16[128,512]{1,0:T(8,128)(2,1)} %v_hbm.1), channel_id=1, source_target_pairs={{0,4},{1,5},{2,6},{3,7},{4,8},{5,9},{6,10},{7,11},{8,12},{9,13},{1... | collective-permute-start | bytes 393224 | tf_op jit(solution)/shard_map/ppermute | solution.py:160
  2.4 11.3 %copy-start = (f32[4,3072]{1,0:T(4,128)S(1)}, f32[4,3072]{1,0:T(4,128)}, u32[]{:S(2)}) copy-start(f32[4,3072]{1,0:T(4,128)} %gate.1) | copy-start | bytes 147460
  2.4 11.3 %copy-start.1 = (s32[4,4]{1,0:T(4,128)S(1)}, s32[4,4]{1,0:T(4,128)}, u32[]{:S(2)}) copy-start(s32[4,4]{1,0:T(4,128)} %mask.1) | copy-start | bytes 196
  2.4 11.3 %copy-start.2 = (s32[4]{0:T(128)S(1)}, s32[4]{0:T(128)}, u32[]{:S(2)}) copy-start(s32[4]{0:T(128)} %section.1) | copy-start | bytes 52
  2.4 10.7 %collective-permute-start.2 = (bf16[128,512]{1,0:T(8,128)(2,1)S(1)}, bf16[128,512]{1,0:T(8,128)(2,1)S(1)}, u32[]{:S(2)}, u32[]{:S(2)}) collective-permute-start(bf16[128,512]{1,0:T(8,128)(2,1)S(1)} %copy-done.4), channel_id=1, source_target_pairs={{0,2},{1,3},{2,0},{3,1},{4,6},{5,7},{6,4},{7,5},{8,10},{9,11},{10,... | collective-permute-start | bytes 393224 | tf_op jit(solution)/shard_map/ppermute | solution.py:160
  4.1 9.5 %collective-permute-start.3 = (bf16[128,512]{1,0:T(8,128)(2,1)S(1)}, bf16[128,512]{1,0:T(8,128)(2,1)S(1)}, u32[]{:S(2)}, u32[]{:S(2)}) collective-permute-start(bf16[128,512]{1,0:T(8,128)(2,1)S(1)} %copy-done.5), channel_id=1, source_target_pairs={{0,2},{1,3},{2,0},{3,1},{4,6},{5,7},{6,4},{7,5},{8,10},{9,11},{10,... | collective-permute-start | bytes 393224 | tf_op jit(solution)/shard_map/ppermute | solution.py:160
  7.3 8.8 %collective-permute-start.5 = (bf16[128,512]{1,0:T(8,128)(2,1)S(1)}, bf16[128,512]{1,0:T(8,128)(2,1)S(1)}, u32[]{:S(2)}, u32[]{:S(2)}) collective-permute-start(bf16[128,512]{1,0:T(8,128)(2,1)S(1)} %collective-permute-done.1.refs_1_), channel_id=1, source_target_pairs={{0,1},{1,0},{2,3},{3,2},{4,8},{5,9},{6,10},{7,11},{8,12},{9,13},{1... | collective-permute-start | bytes 393224 | tf_op jit(solution)/shard_map/ppermute | solution.py:160
  9.9 6.3 %collective-permute-start.4 = (bf16[128,512]{1,0:T(8,128)(2,1)S(1)}, bf16[128,512]{1,0:T(8,128)(2,1)S(1)}, u32[]{:S(2)}, u32[]{:S(2)}) collective-permute-start(bf16[128,512]{1,0:T(8,128)(2,1)S(1)} %collective-permute-done.refs_3_), channel_id=1, source_target_pairs={{0,1},{1,0},{2,3},{3,2},{4,8},{5,9},{6,10},{7,11},{8,12},{9,13},{1... | collective-permute-start | bytes 393224 | tf_op jit(solution)/shard_map/ppermute | solution.py:160
  11.6 8.1 %collective-permute-start.7 = (bf16[128,512]{1,0:T(8,128)(2,1)S(1)}, bf16[128,512]{1,0:T(8,128)(2,1)S(1)}, u32[]{:S(2)}, u32[]{:S(2)}) collective-permute-start(bf16[128,512]{1,0:T(8,128)(2,1)S(1)} %collective-permute-done.refs_3_), channel_id=1, source_target_pairs={{0,1},{1,0},{2,3},{3,2},{4,6},{5,7},{6,4},{7,5},{8,10},{9,11},{10,... | collective-permute-start | bytes 393224 | tf_op jit(solution)/shard_map/ppermute | solution.py:160
  13.1 7.1 %collective-permute-start.6 = (bf16[128,512]{1,0:T(8,128)(2,1)S(1)}, bf16[128,512]{1,0:T(8,128)(2,1)S(1)}, u32[]{:S(2)}, u32[]{:S(2)}) collective-permute-start(bf16[128,512]{1,0:T(8,128)(2,1)S(1)} %collective-permute-done.1.refs_1_), channel_id=1, source_target_pairs={{0,1},{1,0},{2,3},{3,2},{4,6},{5,7},{6,4},{7,5},{8,10},{9,11},{10,... | collective-permute-start | bytes 393224 | tf_op jit(solution)/shard_map/ppermute | solution.py:160
  16.1 6.0 %collective-permute-start.9 = (bf16[128,512]{1,0:T(8,128)(2,1)S(1)}, bf16[128,512]{1,0:T(8,128)(2,1)S(1)}, u32[]{:S(2)}, u32[]{:S(2)}) collective-permute-start(bf16[128,512]{1,0:T(8,128)(2,1)S(1)} %collective-permute-done.5.refs_5_), channel_id=1, source_target_pairs={{0,1},{1,0},{2,3},{3,2},{4,5},{5,4},{6,7},{7,6},{8,12},{9,13},{10,... | collective-permute-start | bytes 393224 | tf_op jit(solution)/shard_map/ppermute | solution.py:160
  16.2 6.0 %collective-permute-start.11 = (bf16[128,512]{1,0:T(8,128)(2,1)S(1)}, bf16[128,512]{1,0:T(8,128)(2,1)S(1)}, u32[]{:S(2)}, u32[]{:S(2)}) collective-permute-start(bf16[128,512]{1,0:T(8,128)(2,1)S(1)} %collective-permute-done.4.refs_7_), channel_id=1, source_target_pairs={{0,1},{1,0},{2,3},{3,2},{4,5},{5,4},{6,7},{7,6},{8,10},{9,11},{10,... | collective-permute-start | bytes 393224 | tf_op jit(solution)/shard_map/ppermute | solution.py:160
  17.8 6.2 %collective-permute-start.8 = (bf16[128,512]{1,0:T(8,128)(2,1)S(1)}, bf16[128,512]{1,0:T(8,128)(2,1)S(1)}, u32[]{:S(2)}, u32[]{:S(2)}) collective-permute-start(bf16[128,512]{1,0:T(8,128)(2,1)S(1)} %collective-permute-done.4.refs_7_), channel_id=1, source_target_pairs={{0,1},{1,0},{2,3},{3,2},{4,5},{5,4},{6,7},{7,6},{8,12},{9,13},{10,... | collective-permute-start | bytes 393224 | tf_op jit(solution)/shard_map/ppermute | solution.py:160
  19.7 5.0 %collective-permute-start.10 = (bf16[128,512]{1,0:T(8,128)(2,1)S(1)}, bf16[128,512]{1,0:T(8,128)(2,1)S(1)}, u32[]{:S(2)}, u32[]{:S(2)}) collective-permute-start(bf16[128,512]{1,0:T(8,128)(2,1)S(1)} %collective-permute-done.5.refs_5_), channel_id=1, source_target_pairs={{0,1},{1,0},{2,3},{3,2},{4,5},{5,4},{6,7},{7,6},{8,10},{9,11},{10,... | collective-permute-start | bytes 393224 | tf_op jit(solution)/shard_map/ppermute | solution.py:160
  22.1 4.5 %collective-permute-start.12 = (bf16[128,512]{1,0:T(8,128)(2,1)S(1)}, bf16[128,512]{1,0:T(8,128)(2,1)S(1)}, u32[]{:S(2)}, u32[]{:S(2)}) collective-permute-start(bf16[128,512]{1,0:T(8,128)(2,1)S(1)} %collective-permute-done.9.refs_5_), channel_id=1, source_target_pairs={{0,1},{1,0},{2,3},{3,2},{4,5},{5,4},{6,7},{7,6},{8,9},{9,8},{10,11... | collective-permute-start | bytes 393224 | tf_op jit(solution)/shard_map/ppermute | solution.py:160
  22.2 6.1 %collective-permute-start.13 = (bf16[128,512]{1,0:T(8,128)(2,1)S(1)}, bf16[128,512]{1,0:T(8,128)(2,1)S(1)}, u32[]{:S(2)}, u32[]{:S(2)}) collective-permute-start(bf16[128,512]{1,0:T(8,128)(2,1)S(1)} %collective-permute-done.11.refs_6_), channel_id=1, source_target_pairs={{0,1},{1,0},{2,3},{3,2},{4,5},{5,4},{6,7},{7,6},{8,12},{9,13},{10,... | collective-permute-start | bytes 393224 | tf_op jit(solution)/shard_map/ppermute | solution.py:160
where the time goes:
time: 29.6 us; the launch traced here: 29.4 us
  starting transfers between devices  15 us (51%)
  Pallas kernels  10.9 us (37%)
  waiting for transfers between devices  2.74 us (9%)
  between operations  0.78 us (3%)
    ppermute x14, starting transfers between devices, send(): return lax.ppermute(value, ('tm', 'head'), pairs)  15 us
    pallas_call x2, Pallas kernels, on_device(): pl.pallas_call(step, out_shape=(acc_shape, stat_shape), in_specs=[VMEM] *...  3.75 us
    ppermute x14, waiting for transfers between devices, send(): return lax.ppermute(value, ('tm', 'head'), pairs)  2.74 us
    pallas_call x1, Pallas kernels, on_device(): pl.pallas_call(first_step, out_shape=(acc_shape, stat_shape, jax.ShapeDty...  2.44 us
    pallas_call x1, Pallas kernels, on_device(): pl.pallas_call(own_kernel, out_shape=(jax.ShapeDtypeStruct((kv_heads, wid...  1.86 us
    pallas_call x1, Pallas kernels, on_device(): pl.pallas_call(close, out_shape=(jax.ShapeDtypeStruct((kv_heads, width, H...  1.69 us
    pallas_call x1, Pallas kernels, on_device(): pl.pallas_call(mix_kernel, out_shape=jax.ShapeDtypeStruct((rows, wide), j...  1.16 us
  transfers between devices with their start and end apart: 14, of which 3 were waited for; matrix products, arithmetic and copies ran while one was open for 0% of the time, Pallas kernels for 33%

commit v1 on v0

--- a/solution.py
+++ b/solution.py
@@ -12,6 +12,7 @@
 LOG2E = math.log2(math.e)
 LN2 = math.log(2.0)
 FAR = 1e30
+LIMIT = 2.0**80
 SCALE = LOG2E / math.sqrt(HEAD_SIZE)
 HBM = pl.BlockSpec(memory_space=pltpu.HBM)
 VMEM = pl.BlockSpec(memory_space=pltpu.VMEM)
@@ -22,7 +23,7 @@
 
 
 def scores_of(k, queries):
-    return SCALE * lax.dot_general(k, queries, (((1,), (1,)), ((), ())), preferred_element_type=jnp.float32)
+    return lax.dot_general(k, queries, (((1,), (1,)), ((), ())), preferred_element_type=jnp.float32)
 
 
 def times_values(v, weight):
@@ -33,13 +34,19 @@
     floor[...] = jnp.full(floor.shape, -FAR, jnp.float32)
 
 
-def own_kernel(floor, q_hbm, k_hbm, v_hbm, stacked, acc, stat, q, k, v, sems):
+def own_kernel(per_span, mask, section, gate, floor, q_hbm, k_hbm, v_hbm,
+               stacked, seen, gate_row, acc, stat, q, k, v, sems):
     copies = [
         pltpu.make_async_copy(src, dst, sems.at[i])
         for i, (src, dst) in enumerate([(q_hbm, q), (k_hbm, k), (v_hbm, v)])
     ]
     for copy in copies:
         copy.start()
+    span = lax.axis_index("tm") // per_span
+    for distance in range(seen.shape[0]):
+        allowed = jnp.logical_and(span >= distance, mask[span, jnp.maximum(span - distance, 0)] > 0)
+        seen[distance : distance + 1, :] = jnp.full((1, seen.shape[1]), allowed.astype(jnp.int32), jnp.int32)
+    gate_row[...] = gate[pl.ds(section[span], 1), :]
     for copy in copies:
         copy.wait()
     rows = q.shape[0]
@@ -48,7 +55,7 @@
         for g in range(group):
             stacked[h, g * rows : (g + 1) * rows, :] = q[:, head_columns(h * group + g)]
     for h in range(stacked.shape[0]):
-        score = scores_of(k[:, head_columns(h)], stacked[h])
+        score = SCALE * scores_of(k[:, head_columns(h)], stacked[h])
         top = jnp.maximum(floor[0:1, :], jnp.max(score, axis=0, keepdims=True))
         weight = jnp.exp2(score - top)
         stat[h, 0:1, :] = top
@@ -56,58 +63,88 @@
         acc[h] = times_values(v[:, head_columns(h)], weight.astype(jnp.bfloat16))
 
 
-def flag_kernel(per_span, mask, section, gate, seen, gate_row):
-    span = lax.axis_index("tm") // per_span
-    for distance in range(seen.shape[0]):
-        allowed = jnp.logical_and(span >= distance, mask[span, jnp.maximum(span - distance, 0)] > 0)
-        seen[distance : distance + 1, :] = jnp.full((1, seen.shape[1]), allowed.astype(jnp.int32), jnp.int32)
-    gate_row[...] = gate[pl.ds(section[span], 1), :]
-
-
-def weigh(h, distances, stacked, seen, stat, key_refs):
-    scores = [scores_of(k[:, head_columns(h)], stacked[h]) for k in key_refs]
-    flags = [seen[d : d + 1, :] > 0 for d in distances]
-    old = stat[h, 0:1, :]
+def chunks_of(width):
+    size = 256 if width % 256 == 0 else width
+    return [slice(at, at + size) for at in range(0, width, size)]
+
+
+def weigh(exact, h, inside, distances, stacked, seen, stat, key_refs):
+    scores = [scores_of(k[:, head_columns(h)], stacked[h, inside, :]) for k in key_refs]
+    flags = [seen[d : d + 1, inside] > 0 for d in distances]
+    old = stat[h, 0:1, inside]
     top = old
-    for score, flag in zip(scores, flags):
-        top = jnp.maximum(top, jnp.where(flag, jnp.max(score, axis=0, keepdims=True), -FAR))
-    weights = [jnp.exp2(score - jnp.where(flag, top, FAR)) for score, flag in zip(scores, flags)]
-    factor = jnp.exp2(old - top)
-    total = stat[h, 1:2, :] * factor
+    if exact:
+        for score, flag in zip(scores, flags):
+            top = jnp.maximum(top, jnp.where(flag, SCALE * jnp.max(score, axis=0, keepdims=True), -FAR))
+    weights = [jnp.exp2(SCALE * score - jnp.where(flag, top, FAR)) for score, flag in zip(scores, flags)]
+    factor = jnp.exp2(old - top) if exact else None
+    total = stat[h, 1:2, inside]
+    if exact:
+        total *= factor
     for weight in weights:
         total += jnp.sum(weight, axis=0, keepdims=True)
     return weights, top, total, factor
 
 
+def with_check(work):
+    largest = None
+    within = None
+    for total in work(False):
+        fits = jnp.where(total <= LIMIT, 0.0, 1.0)
+        within = fits if within is None else within + fits
+    largest = jnp.max(within)
+
+    @pl.when(largest > 0.0)
+    def _():
+        work(True)
+
+
 def step_kernel(distances, stacked, seen, acc_in, stat_in, *refs):
     count = len(distances)
     key_refs, value_refs, (acc, stat) = refs[:count], refs[count : 2 * count], refs[2 * count :]
-    for h in range(stacked.shape[0]):
-        weights, top, total, factor = weigh(h, distances, stacked, seen, stat_in, key_refs)
-        stat[h, 0:1, :] = top
-        stat[h, 1:2, :] = total
-        acc[h] = acc_in[h] * factor + times_values(
-            jnp.concatenate([v[:, head_columns(h)] for v in value_refs], axis=0),
-            jnp.concatenate([weight.astype(jnp.bfloat16) for weight in weights], axis=0),
-        )
+
+    def work(exact):
+        totals = []
+        for h in range(stacked.shape[0]):
+            values = jnp.concatenate([v[:, head_columns(h)] for v in value_refs], axis=0)
+            for inside in chunks_of(stacked.shape[1]):
+                weights, top, total, factor = weigh(exact, h, inside, distances, stacked, seen, stat_in, key_refs)
+                stat[h, 0:1, inside] = top
+                stat[h, 1:2, inside] = total
+                state = acc_in[h, :, inside] * factor if exact else acc_in[h, :, inside]
+                acc[h, :, inside] = state + times_values(
+                    values, jnp.concatenate([weight.astype(jnp.bfloat16) for weight in weights], axis=0)
+                )
+                totals.append(total)
+        return totals
+
+    with_check(work)
 
 
 def close_kernel(distances, stacked, seen, gate_row, acc_in, stat_in, *refs):
     key_refs, (part, last_weight, log_ref) = refs[: len(distances)], refs[len(distances) :]
     rows = log_ref.shape[1]
-    group = stacked.shape[1] // rows
-    for h in range(stacked.shape[0]):
-        weights, top, total, factor = weigh(h, distances, stacked, seen, stat_in, key_refs)
-        inverse = 1.0 / total
-        log_total = top * LN2 + jnp.log(total)
-        turned = (acc_in[h] * (factor * inverse)).T
-        for at, weight in enumerate(weights):
-            last_weight[h, :, head_columns(at)] = (weight * inverse).T.astype(jnp.bfloat16)
-        for g in range(group):
-            head = h * group + g
-            inside = slice(g * rows, (g + 1) * rows)
-            part[h, inside, :] = turned[inside, :] * gate_row[:, head_columns(head)]
-            log_ref[head : head + 1, :] = log_total[:, inside]
+
+    def work(exact):
+        totals = []
+        for h in range(stacked.shape[0]):
+            for inside in chunks_of(stacked.shape[1]):
+                weights, top, total, factor = weigh(exact, h, inside, distances, stacked, seen, stat_in, key_refs)
+                inverse = 1.0 / total
+                log_total = top * LN2 + jnp.log(total)
+                turned = (acc_in[h, :, inside] * (factor * inverse if exact else inverse)).T
+                for at, weight in enumerate(weights):
+                    last_weight[h, inside, head_columns(at)] = (weight * inverse).T.astype(jnp.bfloat16)
+                for at in range(0, turned.shape[0], rows):
+                    head = (h * stacked.shape[1] + inside.start + at) // rows
+                    part[h, inside.start + at : inside.start + at + rows, :] = (
+                        turned[at : at + rows, :] * gate_row[:, head_columns(head)]
+                    )
+                    log_ref[head : head + 1, :] = log_total[:, at : at + rows]
+                totals.append(total)
+        return totals
+
+    with_check(work)
 
 
 def mix_kernel(gate_row, part, last_weight, *refs):
@@ -160,7 +197,7 @@
         return lax.ppermute(value, ("tm", "head"), pairs)
 
     def onward(value, distance):
-        first = (distance - 1) * per_span
+        first = (max(min(distance - 1, spans - 3), 0) if distance > 1 else 0) * per_span
 
         def target(i):
             if i < first:
@@ -192,11 +229,20 @@
     held = [onward(x, 1) for x in (keys, values)] if spans > 1 else []
     near_keys, near_values, floor = lax.optimization_barrier((keys, values, floor))
     turned = list(zip(*[[around(x, 0, turn) for turn in range(1, per_span)] for x in (near_keys, near_values)]))
-    stacked, acc, stat = pl.pallas_call(
-        own_kernel,
-        out_shape=(jax.ShapeDtypeStruct((kv_heads, width, HEAD_SIZE), jnp.bfloat16), acc_shape, stat_shape),
-        in_specs=[VMEM] + [HBM] * 3,
-        out_specs=(VMEM,) * 3,
+    def own(*refs):
+        own_kernel(per_span, *refs)
+
+    stacked, seen, gate_row, acc, stat = pl.pallas_call(
+        own,
+        out_shape=(
+            jax.ShapeDtypeStruct((kv_heads, width, HEAD_SIZE), jnp.bfloat16),
+            jax.ShapeDtypeStruct((spans, width), jnp.int32),
+            jax.ShapeDtypeStruct((1, wide), jnp.float32),
+            acc_shape,
+            stat_shape,
+        ),
+        in_specs=[pl.BlockSpec(memory_space=pltpu.SMEM)] * 2 + [VMEM] * 2 + [HBM] * 3,
+        out_specs=(VMEM,) * 5,
         scratch_shapes=[
             pltpu.VMEM(queries.shape, queries.dtype),
             pltpu.VMEM(keys.shape, keys.dtype),
@@ -206,7 +252,8 @@
         compiler_params=params,
         cost_estimate=cost(1, 10),
         name="own",
-    )(floor, queries, keys, values)
+    )(span_mask, section, section_gate, floor, queries, keys, values)
+
     for distance in range(1, spans):
         waiting = [(distance - 1, t) for t in turned] + [(distance, tuple(held))]
         forward = []
@@ -218,40 +265,20 @@
         turned, held = travel(held, distance, turned)
         distances = [d for d, _ in waiting]
 
-        count_in = 2 * len(waiting)
         blocks = [k for _, (k, _) in waiting] + [v for _, (_, v) in waiting]
-        if distance == 1:
-
-            def first_step(mask, section, gate, stacked, acc, stat, *refs, distances=distances):
-                flag_kernel(per_span, mask, section, gate, *refs[-2:])
-                step_kernel(distances, stacked, refs[-2], acc, stat, *refs[:-2])
-
-            acc, stat, seen, gate_row = pl.pallas_call(
-                first_step,
-                out_shape=(
-                    acc_shape, stat_shape, jax.ShapeDtypeStruct((spans, width), jnp.int32),
-                    jax.ShapeDtypeStruct((1, wide), jnp.float32),
-                ),
-                in_specs=[pl.BlockSpec(memory_space=pltpu.SMEM)] * 2 + [VMEM] * (4 + count_in),
-                out_specs=(VMEM,) * 4,
-                compiler_params=params,
-                cost_estimate=cost(len(waiting)),
-                name="step_1",
-            )(span_mask, section, section_gate, stacked, acc, stat, *blocks)
-        else:
-
-            def step(*refs, distances=distances):
-                step_kernel(distances, *refs)
-
-            acc, stat = pl.pallas_call(
-                step,
-                out_shape=(acc_shape, stat_shape),
-                in_specs=[VMEM] * (4 + count_in),
-                out_specs=(VMEM,) * 2,
-                compiler_params=params,
-                cost_estimate=cost(len(waiting)),
-                name="step_%d" % distance,
-            )(stacked, seen, acc, stat, *blocks)
+
+        def step(*refs, distances=distances):
+            step_kernel(distances, *refs)
+
+        acc, stat = pl.pallas_call(
+            step,
+            out_shape=(acc_shape, stat_shape),
+            in_specs=[VMEM] * (4 + len(blocks)),
+            out_specs=(VMEM,) * 2,
+            compiler_params=params,
+            cost_estimate=cost(len(waiting)),
+            name="step_%d" % distance,
+        )(stacked, seen, acc, stat, *blocks)
 
     distances = [spans - 1] * len(turned)
 

time: 29.6 us -> 30.4 us (1.027)
  the two profiles are of different devices: /device:TPU:16 before, /device:TPU:24 now
where the time goes in v1:
time: 30.4 us; the launch traced here: 30.2 us
  starting transfers between devices  13.1 us (43%)
  Pallas kernels  13 us (43%)
  waiting for transfers between devices  3.2 us (11%)
  between operations  0.91 us (3%)
    ppermute x14, starting transfers between devices, send(): return lax.ppermute(value, ('tm', 'head'), pairs)  13.1 us
    pallas_call x3, Pallas kernels, on_device(): pl.pallas_call(step, out_shape=(acc_shape, stat_shape), in_specs=[VMEM] *...  7.59 us
    ppermute x14, waiting for transfers between devices, send(): return lax.ppermute(value, ('tm', 'head'), pairs)  3.2 us
    pallas_call x1, Pallas kernels, on_device(): pl.pallas_call(own, out_shape=(jax.ShapeDtypeStruct((kv_heads, width, HEA...  2.46 us
    pallas_call x1, Pallas kernels, on_device(): pl.pallas_call(close, out_shape=(jax.ShapeDtypeStruct((kv_heads, width, H...  1.77 us
    pallas_call x1, Pallas kernels, on_device(): pl.pallas_call(mix_kernel, out_shape=jax.ShapeDtypeStruct((rows, wide), j...  1.15 us
  transfers between devices with their start and end apart: 14, of which 4 were waited for; matrix products, arithmetic and copies ran while one was open for 0% of the time, Pallas kernels for 39%

profile of v1, /device:TPU:24, one launch (start us, length us, event | category | flops | bytes accessed | tf_op | source)
XLA Modules:
  0.0 30.2 jit_solution(17862881001467320075)
XLA Ops:
  0.6 0.0 copy-start.1
  0.6 0.0 copy-start.2
  0.7 0.0 copy-start.3
  0.7 0.0 copy-start.5
  0.7 0.0 copy-start.4
  0.7 0.0 copy-start
  0.7 0.1 collective-permute-start.1
  0.8 1.8 %collective-permute-start = (bf16[128,512]{1,0:T(8,128)(2,1)}, bf16[128,512]{1,0:T(8,128)(2,1)S(1)}, u32[]{:S(2)}, u32[]{:S(2)}) collective-permute-start(bf16[128,512]{1,0:T(8,128)(2,1)} %refs_6_.1), channel_id=1, source_target_pairs={{0,4},{1,5},{2,6},{3,7},{4,8},{5,9},{6,10},{7,11},{8,12},{9,13},{1... | collective-permute-start | bytes 393224 | tf_op jit(solution)/shard_map/ppermute | solution.py:197
  2.5 0.0 copy-done.1
  2.5 1.5 %collective-permute-start.2 = (bf16[128,512]{1,0:T(8,128)(2,1)S(1)}, bf16[128,512]{1,0:T(8,128)(2,1)S(1)}, u32[]{:S(2)}, u32[]{:S(2)}) collective-permute-start(bf16[128,512]{1,0:T(8,128)(2,1)S(1)} %copy-done.1), channel_id=1, source_target_pairs={{0,2},{1,3},{2,0},{3,1},{4,6},{5,7},{6,4},{7,5},{8,10},{9,11},{10,... | collective-permute-start | bytes 393224 | tf_op jit(solution)/shard_map/ppermute | solution.py:197
  4.1 0.0 copy-done.2
  4.1 0.5 %collective-permute-start.3 = (bf16[128,512]{1,0:T(8,128)(2,1)S(1)}, bf16[128,512]{1,0:T(8,128)(2,1)S(1)}, u32[]{:S(2)}, u32[]{:S(2)}) collective-permute-start(bf16[128,512]{1,0:T(8,128)(2,1)S(1)} %copy-done.2), channel_id=1, source_target_pairs={{0,2},{1,3},{2,0},{3,1},{4,6},{5,7},{6,4},{7,5},{8,10},{9,11},{10,... | collective-permute-start | bytes 393224 | tf_op jit(solution)/shard_map/ppermute | solution.py:197
  4.6 0.0 copy-done.3
  4.6 0.0 copy-done.5
  4.6 0.0 copy-done.4
  4.6 0.0 copy-done
  4.6 2.5 %own.1 = (bf16[4,768,128]{2,1,0:T(8,128)(2,1)S(1)}, s32[4,768]{1,0:T(4,128)S(1)}, f32[1,3072]{1,0:T(1,128)S(1)}, f32[4,128,768]{2,1,0:T(8,128)S(1)}, f32[4,8,768]{2,1,0:T(8,128)S(1)}) custom-call(s32[4,4]{1,0:T(4,128)S(1)} %copy-done.4, s32[4]{0:T(128)S(1)} %copy-done.5, f32[4,3072]{1,0:T(4,128)S(1)} %copy-done.3, f32[8,768]{1,0:T(8,128)S(1)} %floor.1.refs_3_, ...), custom_call_target="tpu_custom_call" | custom-call | flops 2013265920 | bytes 3145728 | tf_op jit(solution)/shard_map/own/pallas_call | solution.py:235
  7.1 0.3 collective-permute-done.1.refs_5_
  7.3 1.5 %collective-permute-start.5 = (bf16[128,512]{1,0:T(8,128)(2,1)S(1)}, bf16[128,512]{1,0:T(8,128)(2,1)S(1)}, u32[]{:S(2)}, u32[]{:S(2)}) collective-permute-start(bf16[128,512]{1,0:T(8,128)(2,1)S(1)} %collective-permute-done.1.refs_5_), channel_id=1, source_target_pairs={{0,1},{1,0},{2,3},{3,2},{4,8},{5,9},{6,10},{7,11},{8,12},{9,13},{1... | collective-permute-start | bytes 393224 | tf_op jit(solution)/shard_map/ppermute | solution.py:197
  8.8 0.7 %collective-permute-done.refs_7_ = bf16[128,512]{1,0:T(8,128)(2,1)S(1)} collective-permute-done((bf16[128,512]{1,0:T(8,128)(2,1)}, bf16[128,512]{1,0:T(8,128)(2,1)S(1)}, u32[]{:S(2)}, u32[]{:S(2)}) %collective-permute-start) | collective-permute-done | bytes 131104 | tf_op jit(solution)/shard_map/ppermute | solution.py:197
  9.5 0.0 collective-permute-start.4
  9.5 1.5 %collective-permute-start.7 = (bf16[128,512]{1,0:T(8,128)(2,1)S(1)}, bf16[128,512]{1,0:T(8,128)(2,1)S(1)}, u32[]{:S(2)}, u32[]{:S(2)}) collective-permute-start(bf16[128,512]{1,0:T(8,128)(2,1)S(1)} %collective-permute-done.refs_7_), channel_id=1, source_target_pairs={{0,1},{1,0},{2,3},{3,2},{4,6},{5,7},{6,4},{7,5},{8,10},{9,11},{10,... | collective-permute-start | bytes 393224 | tf_op jit(solution)/shard_map/ppermute | solution.py:197
  11.0 0.0 collective-permute-done.2.refs_4_
  11.0 0.5 %collective-permute-start.6 = (bf16[128,512]{1,0:T(8,128)(2,1)S(1)}, bf16[128,512]{1,0:T(8,128)(2,1)S(1)}, u32[]{:S(2)}, u32[]{:S(2)}) collective-permute-start(bf16[128,512]{1,0:T(8,128)(2,1)S(1)} %collective-permute-done.1.refs_5_), channel_id=1, source_target_pairs={{0,1},{1,0},{2,3},{3,2},{4,6},{5,7},{6,4},{7,5},{8,10},{9,11},{10,... | collective-permute-start | bytes 393224 | tf_op jit(solution)/shard_map/ppermute | solution.py:197
  11.5 0.0 collective-permute-done.3.refs_6_
  11.5 2.5 %step_1.1 = (f32[4,128,768]{2,1,0:T(8,128)S(1)}, f32[4,8,768]{2,1,0:T(8,128)S(1)}) custom-call(bf16[4,768,128]{2,1,0:T(8,128)(2,1)S(1)} %get-tuple-element.33.refs_0_, s32[4,768]{1,0:T(4,128)S(1)} %get-tuple-element.34.refs_1_, f32[4,128,768]{2,1,0:T(8,128)S(1)} %get-tuple-element.35.refs_2_, f32[4,8,768]{2,1,0:T(8,128)S(1)} %get-tuple-element.38.refs_3_, ...), custom_call_target="tpu_custom_call" | custom-call | flops 805306368 | bytes 3145728 | tf_op jit(solution)/shard_map/step_1/pallas_call | solution.py:273
  14.1 0.0 collective-permute-done.5.refs_5_
  14.1 1.8 %collective-permute-start.9 = (bf16[128,512]{1,0:T(8,128)(2,1)S(1)}, bf16[128,512]{1,0:T(8,128)(2,1)S(1)}, u32[]{:S(2)}, u32[]{:S(2)}) collective-permute-start(bf16[128,512]{1,0:T(8,128)(2,1)S(1)} %collective-permute-done.5.refs_5_), channel_id=1, source_target_pairs={{0,1},{1,0},{2,3},{3,2},{4,8},{5,9},{6,10},{7,11},{8,12},{9,13},{1... | collective-permute-start | bytes 393224 | tf_op jit(solution)/shard_map/ppermute | solution.py:197
  15.9 0.0 collective-permute-done.4.refs_7_
  15.9 1.5 %collective-permute-start.11 = (bf16[128,512]{1,0:T(8,128)(2,1)S(1)}, bf16[128,512]{1,0:T(8,128)(2,1)S(1)}, u32[]{:S(2)}, u32[]{:S(2)}) collective-permute-start(bf16[128,512]{1,0:T(8,128)(2,1)S(1)} %collective-permute-done.4.refs_7_), channel_id=1, source_target_pairs={{0,1},{1,0},{2,3},{3,2},{4,5},{5,4},{6,7},{7,6},{8,10},{9,11},{10,... | collective-permute-start | bytes 393224 | tf_op jit(solution)/shard_map/ppermute | solution.py:197
  17.4 0.2 collective-permute-start.8
  17.6 0.0 collective-permute-done.7.refs_6_
  17.6 1.5 %collective-permute-start.10 = (bf16[128,512]{1,0:T(8,128)(2,1)S(1)}, bf16[128,512]{1,0:T(8,128)(2,1)S(1)}, u32[]{:S(2)}, u32[]{:S(2)}) collective-permute-start(bf16[128,512]{1,0:T(8,128)(2,1)S(1)} %collective-permute-done.5.refs_5_), channel_id=1, source_target_pairs={{0,1},{1,0},{2,3},{3,2},{4,5},{5,4},{6,7},{7,6},{8,10},{9,11},{10,... | collective-permute-start | bytes 393224 | tf_op jit(solution)/shard_map/ppermute | solution.py:197
  19.2 0.0 collective-permute-done.6.refs_4_
  19.2 2.5 %step_2.1 = (f32[4,128,768]{2,1,0:T(8,128)S(1)}, f32[4,8,768]{2,1,0:T(8,128)S(1)}) custom-call(bf16[4,768,128]{2,1,0:T(8,128)(2,1)S(1)} %get-tuple-element.33.refs_0_, s32[4,768]{1,0:T(4,128)S(1)} %get-tuple-element.34.refs_1_, f32[4,128,768]{2,1,0:T(8,128)S(1)} %get-tuple-element.43.refs_2_, f32[4,8,768]{2,1,0:T(8,128)S(1)} %get-tuple-element.46.refs_3_, ...), custom_call_target="tpu_custom_call" | custom-call | flops 805306368 | bytes 3145728 | tf_op jit(solution)/shard_map/step_2/pallas_call | solution.py:273
  21.7 0.0 collective-permute-done.9.refs_5_
  21.7 0.6 %collective-permute-start.12 = (bf16[128,512]{1,0:T(8,128)(2,1)S(1)}, bf16[128,512]{1,0:T(8,128)(2,1)S(1)}, u32[]{:S(2)}, u32[]{:S(2)}) collective-permute-start(bf16[128,512]{1,0:T(8,128)(2,1)S(1)} %collective-permute-done.9.refs_5_), channel_id=1, source_target_pairs={{0,1},{1,0},{2,3},{3,2},{4,5},{5,4},{6,7},{7,6},{8,9},{9,8},{10,11... | collective-permute-start | bytes 393224 | tf_op jit(solution)/shard_map/ppermute | solution.py:197
  22.3 0.0 collective-permute-done.11.refs_6_
  22.3 0.1 collective-permute-start.13
  22.4 0.0 collective-permute-done.8.refs_7_
  22.4 1.3 %collective-permute-done.10.refs_4_ = bf16[128,512]{1,0:T(8,128)(2,1)S(1)} collective-permute-done((bf16[128,512]{1,0:T(8,128)(2,1)S(1)}, bf16[128,512]{1,0:T(8,128)(2,1)S(1)}, u32[]{:S(2)}, u32[]{:S(2)}) %collective-permute-start.10) | collective-permute-done | bytes 131104 | tf_op jit(solution)/shard_map/ppermute | solution.py:197
  23.7 2.5 %step_3.1 = (f32[4,128,768]{2,1,0:T(8,128)S(1)}, f32[4,8,768]{2,1,0:T(8,128)S(1)}) custom-call(bf16[4,768,128]{2,1,0:T(8,128)(2,1)S(1)} %get-tuple-element.33.refs_0_, s32[4,768]{1,0:T(4,128)S(1)} %get-tuple-element.34.refs_1_, f32[4,128,768]{2,1,0:T(8,128)S(1)} %get-tuple-element.49.refs_2_, f32[4,8,768]{2,1,0:T(8,128)S(1)} %get-tuple-element.52.refs_3_, ...), custom_call_target="tpu_custom_call" | custom-call | flops 805306368 | bytes 3145728 | tf_op jit(solution)/shard_map/step_3/pallas_call | solution.py:273
  26.2 0.9 %collective-permute-done.12.refs_5_ = bf16[128,512]{1,0:T(8,128)(2,1)S(1)} collective-permute-done((bf16[128,512]{1,0:T(8,128)(2,1)S(1)}, bf16[128,512]{1,0:T(8,128)(2,1)S(1)}, u32[]{:S(2)}, u32[]{:S(2)}) %collective-permute-start.12) | collective-permute-done | bytes 131104 | tf_op jit(solution)/shard_map/ppermute | solution.py:197
  27.1 1.8 %close.1 = (f32[4,768,128]{2,1,0:T(8,128)S(1)}, bf16[4,768,128]{2,1,0:T(8,128)(2,1)S(1)}, f32[24,128]{1,0:T(8,128)}) custom-call(bf16[4,768,128]{2,1,0:T(8,128)(2,1)S(1)} %get-tuple-element.33.refs_0_, s32[4,768]{1,0:T(4,128)S(1)} %get-tuple-element.34.refs_1_, f32[1,3072]{1,0:T(1,128)S(1)} %get-tuple-element.32.refs_2_.gate_row, ...), custom_call_target="tpu_custom_call" | custom-call | flops 402653184 | bytes 3145728 | tf_op jit(solution)/shard_map/close/pallas_call | solution.py:288
  28.9 0.0 collective-permute-done.13.refs_0_
  28.9 1.2 %mix.1 = bf16[128,3072]{1,0:T(8,128)(2,1)} custom-call(f32[1,3072]{1,0:T(1,128)S(1)} %get-tuple-element.32.refs_2_.gate_row, f32[4,768,128]{2,1,0:T(8,128)S(1)} %get-tuple-element.57.part, bf16[4,768,128]{2,1,0:T(8,128)(2,1)S(1)} %get-tuple-element.58.last_weight, bf16[128,512]{1,0:T(8,128)(2,1)S(1)} %collective-permute-done.13.refs_0_), custom_call_target="tpu_custom_call" | custom-call | flops 402653184 | bytes 3145728 | tf_op jit(solution)/shard_map/mix/pallas_call | solution.py:301
  (1 shorter events, 0.0 us)
Async XLA Ops:
  0.6 1.9 %copy-start.1 = (bf16[128,512]{1,0:T(8,128)(2,1)S(1)}, bf16[128,512]{1,0:T(8,128)(2,1)}, u32[]{:S(2)}) copy-start(bf16[128,512]{1,0:T(8,128)(2,1)} %refs_5_.1) | copy-start | bytes 393220
  0.6 3.4 %copy-start.2 = (bf16[128,512]{1,0:T(8,128)(2,1)S(1)}, bf16[128,512]{1,0:T(8,128)(2,1)}, u32[]{:S(2)}) copy-start(bf16[128,512]{1,0:T(8,128)(2,1)} %refs_6_.1) | copy-start | bytes 393220
  0.7 3.9 %copy-start.3 = (f32[4,3072]{1,0:T(4,128)S(1)}, f32[4,3072]{1,0:T(4,128)}, u32[]{:S(2)}) copy-start(f32[4,3072]{1,0:T(4,128)} %refs_2_.1) | copy-start | bytes 147460
  0.7 3.9 %copy-start.5 = (s32[4]{0:T(128)S(1)}, s32[4]{0:T(128)}, u32[]{:S(2)}) copy-start(s32[4]{0:T(128)} %refs_1_.1) | copy-start | bytes 52
  0.7 3.9 %copy-start.4 = (s32[4,4]{1,0:T(4,128)S(1)}, s32[4,4]{1,0:T(4,128)}, u32[]{:S(2)}) copy-start(s32[4,4]{1,0:T(4,128)} %refs_0_.1) | copy-start | bytes 196
  0.7 3.9 %copy-start = (bf16[128,3072]{1,0:T(8,128)(2,1)S(1)}, bf16[128,3072]{1,0:T(8,128)(2,1)}, u32[]{:S(2)}) copy-start(bf16[128,3072]{1,0:T(8,128)(2,1)} %refs_4_.1) | copy-start | bytes 2359300
  0.7 6.6 %collective-permute-start.1 = (bf16[128,512]{1,0:T(8,128)(2,1)}, bf16[128,512]{1,0:T(8,128)(2,1)S(1)}, u32[]{:S(2)}, u32[]{:S(2)}) collective-permute-start(bf16[128,512]{1,0:T(8,128)(2,1)} %refs_5_.1), channel_id=1, source_target_pairs={{0,4},{1,5},{2,6},{3,7},{4,8},{5,9},{6,10},{7,11},{8,12},{9,13},{1... | collective-permute-start | bytes 393224 | tf_op jit(solution)/shard_map/ppermute | solution.py:197
  0.8 8.7 %collective-permute-start = (bf16[128,512]{1,0:T(8,128)(2,1)}, bf16[128,512]{1,0:T(8,128)(2,1)S(1)}, u32[]{:S(2)}, u32[]{:S(2)}) collective-permute-start(bf16[128,512]{1,0:T(8,128)(2,1)} %refs_6_.1), channel_id=1, source_target_pairs={{0,4},{1,5},{2,6},{3,7},{4,8},{5,9},{6,10},{7,11},{8,12},{9,13},{1... | collective-permute-start | bytes 393224 | tf_op jit(solution)/shard_map/ppermute | solution.py:197
  2.5 8.5 %collective-permute-start.2 = (bf16[128,512]{1,0:T(8,128)(2,1)S(1)}, bf16[128,512]{1,0:T(8,128)(2,1)S(1)}, u32[]{:S(2)}, u32[]{:S(2)}) collective-permute-start(bf16[128,512]{1,0:T(8,128)(2,1)S(1)} %copy-done.1), channel_id=1, source_target_pairs={{0,2},{1,3},{2,0},{3,1},{4,6},{5,7},{6,4},{7,5},{8,10},{9,11},{10,... | collective-permute-start | bytes 393224 | tf_op jit(solution)/shard_map/ppermute | solution.py:197
  4.1 7.5 %collective-permute-start.3 = (bf16[128,512]{1,0:T(8,128)(2,1)S(1)}, bf16[128,512]{1,0:T(8,128)(2,1)S(1)}, u32[]{:S(2)}, u32[]{:S(2)}) collective-permute-start(bf16[128,512]{1,0:T(8,128)(2,1)S(1)} %copy-done.2), channel_id=1, source_target_pairs={{0,2},{1,3},{2,0},{3,1},{4,6},{5,7},{6,4},{7,5},{8,10},{9,11},{10,... | collective-permute-start | bytes 393224 | tf_op jit(solution)/shard_map/ppermute | solution.py:197
  7.3 6.7 %collective-permute-start.5 = (bf16[128,512]{1,0:T(8,128)(2,1)S(1)}, bf16[128,512]{1,0:T(8,128)(2,1)S(1)}, u32[]{:S(2)}, u32[]{:S(2)}) collective-permute-start(bf16[128,512]{1,0:T(8,128)(2,1)S(1)} %collective-permute-done.1.refs_5_), channel_id=1, source_target_pairs={{0,1},{1,0},{2,3},{3,2},{4,8},{5,9},{6,10},{7,11},{8,12},{9,13},{1... | collective-permute-start | bytes 393224 | tf_op jit(solution)/shard_map/ppermute | solution.py:197
  9.5 6.4 %collective-permute-start.4 = (bf16[128,512]{1,0:T(8,128)(2,1)S(1)}, bf16[128,512]{1,0:T(8,128)(2,1)S(1)}, u32[]{:S(2)}, u32[]{:S(2)}) collective-permute-start(bf16[128,512]{1,0:T(8,128)(2,1)S(1)} %collective-permute-done.refs_7_), channel_id=1, source_target_pairs={{0,1},{1,0},{2,3},{3,2},{4,8},{5,9},{6,10},{7,11},{8,12},{9,13},{1... | collective-permute-start | bytes 393224 | tf_op jit(solution)/shard_map/ppermute | solution.py:197
  9.5 8.1 %collective-permute-start.7 = (bf16[128,512]{1,0:T(8,128)(2,1)S(1)}, bf16[128,512]{1,0:T(8,128)(2,1)S(1)}, u32[]{:S(2)}, u32[]{:S(2)}) collective-permute-start(bf16[128,512]{1,0:T(8,128)(2,1)S(1)} %collective-permute-done.refs_7_), channel_id=1, source_target_pairs={{0,1},{1,0},{2,3},{3,2},{4,6},{5,7},{6,4},{7,5},{8,10},{9,11},{10,... | collective-permute-start | bytes 393224 | tf_op jit(solution)/shard_map/ppermute | solution.py:197
  11.0 8.1 %collective-permute-start.6 = (bf16[128,512]{1,0:T(8,128)(2,1)S(1)}, bf16[128,512]{1,0:T(8,128)(2,1)S(1)}, u32[]{:S(2)}, u32[]{:S(2)}) collective-permute-start(bf16[128,512]{1,0:T(8,128)(2,1)S(1)} %collective-permute-done.1.refs_5_), channel_id=1, source_target_pairs={{0,1},{1,0},{2,3},{3,2},{4,6},{5,7},{6,4},{7,5},{8,10},{9,11},{10,... | collective-permute-start | bytes 393224 | tf_op jit(solution)/shard_map/ppermute | solution.py:197
  14.1 7.6 %collective-permute-start.9 = (bf16[128,512]{1,0:T(8,128)(2,1)S(1)}, bf16[128,512]{1,0:T(8,128)(2,1)S(1)}, u32[]{:S(2)}, u32[]{:S(2)}) collective-permute-start(bf16[128,512]{1,0:T(8,128)(2,1)S(1)} %collective-permute-done.5.refs_5_), channel_id=1, source_target_pairs={{0,1},{1,0},{2,3},{3,2},{4,8},{5,9},{6,10},{7,11},{8,12},{9,13},{1... | collective-permute-start | bytes 393224 | tf_op jit(solution)/shard_map/ppermute | solution.py:197
  15.9 6.4 %collective-permute-start.11 = (bf16[128,512]{1,0:T(8,128)(2,1)S(1)}, bf16[128,512]{1,0:T(8,128)(2,1)S(1)}, u32[]{:S(2)}, u32[]{:S(2)}) collective-permute-start(bf16[128,512]{1,0:T(8,128)(2,1)S(1)} %collective-permute-done.4.refs_7_), channel_id=1, source_target_pairs={{0,1},{1,0},{2,3},{3,2},{4,5},{5,4},{6,7},{7,6},{8,10},{9,11},{10,... | collective-permute-start | bytes 393224 | tf_op jit(solution)/shard_map/ppermute | solution.py:197
  17.4 5.0 %collective-permute-start.8 = (bf16[128,512]{1,0:T(8,128)(2,1)S(1)}, bf16[128,512]{1,0:T(8,128)(2,1)S(1)}, u32[]{:S(2)}, u32[]{:S(2)}) collective-permute-start(bf16[128,512]{1,0:T(8,128)(2,1)S(1)} %collective-permute-done.4.refs_7_), channel_id=1, source_target_pairs={{0,1},{1,0},{2,3},{3,2},{4,8},{5,9},{6,10},{7,11},{8,12},{9,13},{1... | collective-permute-start | bytes 393224 | tf_op jit(solution)/shard_map/ppermute | solution.py:197
  17.6 6.0 %collective-permute-start.10 = (bf16[128,512]{1,0:T(8,128)(2,1)S(1)}, bf16[128,512]{1,0:T(8,128)(2,1)S(1)}, u32[]{:S(2)}, u32[]{:S(2)}) collective-permute-start(bf16[128,512]{1,0:T(8,128)(2,1)S(1)} %collective-permute-done.5.refs_5_), channel_id=1, source_target_pairs={{0,1},{1,0},{2,3},{3,2},{4,5},{5,4},{6,7},{7,6},{8,10},{9,11},{10,... | collective-permute-start | bytes 393224 | tf_op jit(solution)/shard_map/ppermute | solution.py:197
  21.7 5.4 %collective-permute-start.12 = (bf16[128,512]{1,0:T(8,128)(2,1)S(1)}, bf16[128,512]{1,0:T(8,128)(2,1)S(1)}, u32[]{:S(2)}, u32[]{:S(2)}) collective-permute-start(bf16[128,512]{1,0:T(8,128)(2,1)S(1)} %collective-permute-done.9.refs_5_), channel_id=1, source_target_pairs={{0,1},{1,0},{2,3},{3,2},{4,5},{5,4},{6,7},{7,6},{8,9},{9,8},{10,11... | collective-permute-start | bytes 393224 | tf_op jit(solution)/shard_map/ppermute | solution.py:197
  22.3 6.6 %collective-permute-start.13 = (bf16[128,512]{1,0:T(8,128)(2,1)S(1)}, bf16[128,512]{1,0:T(8,128)(2,1)S(1)}, u32[]{:S(2)}, u32[]{:S(2)}) collective-permute-start(bf16[128,512]{1,0:T(8,128)(2,1)S(1)} %collective-permute-done.11.refs_6_), channel_id=1, source_target_pairs={{0,1},{1,0},{2,3},{3,2},{4,8},{5,9},{6,10},{7,11},{8,12},{9,13},{1... | collective-permute-start | bytes 393224 | tf_op jit(solution)/shard_map/ppermute | solution.py:197

commit v2 on v1

v2 whole, which is shorter than its diff:
```python
import math

import jax
import jax.numpy as jnp
from jax import lax
from jax.experimental import pallas as pl
from jax.experimental.pallas import tpu as pltpu
from jax.sharding import PartitionSpec as P

HEAD_SIZE = 128
CH = 256
LOG2E = math.log2(math.e)
FAR = 1e30
LIMIT = 2.0**80
SCALE = LOG2E / math.sqrt(HEAD_SIZE)
HBM = pl.BlockSpec(memory_space=pltpu.HBM)
VMEM = pl.BlockSpec(memory_space=pltpu.VMEM)


def head_columns(h):
    return slice(h * HEAD_SIZE, (h + 1) * HEAD_SIZE)


def against(queries, keys):
    return lax.dot_general(queries, keys, (((1,), (1,)), ((), ())), preferred_element_type=jnp.float32)


def with_ones(values):
    return jnp.concatenate([values, jnp.ones((values.shape[0], HEAD_SIZE), values.dtype)], axis=1)


def lanes(rows):
    return lax.broadcasted_iota(jnp.int32, (rows, HEAD_SIZE), 1)


def floor_kernel(floor):
    floor[...] = jnp.full(floor.shape, -FAR, jnp.float32)


def own_kernel(per_span, mask, section, gate, floor, q_hbm, k_hbm, v_hbm,
               stacked, tails, gate_row, tops, acc, q, k, v, sems):
    copies = [
        pltpu.make_async_copy(src, dst, sems.at[i])
        for i, (src, dst) in enumerate([(q_hbm, q), (k_hbm, k), (v_hbm, v)])
    ]
    for copy in copies:
        copy.start()
    span = lax.axis_index("tm") // per_span
    at = lanes(tails.shape[1])
    for distance in range(tails.shape[0]):
        allowed = jnp.logical_and(span >= distance, mask[span, jnp.maximum(span - distance, 0)] > 0)
        bias = jnp.where(allowed, 0.0, -FAR)
        tails[distance] = jnp.where(at < 3, 1.0, jnp.where(at == 3, bias, 0.0)).astype(jnp.bfloat16)
    gate_row[...] = gate[pl.ds(section[span], 1), :]
    for copy in copies:
        copy.wait()
    rows, width = q.shape[0], stacked.shape[1]
    group = width // rows
    every_top = jnp.zeros((rows, HEAD_SIZE), jnp.float32)
    at, beside = lanes(rows), lanes(width)
    for h in range(stacked.shape[0]):
        queries = jnp.concatenate([q[:, head_columns(h * group + g)] for g in range(group)], axis=0)
        score = against(queries, k[:, head_columns(h)])
        top = jnp.maximum(floor[0:1, 0:1], jnp.max(score, axis=1, keepdims=True))
        weight = jnp.exp2(SCALE * (score - top)).astype(jnp.bfloat16)
        acc[h] = jnp.dot(weight, with_ones(v[:, head_columns(h)]), preferred_element_type=jnp.float32)
        high = top.astype(jnp.bfloat16).astype(jnp.float32)
        middle = (top - high).astype(jnp.bfloat16).astype(jnp.float32)
        low = top - high - middle
        extra = jnp.where(
            beside == 0, -high, jnp.where(beside == 1, -middle, jnp.where(beside == 2, -low, jnp.where(beside == 3, 1.0, 0.0)))
        )
        stacked[h] = jnp.concatenate([queries, extra.astype(jnp.bfloat16)], axis=1)
        for g in range(group):
            every_top = jnp.where(at == h * group + g, top[g * rows : (g + 1) * rows, :], every_top)
    tops[...] = every_top.T[: tops.shape[0], :] * (1.0 / math.sqrt(HEAD_SIZE))


def weights_of(h, distances, stacked, tails, key_refs):
    keys = jnp.concatenate(
        [jnp.concatenate([k[:, head_columns(h)], tails[d]], axis=1) for d, k in zip(distances, key_refs)], axis=0
    )
    return jnp.exp2(SCALE * against(stacked[h], keys))


def step_kernel(distances, stacked, tails, acc_in, *refs):
    count = len(distances)
    key_refs, value_refs, (acc,) = refs[:count], refs[count : 2 * count], refs[2 * count :]
    for h in range(stacked.shape[0]):
        weight = weights_of(h, distances, stacked, tails, key_refs).astype(jnp.bfloat16)
        values = with_ones(jnp.concatenate([v[:, head_columns(h)] for v in value_refs], axis=0))
        acc[h] = acc_in[h] + jnp.dot(weight, values, preferred_element_type=jnp.float32)


def close_kernel(distances, last, stacked, tails, gate_row, tops, acc, *refs):
    count = len(distances)
    key_refs, value_refs, (part, last_weight, log_ref) = refs[:count], refs[count : 2 * count - last], refs[2 * count - last :]
    heads, rows = log_ref.shape
    width = stacked.shape[1]
    group = width // rows
    at = lanes(rows)

    def gated(h, g, attended):
        columns = pl.ds(pl.multiple_of((h * group + g) * HEAD_SIZE, HEAD_SIZE), HEAD_SIZE)
        part[h, g * rows : (g + 1) * rows, :] = attended[g * rows : (g + 1) * rows, :] * gate_row[:, columns]

    every_total = jnp.ones((rows, HEAD_SIZE), jnp.float32)
    for h in range(stacked.shape[0]):
        weight = weights_of(h, distances[-last:], stacked, tails, key_refs[-last:])
        ones = jnp.ones((weight.shape[1], HEAD_SIZE), jnp.bfloat16)
        total = acc[h, :, HEAD_SIZE:] + jnp.dot(weight.astype(jnp.bfloat16), ones, preferred_element_type=jnp.float32)
        inverse = 1.0 / total
        for i in range(last):
            last_weight[h, :, head_columns(i)] = (weight[:, head_columns(i)] * inverse).astype(jnp.bfloat16)
        attended = acc[h, :, :HEAD_SIZE] * inverse
        for g in range(group):
            gated(h, g, attended)
            every_total = jnp.where(at == h * group + g, total[g * rows : (g + 1) * rows, :], every_total)
    log_ref[...] = tops[...] + jnp.log(every_total.T[:heads, :])
    outside = jnp.max(jnp.where(every_total <= LIMIT, 0.0, 1.0))

    @pl.when(outside > 0.0)
    def _():
        def one_head(h, carry):
            every_top, every_total = carry
            inside = pl.ds(pl.multiple_of(h * HEAD_SIZE, HEAD_SIZE), HEAD_SIZE)
            queries = stacked[h, :, :HEAD_SIZE]
            bias = [tails[d, 0:1, 3:4].astype(jnp.float32) for d in distances]
            top = None
            for k, b in zip(key_refs, bias):
                row = jnp.max(against(queries, k[:, inside]) + b, axis=1, keepdims=True)
                top = row if top is None else jnp.maximum(top, row)
            total = jnp.zeros((width, 1), jnp.float32)
            attended = jnp.zeros((width, HEAD_SIZE), jnp.float32)
            late = []
            for i, (k, b) in enumerate(zip(key_refs, bias)):
                weight = jnp.exp2(SCALE * (against(queries, k[:, inside]) + b - top))
                total += jnp.sum(weight, axis=1, keepdims=True)
                if i < count - last:
                    attended += jnp.dot(
                        weight.astype(jnp.bfloat16), value_refs[i][:, inside], preferred_element_type=jnp.float32
                    )
                else:
                    late.append(weight)
            inverse = 1.0 / total
            for i, weight in enumerate(late):
                last_weight[h, :, head_columns(i)] = (weight * inverse).astype(jnp.bfloat16)
            attended = attended * inverse
            for g in range(group):
                gated(h, g, attended)
                here = at == h * group + g
                every_top = jnp.where(here, top[g * rows : (g + 1) * rows, :], every_top)
                every_total = jnp.where(here, total[g * rows : (g + 1) * rows, :], every_total)
            return every_top, every_total

        start = (jnp.zeros((rows, HEAD_SIZE), jnp.float32), jnp.ones((rows, HEAD_SIZE), jnp.float32))
        every_top, every_total = lax.fori_loop(0, stacked.shape[0], one_head, start)
        log_ref[...] = (every_top.T * (1.0 / math.sqrt(HEAD_SIZE)) + jnp.log(every_total.T))[:heads, :]


def mix_kernel(gate_row, part, last_weight, *refs):
    value_refs, (mixed_hbm, mixed, sems) = refs[:-3], refs[-3:]
    kv_heads, width = part.shape[0], part.shape[1]
    rows = mixed.shape[0]
    group = width // rows
    copies = []
    for h in range(kv_heads):
        values = jnp.concatenate([v[:, head_columns(h)] for v in value_refs], axis=0)
        rest = jnp.dot(last_weight[h], values, preferred_element_type=jnp.float32)
        for g in range(group):
            inside = slice(g * rows, (g + 1) * rows)
            columns = head_columns(h * group + g)
            mixed[:, columns] = (part[h, inside, :] + gate_row[:, columns] * rest[inside, :]).astype(jnp.bfloat16)
        columns = pl.ds(h * group * HEAD_SIZE, group * HEAD_SIZE)
        copies.append(pltpu.make_async_copy(mixed.at[:, columns], mixed_hbm.at[:, columns], sems.at[h]))
        copies[-1].start()
    for copy in copies:
        copy.wait()


def on_device(queries, keys, values, span_mask, section, section_gate):
    rows, wide = queries.shape
    heads, kv_heads = wide // HEAD_SIZE, keys.shape[1] // HEAD_SIZE
    width = heads // kv_heads * rows
    count = lax.axis_size("tm")
    per_span = CH // rows
    spans = count // per_span
    params = pltpu.CompilerParams(vmem_limit_bytes=24 * 1024 * 1024)
    acc_shape = jax.ShapeDtypeStruct((kv_heads, width, 2 * HEAD_SIZE), jnp.float32)

    def cost(blocks, times=2):
        return pl.CostEstimate(
            flops=4 * times * blocks * rows * rows * wide, bytes_accessed=rows * wide * 8, transcendentals=blocks * rows * rows * heads
        )

    cores = lax.axis_size("head")

    def send(value, target):
        pairs = []
        for i in range(count):
            for core in range(cores):
                if target(i) is None:
                    goal = i * cores + (core + 1) % cores if cores > 1 else i
                else:
                    goal = target(i) * cores + core
                pairs.append((i * cores + core, goal))
        return lax.ppermute(value, ("tm", "head"), pairs)

    def onward(value, distance):
        first = (distance - 1) * per_span

        def target(i):
            if i < first:
                return None
            return i + per_span if i + per_span < count else first + i % per_span

        return send(value, target)

    def around(value, distance, turn):
        return send(
            value, lambda i: i - i % per_span + (i + turn) % per_span if i >= distance * per_span else None
        )

    def travel(held, distance, turned_before):
        onwards = [onward(x, distance + 1) for x in held] if distance + 1 < spans else []
        turned = [[around(x, distance, turn) for turn in range(1, per_span)] for x in held]
        if not onwards and turned_before:
            turned[1] = [onward(v, distance) for _, v in turned_before]
        return list(zip(*turned)), onwards

    floor = pl.pallas_call(
        floor_kernel,
        out_shape=jax.ShapeDtypeStruct((8, width), jnp.float32),
        out_specs=VMEM,
        compiler_params=params,
        cost_estimate=cost(4, 10),
        name="floor",
    )()
    held = [onward(x, 1) for x in (keys, values)] if spans > 1 else []
    near_keys, near_values, floor = lax.optimization_barrier((keys, values, floor))
    turned = list(zip(*[[around(x, 0, turn) for turn in range(1, per_span)] for x in (near_keys, near_values)]))
    def own(*refs):
        own_kernel(per_span, *refs)

    stacked, tails, gate_row, tops, acc = pl.pallas_call(
        own,
        out_shape=(
            jax.ShapeDtypeStruct((kv_heads, width, 2 * HEAD_SIZE), jnp.bfloat16),
            jax.ShapeDtypeStruct((spans, rows, HEAD_SIZE), jnp.bfloat16),
            jax.ShapeDtypeStruct((1, wide), jnp.float32),
            jax.ShapeDtypeStruct((heads, rows), jnp.float32),
            acc_shape,
        ),
        in_specs=[pl.BlockSpec(memory_space=pltpu.SMEM)] * 2 + [VMEM] * 2 + [HBM] * 3,
        out_specs=(VMEM,) * 5,
        scratch_shapes=[
            pltpu.VMEM(queries.shape, queries.dtype),
            pltpu.VMEM(keys.shape, keys.dtype),
            pltpu.VMEM(values.shape, values.dtype),
            pltpu.SemaphoreType.DMA((3,)),
        ],
        compiler_params=params,
        cost_estimate=cost(1, 10),
        name="own",
    )(span_mask, section, section_gate, floor, queries, keys, values)

    seen_blocks = [(0, (keys, values))]
    for distance in range(1, spans):
        waiting = [(distance - 1, t) for t in turned]
        forward = []
        for x in held:
            x, acc = lax.optimization_barrier((x, acc))
            forward.append(x)
        held = forward
        waiting.append((distance, tuple(held)))
        turned, held = travel(held, distance, turned)
        distances = [d for d, _ in waiting]
        blocks = [k for _, (k, _) in waiting] + [v for _, (_, v) in waiting]
        seen_blocks += waiting

        def step(*refs, distances=distances):
            step_kernel(distances, *refs)

        acc = pl.pallas_call(
            step,
            out_shape=acc_shape,
            in_specs=[VMEM] * (3 + len(blocks)),
            out_specs=VMEM,
            compiler_params=params,
            cost_estimate=cost(len(waiting)),
            name="step_%d" % distance,
        )(stacked, tails, acc, *blocks)

    distances = [d for d, _ in seen_blocks] + [spans - 1] * len(turned)

    def close(*refs):
        close_kernel(distances, len(turned), *refs)

    blocks = [k for _, (k, _) in seen_blocks] + [k for k, _ in turned] + [v for _, (_, v) in seen_blocks]
    part, last_weight, log_total = pl.pallas_call(
        close,
        out_shape=(
            jax.ShapeDtypeStruct((kv_heads, width, HEAD_SIZE), jnp.float32),
            jax.ShapeDtypeStruct((kv_heads, width, len(turned) * rows), jnp.bfloat16),
            jax.ShapeDtypeStruct((heads, rows), jnp.float32),
        ),
        in_specs=[VMEM] * (5 + len(blocks)),
        out_specs=(VMEM,) * 3,
        compiler_params=params,
        cost_estimate=cost(1),
        name="close",
    )(stacked, tails, gate_row, tops, acc, *blocks)
    mixed = pl.pallas_call(
        mix_kernel,
        out_shape=jax.ShapeDtypeStruct((rows, wide), jnp.bfloat16),
        in_specs=[VMEM] * (3 + len(turned)),
        out_specs=HBM,
        scratch_shapes=[pltpu.VMEM((rows, wide), jnp.bfloat16), pltpu.SemaphoreType.DMA((kv_heads,))],
        compiler_params=params,
        cost_estimate=cost(1),
        name="mix",
    )(gate_row, part, last_weight, *[v for _, v in turned])
    return mixed, log_total


def solution(mesh):
    placed = (
        P(("grp", "tm"), "head"),
        P(("grp", "tm"), "head"),
        P(("grp", "tm"), "head"),
        P("grp", None),
        P("grp"),
        P(None, "head"),
    )
    return jax.shard_map(
        on_device,
        mesh=mesh,
        in_specs=placed,
        out_specs=(P(("grp", "tm"), "head"), P("head", ("grp", "tm"))),
        check_vma=False,
    )
```

time: 30.4 us -> 30.3 us (level)
  the two profiles are of different devices: /device:TPU:24 before, /device:TPU:18 now
where the time goes in v2:
time: 30.3 us; the launch traced here: 30.1 us
  starting transfers between devices  16.7 us (55%)
  Pallas kernels  10.9 us (36%)
  waiting for transfers between devices  1.78 us (6%)
  between operations  0.76 us (3%)
    ppermute x14, starting transfers between devices, send(): return lax.ppermute(value, ('tm', 'head'), pairs)  16.7 us
    pallas_call x3, Pallas kernels, on_device(): pl.pallas_call(step, out_shape=acc_shape, in_specs=[VMEM] * (3 + len(bloc...  3.83 us
    pallas_call x1, Pallas kernels, on_device(): pl.pallas_call(own, out_shape=(jax.ShapeDtypeStruct((kv_heads, width, 2 *...  3.79 us
    pallas_call x1, Pallas kernels, on_device(): pl.pallas_call(close, out_shape=(jax.ShapeDtypeStruct((kv_heads, width, H...  2.08 us
    ppermute x14, waiting for transfers between devices, send(): return lax.ppermute(value, ('tm', 'head'), pairs)  1.78 us
    pallas_call x1, Pallas kernels, on_device(): pl.pallas_call(mix_kernel, out_shape=jax.ShapeDtypeStruct((rows, wide), j...  1.16 us
  transfers between devices with their start and end apart: 14, of which 3 were waited for; matrix products, arithmetic and copies ran while one was open for 0% of the time, Pallas kernels for 32%

profile of v2, /device:TPU:18, one launch (start us, length us, event | category | flops | bytes accessed | tf_op | source)
XLA Modules:
  0.0 30.1 jit_solution(17682637244739279714)
XLA Ops:
  0.6 0.0 copy-start.1
  0.6 0.0 copy-start
  0.7 0.0 copy-start.4
  0.7 0.0 copy-start.5
  0.7 0.0 copy-start.3
  0.7 0.0 copy-start.2
  0.7 1.6 %collective-permute-start = (bf16[128,512]{1,0:T(8,128)(2,1)}, bf16[128,512]{1,0:T(8,128)(2,1)S(1)}, u32[]{:S(2)}, u32[]{:S(2)}) collective-permute-start(bf16[128,512]{1,0:T(8,128)(2,1)} %refs_13_.1), channel_id=1, source_target_pairs={{0,4},{1,5},{2,6},{3,7},{4,8},{5,9},{6,10},{7,11},{8,12},{9,13},{1... | collective-permute-start | bytes 393224 | tf_op jit(solution)/shard_map/ppermute | solution.py:207
  2.3 0.2 collective-permute-start.1
  2.5 0.0 copy-done
  2.5 1.5 %collective-permute-start.4 = (bf16[128,512]{1,0:T(8,128)(2,1)S(1)}, bf16[128,512]{1,0:T(8,128)(2,1)S(1)}, u32[]{:S(2)}, u32[]{:S(2)}) collective-permute-start(bf16[128,512]{1,0:T(8,128)(2,1)S(1)} %copy-done), channel_id=1, source_target_pairs={{0,2},{1,3},{2,0},{3,1},{4,6},{5,7},{6,4},{7,5},{8,10},{9,11},{10,... | collective-permute-start | bytes 393224 | tf_op jit(solution)/shard_map/ppermute | solution.py:207
  4.1 0.0 copy-done.1
  4.1 0.5 %collective-permute-start.5 = (bf16[128,512]{1,0:T(8,128)(2,1)S(1)}, bf16[128,512]{1,0:T(8,128)(2,1)S(1)}, u32[]{:S(2)}, u32[]{:S(2)}) collective-permute-start(bf16[128,512]{1,0:T(8,128)(2,1)S(1)} %copy-done.1), channel_id=1, source_target_pairs={{0,2},{1,3},{2,0},{3,1},{4,6},{5,7},{6,4},{7,5},{8,10},{9,11},{10,... | collective-permute-start | bytes 393224 | tf_op jit(solution)/shard_map/ppermute | solution.py:207
  4.6 0.0 copy-done.4
  4.6 0.0 copy-done.5
  4.6 0.0 copy-done.3
  4.6 0.0 copy-done.2
  4.6 3.8 %own.1 = (bf16[4,768,256]{2,1,0:T(8,128)(2,1)S(1)}, bf16[4,128,128]{2,1,0:T(8,128)(2,1)S(1)}, f32[1,3072]{1,0:T(1,128)S(1)}, f32[24,128]{1,0:T(8,128)S(1)}, f32[4,768,256]{2,1,0:T(8,128)S(1)}) custom-call(s32[4,4]{1,0:T(4,128)S(1)} %copy-done.4, s32[4]{0:T(128)S(1)} %copy-done.5, f32[4,3072]{1,0:T(4,128)S(1)} %copy-done.3, f32[8,768]{1,0:T(8,128)S(1)} %floor.1.refs_3_, ...), custom_call_target="tpu_custom_call" | custom-call | flops 2013265920 | bytes 3145728 | tf_op jit(solution)/shard_map/own/pallas_call | solution.py:245
  8.4 0.6 %collective-permute-done.1.refs_4_.refs_7_ = bf16[128,512]{1,0:T(8,128)(2,1)S(1)} collective-permute-done((bf16[128,512]{1,0:T(8,128)(2,1)}, bf16[128,512]{1,0:T(8,128)(2,1)S(1)}, u32[]{:S(2)}, u32[]{:S(2)}) %collective-permute-start.1) | collective-permute-done | bytes 131104 | tf_op jit(solution)/shard_map/ppermute | solution.py:207
  9.0 1.6 %collective-permute-start.3 = (bf16[128,512]{1,0:T(8,128)(2,1)S(1)}, bf16[128,512]{1,0:T(8,128)(2,1)S(1)}, u32[]{:S(2)}, u32[]{:S(2)}) collective-permute-start(bf16[128,512]{1,0:T(8,128)(2,1)S(1)} %collective-permute-done.1.refs_4_.refs_7_), channel_id=1, source_target_pairs={{0,1},{1,0},{2,3},{3,2},{4,8},{5,9},{6,10},{7,11},{8,12},{9,13},{1... | collective-permute-start | bytes 393224 | tf_op jit(solution)/shard_map/ppermute | solution.py:207
  10.6 0.0 collective-permute-done.refs_6_.refs_15_
  10.6 1.1 %collective-permute-start.2 = (bf16[128,512]{1,0:T(8,128)(2,1)S(1)}, bf16[128,512]{1,0:T(8,128)(2,1)S(1)}, u32[]{:S(2)}, u32[]{:S(2)}) collective-permute-start(bf16[128,512]{1,0:T(8,128)(2,1)S(1)} %collective-permute-done.refs_6_.refs_15_), channel_id=1, source_target_pairs={{0,1},{1,0},{2,3},{3,2},{4,8},{5,9},{6,10},{7,11},{8,12},{9,13},{1... | collective-permute-start | bytes 393224 | tf_op jit(solution)/shard_map/ppermute | solution.py:207
  11.7 1.5 %collective-permute-start.8 = (bf16[128,512]{1,0:T(8,128)(2,1)S(1)}, bf16[128,512]{1,0:T(8,128)(2,1)S(1)}, u32[]{:S(2)}, u32[]{:S(2)}) collective-permute-start(bf16[128,512]{1,0:T(8,128)(2,1)S(1)} %collective-permute-done.1.refs_4_.refs_7_), channel_id=1, source_target_pairs={{0,1},{1,0},{2,3},{3,2},{4,6},{5,7},{6,4},{7,5},{8,10},{9,11},{10,... | collective-permute-start | bytes 393224 | tf_op jit(solution)/shard_map/ppermute | solution.py:207
  13.2 0.0 collective-permute-done.4.refs_3_.refs_6_
  13.2 0.5 %collective-permute-start.9 = (bf16[128,512]{1,0:T(8,128)(2,1)S(1)}, bf16[128,512]{1,0:T(8,128)(2,1)S(1)}, u32[]{:S(2)}, u32[]{:S(2)}) collective-permute-start(bf16[128,512]{1,0:T(8,128)(2,1)S(1)} %collective-permute-done.refs_6_.refs_15_), channel_id=1, source_target_pairs={{0,1},{1,0},{2,3},{3,2},{4,6},{5,7},{6,4},{7,5},{8,10},{9,11},{10,... | collective-permute-start | bytes 393224 | tf_op jit(solution)/shard_map/ppermute | solution.py:207
  13.7 0.0 collective-permute-done.5.refs_5_.refs_14_
  13.7 1.3 %step_1.1.refs_2_ = f32[4,768,256]{2,1,0:T(8,128)S(1)} custom-call(bf16[4,768,256]{2,1,0:T(8,128)(2,1)S(1)} %get-tuple-element.27.refs_0_, bf16[4,128,128]{2,1,0:T(8,128)(2,1)S(1)} %get-tuple-element.28.refs_1_, f32[4,768,256]{2,1,0:T(8,128)S(1)} %get-tuple-element.34.refs_2_, bf16[128,512]{1,0:T(8,128)(2,1)S(1)} %collective-permute-done.4.refs_3_.refs_6_, ...), custom_call_target="tpu_custom_call" | custom-call | flops 805306368 | bytes 3145728 | tf_op jit(solution)/shard_map/step_1/pallas_call | solution.py:284
  15.0 0.0 collective-permute-done.3.refs_4_.refs_9_
  15.1 1.3 %collective-permute-start.7 = (bf16[128,512]{1,0:T(8,128)(2,1)S(1)}, bf16[128,512]{1,0:T(8,128)(2,1)S(1)}, u32[]{:S(2)}, u32[]{:S(2)}) collective-permute-start(bf16[128,512]{1,0:T(8,128)(2,1)S(1)} %collective-permute-done.3.refs_4_.refs_9_), channel_id=1, source_target_pairs={{0,1},{1,0},{2,3},{3,2},{4,5},{5,4},{6,7},{7,6},{8,12},{9,13},{10,... | collective-permute-start | bytes 393224 | tf_op jit(solution)/shard_map/ppermute | solution.py:207
  16.3 0.3 collective-permute-done.2.refs_6_.refs_17_
  16.6 1.5 %collective-permute-start.11 = (bf16[128,512]{1,0:T(8,128)(2,1)S(1)}, bf16[128,512]{1,0:T(8,128)(2,1)S(1)}, u32[]{:S(2)}, u32[]{:S(2)}) collective-permute-start(bf16[128,512]{1,0:T(8,128)(2,1)S(1)} %collective-permute-done.2.refs_6_.refs_17_), channel_id=1, source_target_pairs={{0,1},{1,0},{2,3},{3,2},{4,5},{5,4},{6,7},{7,6},{8,10},{9,11},{10,... | collective-permute-start | bytes 393224 | tf_op jit(solution)/shard_map/ppermute | solution.py:207
  18.1 2.5 %collective-permute-start.6 = (bf16[128,512]{1,0:T(8,128)(2,1)S(1)}, bf16[128,512]{1,0:T(8,128)(2,1)S(1)}, u32[]{:S(2)}, u32[]{:S(2)}) collective-permute-start(bf16[128,512]{1,0:T(8,128)(2,1)S(1)} %collective-permute-done.2.refs_6_.refs_17_), channel_id=1, source_target_pairs={{0,1},{1,0},{2,3},{3,2},{4,5},{5,4},{6,7},{7,6},{8,12},{9,13},{10,... | collective-permute-start | bytes 393224 | tf_op jit(solution)/shard_map/ppermute | solution.py:207
  20.6 0.0 collective-permute-done.8.refs_3_.refs_8_
  20.6 0.5 %collective-permute-start.10 = (bf16[128,512]{1,0:T(8,128)(2,1)S(1)}, bf16[128,512]{1,0:T(8,128)(2,1)S(1)}, u32[]{:S(2)}, u32[]{:S(2)}) collective-permute-start(bf16[128,512]{1,0:T(8,128)(2,1)S(1)} %collective-permute-done.3.refs_4_.refs_9_), channel_id=1, source_target_pairs={{0,1},{1,0},{2,3},{3,2},{4,5},{5,4},{6,7},{7,6},{8,10},{9,11},{10,... | collective-permute-start | bytes 393224 | tf_op jit(solution)/shard_map/ppermute | solution.py:207
  21.1 0.0 collective-permute-done.9.refs_5_.refs_16_
  21.1 1.3 %step_2.1.refs_2_ = f32[4,768,256]{2,1,0:T(8,128)S(1)} custom-call(bf16[4,768,256]{2,1,0:T(8,128)(2,1)S(1)} %get-tuple-element.27.refs_0_, bf16[4,128,128]{2,1,0:T(8,128)(2,1)S(1)} %get-tuple-element.28.refs_1_, f32[4,768,256]{2,1,0:T(8,128)S(1)} %step_1.1.refs_2_, bf16[128,512]{1,0:T(8,128)(2,1)S(1)} %collective-permute-done.8.refs_3_.refs_8_, ...), custom_call_target="tpu_custom_call" | custom-call | flops 805306368 | bytes 3145728 | tf_op jit(solution)/shard_map/step_2/pallas_call | solution.py:284
  22.4 0.0 collective-permute-done.7.refs_4_.refs_11_
  22.4 0.1 collective-permute-start.12
  22.5 0.0 collective-permute-done.11.refs_5_.refs_18_
  22.5 2.2 %collective-permute-start.13 = (bf16[128,512]{1,0:T(8,128)(2,1)S(1)}, bf16[128,512]{1,0:T(8,128)(2,1)S(1)}, u32[]{:S(2)}, u32[]{:S(2)}) collective-permute-start(bf16[128,512]{1,0:T(8,128)(2,1)S(1)} %collective-permute-done.11.refs_5_.refs_18_), channel_id=1, source_target_pairs={{0,1},{1,0},{2,3},{3,2},{4,5},{5,4},{6,7},{7,6},{8,12},{9,13},{10,... | collective-permute-start | bytes 393224 | tf_op jit(solution)/shard_map/ppermute | solution.py:207
  24.7 0.0 collective-permute-done.6.refs_6_.refs_19_
  24.7 0.9 %collective-permute-done.10.refs_3_.refs_10_ = bf16[128,512]{1,0:T(8,128)(2,1)S(1)} collective-permute-done((bf16[128,512]{1,0:T(8,128)(2,1)S(1)}, bf16[128,512]{1,0:T(8,128)(2,1)S(1)}, u32[]{:S(2)}, u32[]{:S(2)}) %collective-permute-start.10) | collective-permute-done | bytes 131104 | tf_op jit(solution)/shard_map/ppermute | solution.py:207
  25.6 1.3 %step_3.1.refs_4_ = f32[4,768,256]{2,1,0:T(8,128)S(1)} custom-call(bf16[4,768,256]{2,1,0:T(8,128)(2,1)S(1)} %get-tuple-element.27.refs_0_, bf16[4,128,128]{2,1,0:T(8,128)(2,1)S(1)} %get-tuple-element.28.refs_1_, f32[4,768,256]{2,1,0:T(8,128)S(1)} %step_2.1.refs_2_, bf16[128,512]{1,0:T(8,128)(2,1)S(1)} %collective-permute-done.10.refs_3_.refs_10_, ...), custom_call_target="tpu_custom_call" | custom-call | flops 805306368 | bytes 3145728 | tf_op jit(solution)/shard_map/step_3/pallas_call | solution.py:284
  26.9 0.0 collective-permute-done.12.refs_12_
  26.9 2.1 %close.1 = (f32[4,768,128]{2,1,0:T(8,128)S(1)}, bf16[4,768,128]{2,1,0:T(8,128)(2,1)S(1)}, f32[24,128]{1,0:T(8,128)}) custom-call(bf16[4,768,256]{2,1,0:T(8,128)(2,1)S(1)} %get-tuple-element.27.refs_0_, bf16[4,128,128]{2,1,0:T(8,128)(2,1)S(1)} %get-tuple-element.28.refs_1_, f32[1,3072]{1,0:T(1,128)S(1)} %get-tuple-element.26.refs_2_.gate_row, ...), custom_call_target="tpu_custom_call" | custom-call | flops 402653184 | bytes 3145728 | tf_op jit(solution)/shard_map/close/pallas_call | solution.py:300
  29.0 0.0 collective-permute-done.13.refs_0_
  29.0 1.2 %mix.1 = bf16[128,3072]{1,0:T(8,128)(2,1)} custom-call(f32[1,3072]{1,0:T(1,128)S(1)} %get-tuple-element.26.refs_2_.gate_row, f32[4,768,128]{2,1,0:T(8,128)S(1)} %get-tuple-element.45.part, bf16[4,768,128]{2,1,0:T(8,128)(2,1)S(1)} %get-tuple-element.46.last_weight, bf16[128,512]{1,0:T(8,128)(2,1)S(1)} %collective-permute-done.13.refs_0_), custom_call_target="tpu_custom_call" | custom-call | flops 402653184 | bytes 3145728 | tf_op jit(solution)/shard_map/mix/pallas_call | solution.py:313
  (1 shorter events, 0.0 us)
Async XLA Ops:
  0.6 3.4 %copy-start.1 = (bf16[128,512]{1,0:T(8,128)(2,1)S(1)}, bf16[128,512]{1,0:T(8,128)(2,1)}, u32[]{:S(2)}) copy-start(bf16[128,512]{1,0:T(8,128)(2,1)} %refs_13_.1) | copy-start | bytes 393220
  0.6 1.9 %copy-start = (bf16[128,512]{1,0:T(8,128)(2,1)S(1)}, bf16[128,512]{1,0:T(8,128)(2,1)}, u32[]{:S(2)}) copy-start(bf16[128,512]{1,0:T(8,128)(2,1)} %refs_5_.3) | copy-start | bytes 393220
  0.7 3.9 %copy-start.4 = (s32[4,4]{1,0:T(4,128)S(1)}, s32[4,4]{1,0:T(4,128)}, u32[]{:S(2)}) copy-start(s32[4,4]{1,0:T(4,128)} %refs_0_.1) | copy-start | bytes 196
  0.7 3.9 %copy-start.5 = (s32[4]{0:T(128)S(1)}, s32[4]{0:T(128)}, u32[]{:S(2)}) copy-start(s32[4]{0:T(128)} %refs_1_.1) | copy-start | bytes 52
  0.7 3.9 %copy-start.3 = (f32[4,3072]{1,0:T(4,128)S(1)}, f32[4,3072]{1,0:T(4,128)}, u32[]{:S(2)}) copy-start(f32[4,3072]{1,0:T(4,128)} %refs_2_.1) | copy-start | bytes 147460
  0.7 3.9 %copy-start.2 = (bf16[128,3072]{1,0:T(8,128)(2,1)S(1)}, bf16[128,3072]{1,0:T(8,128)(2,1)}, u32[]{:S(2)}) copy-start(bf16[128,3072]{1,0:T(8,128)(2,1)} %refs_4_.1) | copy-start | bytes 2359300
  0.7 9.9 %collective-permute-start = (bf16[128,512]{1,0:T(8,128)(2,1)}, bf16[128,512]{1,0:T(8,128)(2,1)S(1)}, u32[]{:S(2)}, u32[]{:S(2)}) collective-permute-start(bf16[128,512]{1,0:T(8,128)(2,1)} %refs_13_.1), channel_id=1, source_target_pairs={{0,4},{1,5},{2,6},{3,7},{4,8},{5,9},{6,10},{7,11},{8,12},{9,13},{1... | collective-permute-start | bytes 393224 | tf_op jit(solution)/shard_map/ppermute | solution.py:207
  2.3 6.7 %collective-permute-start.1 = (bf16[128,512]{1,0:T(8,128)(2,1)}, bf16[128,512]{1,0:T(8,128)(2,1)S(1)}, u32[]{:S(2)}, u32[]{:S(2)}) collective-permute-start(bf16[128,512]{1,0:T(8,128)(2,1)} %refs_5_.3), channel_id=1, source_target_pairs={{0,4},{1,5},{2,6},{3,7},{4,8},{5,9},{6,10},{7,11},{8,12},{9,13},{1... | collective-permute-start | bytes 393224 | tf_op jit(solution)/shard_map/ppermute | solution.py:207
  2.5 10.7 %collective-permute-start.4 = (bf16[128,512]{1,0:T(8,128)(2,1)S(1)}, bf16[128,512]{1,0:T(8,128)(2,1)S(1)}, u32[]{:S(2)}, u32[]{:S(2)}) collective-permute-start(bf16[128,512]{1,0:T(8,128)(2,1)S(1)} %copy-done), channel_id=1, source_target_pairs={{0,2},{1,3},{2,0},{3,1},{4,6},{5,7},{6,4},{7,5},{8,10},{9,11},{10,... | collective-permute-start | bytes 393224 | tf_op jit(solution)/shard_map/ppermute | solution.py:207
  4.1 9.7 %collective-permute-start.5 = (bf16[128,512]{1,0:T(8,128)(2,1)S(1)}, bf16[128,512]{1,0:T(8,128)(2,1)S(1)}, u32[]{:S(2)}, u32[]{:S(2)}) collective-permute-start(bf16[128,512]{1,0:T(8,128)(2,1)S(1)} %copy-done.1), channel_id=1, source_target_pairs={{0,2},{1,3},{2,0},{3,1},{4,6},{5,7},{6,4},{7,5},{8,10},{9,11},{10,... | collective-permute-start | bytes 393224 | tf_op jit(solution)/shard_map/ppermute | solution.py:207
  9.0 6.0 %collective-permute-start.3 = (bf16[128,512]{1,0:T(8,128)(2,1)S(1)}, bf16[128,512]{1,0:T(8,128)(2,1)S(1)}, u32[]{:S(2)}, u32[]{:S(2)}) collective-permute-start(bf16[128,512]{1,0:T(8,128)(2,1)S(1)} %collective-permute-done.1.refs_4_.refs_7_), channel_id=1, source_target_pairs={{0,1},{1,0},{2,3},{3,2},{4,8},{5,9},{6,10},{7,11},{8,12},{9,13},{1... | collective-permute-start | bytes 393224 | tf_op jit(solution)/shard_map/ppermute | solution.py:207
  10.6 6.0 %collective-permute-start.2 = (bf16[128,512]{1,0:T(8,128)(2,1)S(1)}, bf16[128,512]{1,0:T(8,128)(2,1)S(1)}, u32[]{:S(2)}, u32[]{:S(2)}) collective-permute-start(bf16[128,512]{1,0:T(8,128)(2,1)S(1)} %collective-permute-done.refs_6_.refs_15_), channel_id=1, source_target_pairs={{0,1},{1,0},{2,3},{3,2},{4,8},{5,9},{6,10},{7,11},{8,12},{9,13},{1... | collective-permute-start | bytes 393224 | tf_op jit(solution)/shard_map/ppermute | solution.py:207
  11.7 8.9 %collective-permute-start.8 = (bf16[128,512]{1,0:T(8,128)(2,1)S(1)}, bf16[128,512]{1,0:T(8,128)(2,1)S(1)}, u32[]{:S(2)}, u32[]{:S(2)}) collective-permute-start(bf16[128,512]{1,0:T(8,128)(2,1)S(1)} %collective-permute-done.1.refs_4_.refs_7_), channel_id=1, source_target_pairs={{0,1},{1,0},{2,3},{3,2},{4,6},{5,7},{6,4},{7,5},{8,10},{9,11},{10,... | collective-permute-start | bytes 393224 | tf_op jit(solution)/shard_map/ppermute | solution.py:207
  13.2 7.9 %collective-permute-start.9 = (bf16[128,512]{1,0:T(8,128)(2,1)S(1)}, bf16[128,512]{1,0:T(8,128)(2,1)S(1)}, u32[]{:S(2)}, u32[]{:S(2)}) collective-permute-start(bf16[128,512]{1,0:T(8,128)(2,1)S(1)} %collective-permute-done.refs_6_.refs_15_), channel_id=1, source_target_pairs={{0,1},{1,0},{2,3},{3,2},{4,6},{5,7},{6,4},{7,5},{8,10},{9,11},{10,... | collective-permute-start | bytes 393224 | tf_op jit(solution)/shard_map/ppermute | solution.py:207
  15.1 7.3 %collective-permute-start.7 = (bf16[128,512]{1,0:T(8,128)(2,1)S(1)}, bf16[128,512]{1,0:T(8,128)(2,1)S(1)}, u32[]{:S(2)}, u32[]{:S(2)}) collective-permute-start(bf16[128,512]{1,0:T(8,128)(2,1)S(1)} %collective-permute-done.3.refs_4_.refs_9_), channel_id=1, source_target_pairs={{0,1},{1,0},{2,3},{3,2},{4,5},{5,4},{6,7},{7,6},{8,12},{9,13},{10,... | collective-permute-start | bytes 393224 | tf_op jit(solution)/shard_map/ppermute | solution.py:207
  16.6 5.9 %collective-permute-start.11 = (bf16[128,512]{1,0:T(8,128)(2,1)S(1)}, bf16[128,512]{1,0:T(8,128)(2,1)S(1)}, u32[]{:S(2)}, u32[]{:S(2)}) collective-permute-start(bf16[128,512]{1,0:T(8,128)(2,1)S(1)} %collective-permute-done.2.refs_6_.refs_17_), channel_id=1, source_target_pairs={{0,1},{1,0},{2,3},{3,2},{4,5},{5,4},{6,7},{7,6},{8,10},{9,11},{10,... | collective-permute-start | bytes 393224 | tf_op jit(solution)/shard_map/ppermute | solution.py:207
  18.1 6.6 %collective-permute-start.6 = (bf16[128,512]{1,0:T(8,128)(2,1)S(1)}, bf16[128,512]{1,0:T(8,128)(2,1)S(1)}, u32[]{:S(2)}, u32[]{:S(2)}) collective-permute-start(bf16[128,512]{1,0:T(8,128)(2,1)S(1)} %collective-permute-done.2.refs_6_.refs_17_), channel_id=1, source_target_pairs={{0,1},{1,0},{2,3},{3,2},{4,5},{5,4},{6,7},{7,6},{8,12},{9,13},{10,... | collective-permute-start | bytes 393224 | tf_op jit(solution)/shard_map/ppermute | solution.py:207
  20.6 5.0 %collective-permute-start.10 = (bf16[128,512]{1,0:T(8,128)(2,1)S(1)}, bf16[128,512]{1,0:T(8,128)(2,1)S(1)}, u32[]{:S(2)}, u32[]{:S(2)}) collective-permute-start(bf16[128,512]{1,0:T(8,128)(2,1)S(1)} %collective-permute-done.3.refs_4_.refs_9_), channel_id=1, source_target_pairs={{0,1},{1,0},{2,3},{3,2},{4,5},{5,4},{6,7},{7,6},{8,10},{9,11},{10,... | collective-permute-start | bytes 393224 | tf_op jit(solution)/shard_map/ppermute | solution.py:207
  22.4 4.5 %collective-permute-start.12 = (bf16[128,512]{1,0:T(8,128)(2,1)S(1)}, bf16[128,512]{1,0:T(8,128)(2,1)S(1)}, u32[]{:S(2)}, u32[]{:S(2)}) collective-permute-start(bf16[128,512]{1,0:T(8,128)(2,1)S(1)} %collective-permute-done.7.refs_4_.refs_11_), channel_id=1, source_target_pairs={{0,1},{1,0},{2,3},{3,2},{4,5},{5,4},{6,7},{7,6},{8,9},{9,8},{10,11... | collective-permute-start | bytes 393224 | tf_op jit(solution)/shard_map/ppermute | solution.py:207
  22.5 6.5 %collective-permute-start.13 = (bf16[128,512]{1,0:T(8,128)(2,1)S(1)}, bf16[128,512]{1,0:T(8,128)(2,1)S(1)}, u32[]{:S(2)}, u32[]{:S(2)}) collective-permute-start(bf16[128,512]{1,0:T(8,128)(2,1)S(1)} %collective-permute-done.11.refs_5_.refs_18_), channel_id=1, source_target_pairs={{0,1},{1,0},{2,3},{3,2},{4,5},{5,4},{6,7},{7,6},{8,12},{9,13},{10,... | collective-permute-start | bytes 393224 | tf_op jit(solution)/shard_map/ppermute | solution.py:207

commit v3 on v2

--- a/solution.py
+++ b/solution.py
@@ -56,24 +56,20 @@
         copy.wait()
     rows, width = q.shape[0], stacked.shape[1]
     group = width // rows
-    every_top = jnp.zeros((rows, HEAD_SIZE), jnp.float32)
-    at, beside = lanes(rows), lanes(width)
+    at = lanes(1)
     for h in range(stacked.shape[0]):
         queries = jnp.concatenate([q[:, head_columns(h * group + g)] for g in range(group)], axis=0)
         score = against(queries, k[:, head_columns(h)])
-        top = jnp.maximum(floor[0:1, 0:1], jnp.max(score, axis=1, keepdims=True))
+        top = jnp.maximum(floor[0:1, 0:1], jnp.max(jnp.max(score, axis=0, keepdims=True), axis=1, keepdims=True))
         weight = jnp.exp2(SCALE * (score - top)).astype(jnp.bfloat16)
         acc[h] = jnp.dot(weight, with_ones(v[:, head_columns(h)]), preferred_element_type=jnp.float32)
         high = top.astype(jnp.bfloat16).astype(jnp.float32)
         middle = (top - high).astype(jnp.bfloat16).astype(jnp.float32)
         low = top - high - middle
-        extra = jnp.where(
-            beside == 0, -high, jnp.where(beside == 1, -middle, jnp.where(beside == 2, -low, jnp.where(beside == 3, 1.0, 0.0)))
-        )
-        stacked[h] = jnp.concatenate([queries, extra.astype(jnp.bfloat16)], axis=1)
-        for g in range(group):
-            every_top = jnp.where(at == h * group + g, top[g * rows : (g + 1) * rows, :], every_top)
-    tops[...] = every_top.T[: tops.shape[0], :] * (1.0 / math.sqrt(HEAD_SIZE))
+        extra = jnp.where(at == 0, -high, jnp.where(at == 1, -middle, jnp.where(at == 2, -low, jnp.where(at == 3, 1.0, 0.0))))
+        extra = jnp.broadcast_to(extra, (width, HEAD_SIZE)).astype(jnp.bfloat16)
+        stacked[h] = jnp.concatenate([queries, extra], axis=1)
+        tops[h * group : (h + 1) * group, :] = jnp.broadcast_to(top * (1.0 / math.sqrt(HEAD_SIZE)), (group, rows))
 
 
 def weights_of(h, distances, stacked, tails, key_refs):
@@ -109,7 +105,8 @@
         weight = weights_of(h, distances[-last:], stacked, tails, key_refs[-last:])
         ones = jnp.ones((weight.shape[1], HEAD_SIZE), jnp.bfloat16)
         total = acc[h, :, HEAD_SIZE:] + jnp.dot(weight.astype(jnp.bfloat16), ones, preferred_element_type=jnp.float32)
-        inverse = 1.0 / total
+        inverse = pl.reciprocal(total, approx=True)
+        inverse = inverse * (2.0 - total * inverse)
         for i in range(last):
             last_weight[h, :, head_columns(i)] = (weight[:, head_columns(i)] * inverse).astype(jnp.bfloat16)
         attended = acc[h, :, :HEAD_SIZE] * inverse
@@ -117,7 +114,8 @@
             gated(h, g, attended)
             every_total = jnp.where(at == h * group + g, total[g * rows : (g + 1) * rows, :], every_total)
     log_ref[...] = tops[...] + jnp.log(every_total.T[:heads, :])
-    outside = jnp.max(jnp.where(every_total <= LIMIT, 0.0, 1.0))
+    fits = jnp.logical_and(every_total <= LIMIT, every_total >= 1.0 / LIMIT)
+    outside = jnp.max(jnp.where(fits, 0.0, 1.0))
 
     @pl.when(outside > 0.0)
     def _():
@@ -193,18 +191,18 @@
             flops=4 * times * blocks * rows * rows * wide, bytes_accessed=rows * wide * 8, transcendentals=blocks * rows * rows * heads
         )
 
-    cores = lax.axis_size("head")
+    cores, clips = lax.axis_size("head"), lax.axis_size("grp")
 
     def send(value, target):
         pairs = []
-        for i in range(count):
-            for core in range(cores):
-                if target(i) is None:
-                    goal = i * cores + (core + 1) % cores if cores > 1 else i
-                else:
-                    goal = target(i) * cores + core
-                pairs.append((i * cores + core, goal))
-        return lax.ppermute(value, ("tm", "head"), pairs)
+        for clip in range(clips):
+            for i in range(count):
+                for core in range(cores):
+                    goal = (clip, target(i), core)
+                    if target(i) is None:
+                        goal = ((clip + 1) % clips, i, core if clips > 1 else (core + 1) % cores)
+                    pairs.append(tuple((c * count + j) * cores + k for c, j, k in ((clip, i, core), goal)))
+        return lax.ppermute(value, ("grp", "tm", "head"), pairs)
 
     def onward(value, distance):
         first = (distance - 1) * per_span
@@ -221,12 +219,16 @@
             value, lambda i: i - i % per_span + (i + turn) % per_span if i >= distance * per_span else None
         )
 
-    def travel(held, distance, turned_before):
-        onwards = [onward(x, distance + 1) for x in held] if distance + 1 < spans else []
-        turned = [[around(x, distance, turn) for turn in range(1, per_span)] for x in held]
-        if not onwards and turned_before:
-            turned[1] = [onward(v, distance) for _, v in turned_before]
-        return list(zip(*turned)), onwards
+    def leap(value):
+        far = (spans - 1) * per_span
+
+        def target(i):
+            return i + far if i < per_span else i - far if i >= far else None
+
+        return send(value, target)
+
+    def exchange(held, distance):
+        return list(zip(*[[around(x, distance, turn) for turn in range(1, per_span)] for x in held]))
 
     floor = pl.pallas_call(
         floor_kernel,
@@ -236,9 +238,10 @@
         cost_estimate=cost(4, 10),
         name="floor",
     )()
-    held = [onward(x, 1) for x in (keys, values)] if spans > 1 else []
+    held = [onward(x, 1) for x in (keys, values)] if spans > 2 else []
     near_keys, near_values, floor = lax.optimization_barrier((keys, values, floor))
-    turned = list(zip(*[[around(x, 0, turn) for turn in range(1, per_span)] for x in (near_keys, near_values)]))
+    turned = exchange((near_keys, near_values), 0)
+    beside_keys = [k for k, _ in turned]
     def own(*refs):
         own_kernel(per_span, *refs)
 
@@ -265,43 +268,63 @@
     )(span_mask, section, section_gate, floor, queries, keys, values)
 
     seen_blocks = [(0, (keys, values))]
-    for distance in range(1, spans):
+
+    def advance(acc, blocks):
+        seen_blocks.extend(blocks)
+        operands = [k for _, (k, _) in blocks] + [v for _, (_, v) in blocks]
+
+        def step(*refs):
+            step_kernel([d for d, _ in blocks], *refs)
+
+        return pl.pallas_call(
+            step,
+            out_shape=acc_shape,
+            in_specs=[VMEM] * (3 + len(operands)),
+            out_specs=VMEM,
+            compiler_params=params,
+            cost_estimate=cost(len(blocks)),
+            name="step_%d" % blocks[-1][0],
+        )(stacked, tails, acc, *operands)
+
+    def far_sends(acc):
+        sent = []
+        for x in [keys, values] + beside_keys:
+            x, acc = lax.optimization_barrier((x, acc))
+            sent.append(leap(x))
+        return acc, sent[:2], sent[2:]
+
+    far_held = None
+    for distance in range(1, spans - 1):
         waiting = [(distance - 1, t) for t in turned]
         forward = []
         for x in held:
             x, acc = lax.optimization_barrier((x, acc))
             forward.append(x)
-        held = forward
-        waiting.append((distance, tuple(held)))
-        turned, held = travel(held, distance, turned)
-        distances = [d for d, _ in waiting]
-        blocks = [k for _, (k, _) in waiting] + [v for _, (_, v) in waiting]
-        seen_blocks += waiting
-
-        def step(*refs, distances=distances):
-            step_kernel(distances, *refs)
-
-        acc = pl.pallas_call(
-            step,
-            out_shape=acc_shape,
-            in_specs=[VMEM] * (3 + len(blocks)),
-            out_specs=VMEM,
-            compiler_params=params,
-            cost_estimate=cost(len(waiting)),
-            name="step_%d" % distance,
-        )(stacked, tails, acc, *blocks)
-
-    distances = [d for d, _ in seen_blocks] + [spans - 1] * len(turned)
+        waiting.append((distance, tuple(forward)))
+        held = [onward(x, distance + 1) for x in forward] if distance + 2 < spans else []
+        turned = exchange(forward, distance)
+        acc = advance(acc, waiting)
+        if far_held is None:
+            acc, far_held, far_keys = far_sends(acc)
+    last_blocks = [(max(spans - 2, 0), t) for t in turned]
+    if spans > 1:
+        if far_held is None:
+            acc, far_held, far_keys = far_sends(acc)
+        far_values = [around(far_held[1], spans - 1, turn) for turn in range(1, per_span)]
+        acc = advance(acc, [(spans - 1, tuple(far_held))])
+        last_blocks += [(spans - 1, t) for t in zip(far_keys, far_values)]
+
+    distances = [d for d, _ in seen_blocks + last_blocks]
 
     def close(*refs):
-        close_kernel(distances, len(turned), *refs)
-
-    blocks = [k for _, (k, _) in seen_blocks] + [k for k, _ in turned] + [v for _, (_, v) in seen_blocks]
+        close_kernel(distances, len(last_blocks), *refs)
+
+    blocks = [k for _, (k, _) in seen_blocks + last_blocks] + [v for _, (_, v) in seen_blocks]
     part, last_weight, log_total = pl.pallas_call(
         close,
         out_shape=(
             jax.ShapeDtypeStruct((kv_heads, width, HEAD_SIZE), jnp.float32),
-            jax.ShapeDtypeStruct((kv_heads, width, len(turned) * rows), jnp.bfloat16),
+            jax.ShapeDtypeStruct((kv_heads, width, len(last_blocks) * rows), jnp.bfloat16),
             jax.ShapeDtypeStruct((heads, rows), jnp.float32),
         ),
         in_specs=[VMEM] * (5 + len(blocks)),
@@ -313,13 +336,13 @@
     mixed = pl.pallas_call(
         mix_kernel,
         out_shape=jax.ShapeDtypeStruct((rows, wide), jnp.bfloat16),
-        in_specs=[VMEM] * (3 + len(turned)),
+        in_specs=[VMEM] * (3 + len(last_blocks)),
         out_specs=HBM,
         scratch_shapes=[pltpu.VMEM((rows, wide), jnp.bfloat16), pltpu.SemaphoreType.DMA((kv_heads,))],
         compiler_params=params,
         cost_estimate=cost(1),
         name="mix",
-    )(gate_row, part, last_weight, *[v for _, v in turned])
+    )(gate_row, part, last_weight, *[v for _, (_, v) in last_blocks])
     return mixed, log_total
 
 

time: 30.3 us -> 45.4 us (1.50)
  the two profiles are of different devices: /device:TPU:18 before, /device:TPU:0 now
where the time goes in v3:
time: 45.4 us; the launch traced here: 45.2 us
  starting transfers between devices  19.5 us (43%)
  Pallas kernels  18.3 us (40%)
  waiting for transfers between devices  6.67 us (15%)
  between operations  0.75 us (2%)
    ppermute x14, starting transfers between devices, send(): return lax.ppermute(value, ('grp', 'tm', 'head'), pairs)  19.5 us
    pallas_call x1, Pallas kernels, on_device(): pl.pallas_call(close, out_shape=(jax.ShapeDtypeStruct((kv_heads, width, H...  10.2 us
    ppermute x14, waiting for transfers between devices, send(): return lax.ppermute(value, ('grp', 'tm', 'head'), pairs)  6.67 us
    pallas_call x3, Pallas kernels, advance(): pl.pallas_call(step, out_shape=acc_shape, in_specs=[VMEM] * (3 + len(oper...  3.77 us
    pallas_call x1, Pallas kernels, on_device(): pl.pallas_call(own, out_shape=(jax.ShapeDtypeStruct((kv_heads, width, 2 *...  2.92 us
    pallas_call x1, Pallas kernels, on_device(): pl.pallas_call(mix_kernel, out_shape=jax.ShapeDtypeStruct((rows, wide), j...  1.42 us
  transfers between devices with their start and end apart: 14, of which 2 were waited for; matrix products, arithmetic and copies ran while one was open for 0% of the time, Pallas kernels for 37%

profile of v3, /device:TPU:0, one launch (start us, length us, event | category | flops | bytes accessed | tf_op | source)
XLA Modules:
  0.0 45.2 jit_solution(9480861034297432243)
XLA Ops:
  0.6 0.0 copy-start
  0.6 0.0 copy-start.1
  0.7 0.0 copy-start.5
  0.7 0.0 copy-start.3
  0.7 0.0 copy-start.2
  0.7 0.0 copy-start.4
  0.7 3.1 %collective-permute-start.1 = (bf16[128,512]{1,0:T(8,128)(2,1)}, bf16[128,512]{1,0:T(8,128)(2,1)S(1)}, u32[]{:S(2)}, u32[]{:S(2)}) collective-permute-start(bf16[128,512]{1,0:T(8,128)(2,1)} %refs_5_.3), channel_id=1, source_target_pairs={{0,4},{1,5},{2,6},{3,7},{4,8},{5,9},{6,10},{7,11},{8,12},{9,13},{1... | collective-permute-start | bytes 393224 | tf_op jit(solution)/shard_map/ppermute | solution.py:205
  3.8 1.6 %collective-permute-start = (bf16[128,512]{1,0:T(8,128)(2,1)}, bf16[128,512]{1,0:T(8,128)(2,1)S(1)}, u32[]{:S(2)}, u32[]{:S(2)}) collective-permute-start(bf16[128,512]{1,0:T(8,128)(2,1)} %refs_13_.1), channel_id=1, source_target_pairs={{0,4},{1,5},{2,6},{3,7},{4,8},{5,9},{6,10},{7,11},{8,12},{9,13},{1... | collective-permute-start | bytes 393224 | tf_op jit(solution)/shard_map/ppermute | solution.py:205
  5.3 0.0 copy-done
  5.4 1.5 %collective-permute-start.4 = (bf16[128,512]{1,0:T(8,128)(2,1)S(1)}, bf16[128,512]{1,0:T(8,128)(2,1)S(1)}, u32[]{:S(2)}, u32[]{:S(2)}) collective-permute-start(bf16[128,512]{1,0:T(8,128)(2,1)S(1)} %copy-done), channel_id=1, source_target_pairs={{0,2},{1,3},{2,0},{3,1},{4,6},{5,7},{6,4},{7,5},{8,10},{9,11},{10,... | collective-permute-start | bytes 393224 | tf_op jit(solution)/shard_map/ppermute | solution.py:205
  6.9 0.0 copy-done.1
  6.9 0.5 %collective-permute-start.5 = (bf16[128,512]{1,0:T(8,128)(2,1)S(1)}, bf16[128,512]{1,0:T(8,128)(2,1)S(1)}, u32[]{:S(2)}, u32[]{:S(2)}) collective-permute-start(bf16[128,512]{1,0:T(8,128)(2,1)S(1)} %copy-done.1), channel_id=1, source_target_pairs={{0,2},{1,3},{2,0},{3,1},{4,6},{5,7},{6,4},{7,5},{8,10},{9,11},{10,... | collective-permute-start | bytes 393224 | tf_op jit(solution)/shard_map/ppermute | solution.py:205
  7.4 0.0 copy-done.5
  7.4 0.0 copy-done.3
  7.4 0.0 copy-done.2
  7.4 0.0 copy-done.4
  7.4 2.9 %own.1 = (bf16[4,768,256]{2,1,0:T(8,128)(2,1)S(1)}, bf16[4,128,128]{2,1,0:T(8,128)(2,1)S(1)}, f32[1,3072]{1,0:T(1,128)S(1)}, f32[24,128]{1,0:T(8,128)S(1)}, f32[4,768,256]{2,1,0:T(8,128)S(1)}) custom-call(s32[4,4]{1,0:T(4,128)S(1)} %copy-done.4, s32[4]{0:T(128)S(1)} %copy-done.5, f32[4,3072]{1,0:T(4,128)S(1)} %copy-done.3, f32[8,768]{1,0:T(8,128)S(1)} %floor.1.refs_3_, ...), custom_call_target="tpu_custom_call" | custom-call | flops 2013265920 | bytes 3145728 | tf_op jit(solution)/shard_map/own/pallas_call | solution.py:248
  10.3 0.0 collective-permute-done.1.refs_4_.refs_7_
  10.3 2.0 %collective-permute-done.refs_6_.refs_15_ = bf16[128,512]{1,0:T(8,128)(2,1)S(1)} collective-permute-done((bf16[128,512]{1,0:T(8,128)(2,1)}, bf16[128,512]{1,0:T(8,128)(2,1)S(1)}, u32[]{:S(2)}, u32[]{:S(2)}) %collective-permute-start) | collective-permute-done | bytes 131104 | tf_op jit(solution)/shard_map/ppermute | solution.py:205
  12.3 1.5 %collective-permute-start.2 = (bf16[128,512]{1,0:T(8,128)(2,1)S(1)}, bf16[128,512]{1,0:T(8,128)(2,1)S(1)}, u32[]{:S(2)}, u32[]{:S(2)}) collective-permute-start(bf16[128,512]{1,0:T(8,128)(2,1)S(1)} %collective-permute-done.refs_6_.refs_15_), channel_id=1, source_target_pairs={{0,16},{1,17},{2,18},{3,19},{4,8},{5,9},{6,10},{7,11},{8,12},{9,13... | collective-permute-start | bytes 393224 | tf_op jit(solution)/shard_map/ppermute | solution.py:205
  13.8 0.5 %collective-permute-start.7 = (bf16[128,512]{1,0:T(8,128)(2,1)S(1)}, bf16[128,512]{1,0:T(8,128)(2,1)S(1)}, u32[]{:S(2)}, u32[]{:S(2)}) collective-permute-start(bf16[128,512]{1,0:T(8,128)(2,1)S(1)} %collective-permute-done.refs_6_.refs_15_), channel_id=1, source_target_pairs={{0,16},{1,17},{2,18},{3,19},{4,6},{5,7},{6,4},{7,5},{8,10},{9,11},... | collective-permute-start | bytes 393224 | tf_op jit(solution)/shard_map/ppermute | solution.py:205
  14.3 1.5 %collective-permute-start.3 = (bf16[128,512]{1,0:T(8,128)(2,1)S(1)}, bf16[128,512]{1,0:T(8,128)(2,1)S(1)}, u32[]{:S(2)}, u32[]{:S(2)}) collective-permute-start(bf16[128,512]{1,0:T(8,128)(2,1)S(1)} %collective-permute-done.1.refs_4_.refs_7_), channel_id=1, source_target_pairs={{0,16},{1,17},{2,18},{3,19},{4,8},{5,9},{6,10},{7,11},{8,12},{9,13... | collective-permute-start | bytes 393224 | tf_op jit(solution)/shard_map/ppermute | solution.py:205
  15.8 0.0 collective-permute-done.4.refs_3_.refs_6_
  15.8 0.5 %collective-permute-start.6 = (bf16[128,512]{1,0:T(8,128)(2,1)S(1)}, bf16[128,512]{1,0:T(8,128)(2,1)S(1)}, u32[]{:S(2)}, u32[]{:S(2)}) collective-permute-start(bf16[128,512]{1,0:T(8,128)(2,1)S(1)} %collective-permute-done.1.refs_4_.refs_7_), channel_id=1, source_target_pairs={{0,16},{1,17},{2,18},{3,19},{4,6},{5,7},{6,4},{7,5},{8,10},{9,11},... | collective-permute-start | bytes 393224 | tf_op jit(solution)/shard_map/ppermute | solution.py:205
  16.4 0.0 collective-permute-done.5.refs_5_.refs_14_
  16.4 1.3 %step_1.1.refs_2_ = f32[4,768,256]{2,1,0:T(8,128)S(1)} custom-call(bf16[4,768,256]{2,1,0:T(8,128)(2,1)S(1)} %get-tuple-element.29.refs_0_, bf16[4,128,128]{2,1,0:T(8,128)(2,1)S(1)} %get-tuple-element.30.refs_1_, f32[4,768,256]{2,1,0:T(8,128)S(1)} %get-tuple-element.37.refs_2_, bf16[128,512]{1,0:T(8,128)(2,1)S(1)} %collective-permute-done.4.refs_3_.refs_6_, ...), custom_call_target="tpu_custom_call" | custom-call | flops 805306368 | bytes 3145728 | tf_op jit(solution)/shard_map/step_1/pallas_call | solution.py:279
  17.7 1.7 %collective-permute-start.9 = (bf16[128,512]{1,0:T(8,128)(2,1)S(1)}, bf16[128,512]{1,0:T(8,128)(2,1)S(1)}, u32[]{:S(2)}, u32[]{:S(2)}) collective-permute-start(bf16[128,512]{1,0:T(8,128)(2,1)S(1)} %copy-done.1), channel_id=1, source_target_pairs={{0,12},{1,13},{2,14},{3,15},{4,20},{5,21},{6,22},{7,23},{8,24},{9,... | collective-permute-start | bytes 393224 | tf_op jit(solution)/shard_map/ppermute | solution.py:205
  19.4 4.7 %collective-permute-done.3.refs_4_.refs_9_ = bf16[128,512]{1,0:T(8,128)(2,1)S(1)} collective-permute-done((bf16[128,512]{1,0:T(8,128)(2,1)S(1)}, bf16[128,512]{1,0:T(8,128)(2,1)S(1)}, u32[]{:S(2)}, u32[]{:S(2)}) %collective-permute-start.3) | collective-permute-done | bytes 131104 | tf_op jit(solution)/shard_map/ppermute | solution.py:205
  24.0 0.0 collective-permute-start.8
  24.0 0.0 collective-permute-done.2.refs_6_.refs_17_
  24.0 3.8 %collective-permute-start.11 = (bf16[128,512]{1,0:T(8,128)(2,1)S(1)}, bf16[128,512]{1,0:T(8,128)(2,1)S(1)}, u32[]{:S(2)}, u32[]{:S(2)}) collective-permute-start(bf16[128,512]{1,0:T(8,128)(2,1)S(1)} %collective-permute-done.4.refs_3_.refs_6_), channel_id=1, source_target_pairs={{0,12},{1,13},{2,14},{3,15},{4,20},{5,21},{6,22},{7,23},{8,24},{9,... | collective-permute-start | bytes 393224 | tf_op jit(solution)/shard_map/ppermute | solution.py:205
  27.8 0.0 collective-permute-done.7.refs_5_.refs_16_
  27.8 1.2 %collective-permute-start.10 = (bf16[128,512]{1,0:T(8,128)(2,1)S(1)}, bf16[128,512]{1,0:T(8,128)(2,1)S(1)}, u32[]{:S(2)}, u32[]{:S(2)}) collective-permute-start(bf16[128,512]{1,0:T(8,128)(2,1)S(1)} %collective-permute-done.3.refs_4_.refs_9_), channel_id=1, source_target_pairs={{0,16},{1,17},{2,18},{3,19},{4,20},{5,21},{6,22},{7,23},{8,10},{9,... | collective-permute-start | bytes 393224 | tf_op jit(solution)/shard_map/ppermute | solution.py:205
  29.1 0.0 collective-permute-done.6.refs_3_.refs_8_
  29.1 0.8 %collective-permute-start.12 = (bf16[128,512]{1,0:T(8,128)(2,1)S(1)}, bf16[128,512]{1,0:T(8,128)(2,1)S(1)}, u32[]{:S(2)}, u32[]{:S(2)}) collective-permute-start(bf16[128,512]{1,0:T(8,128)(2,1)S(1)} %collective-permute-done.2.refs_6_.refs_17_), channel_id=1, source_target_pairs={{0,16},{1,17},{2,18},{3,19},{4,20},{5,21},{6,22},{7,23},{8,10},{9,... | collective-permute-start | bytes 393224 | tf_op jit(solution)/shard_map/ppermute | solution.py:205
  29.9 0.0 collective-permute-done.9.refs_4_.refs_18_
  29.9 1.2 %collective-permute-start.13 = (bf16[128,512]{1,0:T(8,128)(2,1)S(1)}, bf16[128,512]{1,0:T(8,128)(2,1)S(1)}, u32[]{:S(2)}, u32[]{:S(2)}) collective-permute-start(bf16[128,512]{1,0:T(8,128)(2,1)S(1)} %collective-permute-done.9.refs_4_.refs_18_), channel_id=1, source_target_pairs={{0,16},{1,17},{2,18},{3,19},{4,20},{5,21},{6,22},{7,23},{8,24},{9,... | collective-permute-start | bytes 393224 | tf_op jit(solution)/shard_map/ppermute | solution.py:205
  31.1 1.3 %step_2.1.refs_2_ = f32[4,768,256]{2,1,0:T(8,128)S(1)} custom-call(bf16[4,768,256]{2,1,0:T(8,128)(2,1)S(1)} %get-tuple-element.29.refs_0_, bf16[4,128,128]{2,1,0:T(8,128)(2,1)S(1)} %get-tuple-element.30.refs_1_, f32[4,768,256]{2,1,0:T(8,128)S(1)} %step_1.1.refs_2_, bf16[128,512]{1,0:T(8,128)(2,1)S(1)} %collective-permute-done.6.refs_3_.refs_8_, ...), custom_call_target="tpu_custom_call" | custom-call | flops 805306368 | bytes 3145728 | tf_op jit(solution)/shard_map/step_2/pallas_call | solution.py:279
  32.4 0.0 collective-permute-done.8.refs_3_.refs_10_
  32.4 1.2 %step_3.1.refs_4_ = f32[4,768,256]{2,1,0:T(8,128)S(1)} custom-call(bf16[4,768,256]{2,1,0:T(8,128)(2,1)S(1)} %get-tuple-element.29.refs_0_, bf16[4,128,128]{2,1,0:T(8,128)(2,1)S(1)} %get-tuple-element.30.refs_1_, f32[4,768,256]{2,1,0:T(8,128)S(1)} %step_2.1.refs_2_, bf16[128,512]{1,0:T(8,128)(2,1)S(1)} %collective-permute-done.8.refs_3_.refs_10_, ...), custom_call_target="tpu_custom_call" | custom-call | flops 402653184 | bytes 3145728 | tf_op jit(solution)/shard_map/step_3/pallas_call | solution.py:279
  33.6 0.0 collective-permute-done.11.refs_12_
  33.6 0.0 collective-permute-done.10.refs_11_
  33.7 10.2 %close.1 = (f32[4,768,128]{2,1,0:T(8,128)S(1)}, bf16[4,768,256]{2,1,0:T(8,128)(2,1)S(1)}, f32[24,128]{1,0:T(8,128)}) custom-call(bf16[4,768,256]{2,1,0:T(8,128)(2,1)S(1)} %get-tuple-element.29.refs_0_, bf16[4,128,128]{2,1,0:T(8,128)(2,1)S(1)} %get-tuple-element.30.refs_1_, f32[1,3072]{1,0:T(1,128)S(1)} %get-tuple-element.28.refs_2_.gate_row, ...), custom_call_target="tpu_custom_call" | custom-call | flops 402653184 | bytes 3145728 | tf_op jit(solution)/shard_map/close/pallas_call | solution.py:323
  43.8 0.0 collective-permute-done.12.refs_0_
  43.8 0.0 collective-permute-done.13.refs_1_
  43.8 1.4 %mix.1 = bf16[128,3072]{1,0:T(8,128)(2,1)} custom-call(f32[1,3072]{1,0:T(1,128)S(1)} %get-tuple-element.28.refs_2_.gate_row, f32[4,768,128]{2,1,0:T(8,128)S(1)} %get-tuple-element.49.part, bf16[4,768,256]{2,1,0:T(8,128)(2,1)S(1)} %get-tuple-element.50.last_weight, bf16[128,512]{1,0:T(8,128)(2,1)S(1)} %collective-permute-done.12.refs_0_, ...), custom_call_target="tpu_custom_call" | custom-call | flops 402653184 | bytes 3145728 | tf_op jit(solution)/shard_map/mix/pallas_call | solution.py:336
  (1 shorter events, 0.0 us)
Async XLA Ops:
  0.6 4.7 %copy-start = (bf16[128,512]{1,0:T(8,128)(2,1)S(1)}, bf16[128,512]{1,0:T(8,128)(2,1)}, u32[]{:S(2)}) copy-start(bf16[128,512]{1,0:T(8,128)(2,1)} %refs_5_.3) | copy-start | bytes 393220
  0.6 6.2 %copy-start.1 = (bf16[128,512]{1,0:T(8,128)(2,1)S(1)}, bf16[128,512]{1,0:T(8,128)(2,1)}, u32[]{:S(2)}) copy-start(bf16[128,512]{1,0:T(8,128)(2,1)} %refs_13_.1) | copy-start | bytes 393220
  0.7 6.7 %copy-start.5 = (s32[4]{0:T(128)S(1)}, s32[4]{0:T(128)}, u32[]{:S(2)}) copy-start(s32[4]{0:T(128)} %refs_1_.1) | copy-start | bytes 52
  0.7 6.7 %copy-start.3 = (f32[4,3072]{1,0:T(4,128)S(1)}, f32[4,3072]{1,0:T(4,128)}, u32[]{:S(2)}) copy-start(f32[4,3072]{1,0:T(4,128)} %refs_2_.1) | copy-start | bytes 147460
  0.7 6.7 %copy-start.2 = (bf16[128,3072]{1,0:T(8,128)(2,1)S(1)}, bf16[128,3072]{1,0:T(8,128)(2,1)}, u32[]{:S(2)}) copy-start(bf16[128,3072]{1,0:T(8,128)(2,1)} %refs_4_.1) | copy-start | bytes 2359300
  0.7 6.7 %copy-start.4 = (s32[4,4]{1,0:T(4,128)S(1)}, s32[4,4]{1,0:T(4,128)}, u32[]{:S(2)}) copy-start(s32[4,4]{1,0:T(4,128)} %refs_0_.1) | copy-start | bytes 196
  0.7 9.6 %collective-permute-start.1 = (bf16[128,512]{1,0:T(8,128)(2,1)}, bf16[128,512]{1,0:T(8,128)(2,1)S(1)}, u32[]{:S(2)}, u32[]{:S(2)}) collective-permute-start(bf16[128,512]{1,0:T(8,128)(2,1)} %refs_5_.3), channel_id=1, source_target_pairs={{0,4},{1,5},{2,6},{3,7},{4,8},{5,9},{6,10},{7,11},{8,12},{9,13},{1... | collective-permute-start | bytes 393224 | tf_op jit(solution)/shard_map/ppermute | solution.py:205
  3.8 8.5 %collective-permute-start = (bf16[128,512]{1,0:T(8,128)(2,1)}, bf16[128,512]{1,0:T(8,128)(2,1)S(1)}, u32[]{:S(2)}, u32[]{:S(2)}) collective-permute-start(bf16[128,512]{1,0:T(8,128)(2,1)} %refs_13_.1), channel_id=1, source_target_pairs={{0,4},{1,5},{2,6},{3,7},{4,8},{5,9},{6,10},{7,11},{8,12},{9,13},{1... | collective-permute-start | bytes 393224 | tf_op jit(solution)/shard_map/ppermute | solution.py:205
  5.4 10.5 %collective-permute-start.4 = (bf16[128,512]{1,0:T(8,128)(2,1)S(1)}, bf16[128,512]{1,0:T(8,128)(2,1)S(1)}, u32[]{:S(2)}, u32[]{:S(2)}) collective-permute-start(bf16[128,512]{1,0:T(8,128)(2,1)S(1)} %copy-done), channel_id=1, source_target_pairs={{0,2},{1,3},{2,0},{3,1},{4,6},{5,7},{6,4},{7,5},{8,10},{9,11},{10,... | collective-permute-start | bytes 393224 | tf_op jit(solution)/shard_map/ppermute | solution.py:205
  6.9 9.5 %collective-permute-start.5 = (bf16[128,512]{1,0:T(8,128)(2,1)S(1)}, bf16[128,512]{1,0:T(8,128)(2,1)S(1)}, u32[]{:S(2)}, u32[]{:S(2)}) collective-permute-start(bf16[128,512]{1,0:T(8,128)(2,1)S(1)} %copy-done.1), channel_id=1, source_target_pairs={{0,2},{1,3},{2,0},{3,1},{4,6},{5,7},{6,4},{7,5},{8,10},{9,11},{10,... | collective-permute-start | bytes 393224 | tf_op jit(solution)/shard_map/ppermute | solution.py:205
  12.3 11.7 %collective-permute-start.2 = (bf16[128,512]{1,0:T(8,128)(2,1)S(1)}, bf16[128,512]{1,0:T(8,128)(2,1)S(1)}, u32[]{:S(2)}, u32[]{:S(2)}) collective-permute-start(bf16[128,512]{1,0:T(8,128)(2,1)S(1)} %collective-permute-done.refs_6_.refs_15_), channel_id=1, source_target_pairs={{0,16},{1,17},{2,18},{3,19},{4,8},{5,9},{6,10},{7,11},{8,12},{9,13... | collective-permute-start | bytes 393224 | tf_op jit(solution)/shard_map/ppermute | solution.py:205
  13.8 14.0 %collective-permute-start.7 = (bf16[128,512]{1,0:T(8,128)(2,1)S(1)}, bf16[128,512]{1,0:T(8,128)(2,1)S(1)}, u32[]{:S(2)}, u32[]{:S(2)}) collective-permute-start(bf16[128,512]{1,0:T(8,128)(2,1)S(1)} %collective-permute-done.refs_6_.refs_15_), channel_id=1, source_target_pairs={{0,16},{1,17},{2,18},{3,19},{4,6},{5,7},{6,4},{7,5},{8,10},{9,11},... | collective-permute-start | bytes 393224 | tf_op jit(solution)/shard_map/ppermute | solution.py:205
  14.3 9.7 %collective-permute-start.3 = (bf16[128,512]{1,0:T(8,128)(2,1)S(1)}, bf16[128,512]{1,0:T(8,128)(2,1)S(1)}, u32[]{:S(2)}, u32[]{:S(2)}) collective-permute-start(bf16[128,512]{1,0:T(8,128)(2,1)S(1)} %collective-permute-done.1.refs_4_.refs_7_), channel_id=1, source_target_pairs={{0,16},{1,17},{2,18},{3,19},{4,8},{5,9},{6,10},{7,11},{8,12},{9,13... | collective-permute-start | bytes 393224 | tf_op jit(solution)/shard_map/ppermute | solution.py:205
  15.8 13.3 %collective-permute-start.6 = (bf16[128,512]{1,0:T(8,128)(2,1)S(1)}, bf16[128,512]{1,0:T(8,128)(2,1)S(1)}, u32[]{:S(2)}, u32[]{:S(2)}) collective-permute-start(bf16[128,512]{1,0:T(8,128)(2,1)S(1)} %collective-permute-done.1.refs_4_.refs_7_), channel_id=1, source_target_pairs={{0,16},{1,17},{2,18},{3,19},{4,6},{5,7},{6,4},{7,5},{8,10},{9,11},... | collective-permute-start | bytes 393224 | tf_op jit(solution)/shard_map/ppermute | solution.py:205
  17.7 12.2 %collective-permute-start.9 = (bf16[128,512]{1,0:T(8,128)(2,1)S(1)}, bf16[128,512]{1,0:T(8,128)(2,1)S(1)}, u32[]{:S(2)}, u32[]{:S(2)}) collective-permute-start(bf16[128,512]{1,0:T(8,128)(2,1)S(1)} %copy-done.1), channel_id=1, source_target_pairs={{0,12},{1,13},{2,14},{3,15},{4,20},{5,21},{6,22},{7,23},{8,24},{9,... | collective-permute-start | bytes 393224 | tf_op jit(solution)/shard_map/ppermute | solution.py:205
  24.0 8.4 %collective-permute-start.8 = (bf16[128,512]{1,0:T(8,128)(2,1)S(1)}, bf16[128,512]{1,0:T(8,128)(2,1)S(1)}, u32[]{:S(2)}, u32[]{:S(2)}) collective-permute-start(bf16[128,512]{1,0:T(8,128)(2,1)S(1)} %copy-done), channel_id=1, source_target_pairs={{0,12},{1,13},{2,14},{3,15},{4,20},{5,21},{6,22},{7,23},{8,24},{9,... | collective-permute-start | bytes 393224 | tf_op jit(solution)/shard_map/ppermute | solution.py:205
  24.0 9.6 %collective-permute-start.11 = (bf16[128,512]{1,0:T(8,128)(2,1)S(1)}, bf16[128,512]{1,0:T(8,128)(2,1)S(1)}, u32[]{:S(2)}, u32[]{:S(2)}) collective-permute-start(bf16[128,512]{1,0:T(8,128)(2,1)S(1)} %collective-permute-done.4.refs_3_.refs_6_), channel_id=1, source_target_pairs={{0,12},{1,13},{2,14},{3,15},{4,20},{5,21},{6,22},{7,23},{8,24},{9,... | collective-permute-start | bytes 393224 | tf_op jit(solution)/shard_map/ppermute | solution.py:205
  27.8 5.8 %collective-permute-start.10 = (bf16[128,512]{1,0:T(8,128)(2,1)S(1)}, bf16[128,512]{1,0:T(8,128)(2,1)S(1)}, u32[]{:S(2)}, u32[]{:S(2)}) collective-permute-start(bf16[128,512]{1,0:T(8,128)(2,1)S(1)} %collective-permute-done.3.refs_4_.refs_9_), channel_id=1, source_target_pairs={{0,16},{1,17},{2,18},{3,19},{4,20},{5,21},{6,22},{7,23},{8,10},{9,... | collective-permute-start | bytes 393224 | tf_op jit(solution)/shard_map/ppermute | solution.py:205
  29.1 14.7 %collective-permute-start.12 = (bf16[128,512]{1,0:T(8,128)(2,1)S(1)}, bf16[128,512]{1,0:T(8,128)(2,1)S(1)}, u32[]{:S(2)}, u32[]{:S(2)}) collective-permute-start(bf16[128,512]{1,0:T(8,128)(2,1)S(1)} %collective-permute-done.2.refs_6_.refs_17_), channel_id=1, source_target_pairs={{0,16},{1,17},{2,18},{3,19},{4,20},{5,21},{6,22},{7,23},{8,10},{9,... | collective-permute-start | bytes 393224 | tf_op jit(solution)/shard_map/ppermute | solution.py:205
  29.9 13.9 %collective-permute-start.13 = (bf16[128,512]{1,0:T(8,128)(2,1)S(1)}, bf16[128,512]{1,0:T(8,128)(2,1)S(1)}, u32[]{:S(2)}, u32[]{:S(2)}) collective-permute-start(bf16[128,512]{1,0:T(8,128)(2,1)S(1)} %collective-permute-done.9.refs_4_.refs_18_), channel_id=1, source_target_pairs={{0,16},{1,17},{2,18},{3,19},{4,20},{5,21},{6,22},{7,23},{8,24},{9,... | collective-permute-start | bytes 393224 | tf_op jit(solution)/shard_map/ppermute | solution.py:205

commit v4 on v2

--- a/solution.py
+++ b/solution.py
@@ -37,11 +37,10 @@
     floor[...] = jnp.full(floor.shape, -FAR, jnp.float32)
 
 
-def own_kernel(per_span, mask, section, gate, floor, q_hbm, k_hbm, v_hbm,
-               stacked, tails, gate_row, tops, acc, q, k, v, sems):
+def prepare_kernel(per_span, mask, section, gate, floor, q_hbm, k_hbm, stacked, tails, gate_row, tops, q, k, sems):
     copies = [
         pltpu.make_async_copy(src, dst, sems.at[i])
-        for i, (src, dst) in enumerate([(q_hbm, q), (k_hbm, k), (v_hbm, v)])
+        for i, (src, dst) in enumerate([(q_hbm, q), (k_hbm, k)])
     ]
     for copy in copies:
         copy.start()
@@ -56,24 +55,18 @@
         copy.wait()
     rows, width = q.shape[0], stacked.shape[1]
     group = width // rows
-    every_top = jnp.zeros((rows, HEAD_SIZE), jnp.float32)
-    at, beside = lanes(rows), lanes(width)
+    at = lanes(1)
     for h in range(stacked.shape[0]):
         queries = jnp.concatenate([q[:, head_columns(h * group + g)] for g in range(group)], axis=0)
         score = against(queries, k[:, head_columns(h)])
-        top = jnp.maximum(floor[0:1, 0:1], jnp.max(score, axis=1, keepdims=True))
-        weight = jnp.exp2(SCALE * (score - top)).astype(jnp.bfloat16)
-        acc[h] = jnp.dot(weight, with_ones(v[:, head_columns(h)]), preferred_element_type=jnp.float32)
+        top = jnp.maximum(floor[0:1, 0:1], jnp.max(jnp.max(score, axis=0, keepdims=True), axis=1, keepdims=True))
         high = top.astype(jnp.bfloat16).astype(jnp.float32)
         middle = (top - high).astype(jnp.bfloat16).astype(jnp.float32)
         low = top - high - middle
-        extra = jnp.where(
-            beside == 0, -high, jnp.where(beside == 1, -middle, jnp.where(beside == 2, -low, jnp.where(beside == 3, 1.0, 0.0)))
-        )
-        stacked[h] = jnp.concatenate([queries, extra.astype(jnp.bfloat16)], axis=1)
-        for g in range(group):
-            every_top = jnp.where(at == h * group + g, top[g * rows : (g + 1) * rows, :], every_top)
-    tops[...] = every_top.T[: tops.shape[0], :] * (1.0 / math.sqrt(HEAD_SIZE))
+        extra = jnp.where(at == 0, -high, jnp.where(at == 1, -middle, jnp.where(at == 2, -low, jnp.where(at == 3, 1.0, 0.0))))
+        extra = jnp.broadcast_to(extra, (width, HEAD_SIZE)).astype(jnp.bfloat16)
+        stacked[h] = jnp.concatenate([queries, extra], axis=1)
+        tops[h * group : (h + 1) * group, :] = jnp.broadcast_to(top * (1.0 / math.sqrt(HEAD_SIZE)), (group, rows))
 
 
 def weights_of(h, distances, stacked, tails, key_refs):
@@ -83,13 +76,16 @@
     return jnp.exp2(SCALE * against(stacked[h], keys))
 
 
-def step_kernel(distances, stacked, tails, acc_in, *refs):
+def step_kernel(distances, first, stacked, tails, *refs):
     count = len(distances)
+    acc_in = None if first else refs[0]
+    refs = refs[0 if first else 1 :]
     key_refs, value_refs, (acc,) = refs[:count], refs[count : 2 * count], refs[2 * count :]
     for h in range(stacked.shape[0]):
         weight = weights_of(h, distances, stacked, tails, key_refs).astype(jnp.bfloat16)
         values = with_ones(jnp.concatenate([v[:, head_columns(h)] for v in value_refs], axis=0))
-        acc[h] = acc_in[h] + jnp.dot(weight, values, preferred_element_type=jnp.float32)
+        attended = jnp.dot(weight, values, preferred_element_type=jnp.float32)
+        acc[h] = attended if first else acc_in[h] + attended
 
 
 def close_kernel(distances, last, stacked, tails, gate_row, tops, acc, *refs):
@@ -109,7 +105,8 @@
         weight = weights_of(h, distances[-last:], stacked, tails, key_refs[-last:])
         ones = jnp.ones((weight.shape[1], HEAD_SIZE), jnp.bfloat16)
         total = acc[h, :, HEAD_SIZE:] + jnp.dot(weight.astype(jnp.bfloat16), ones, preferred_element_type=jnp.float32)
-        inverse = 1.0 / total
+        inverse = pl.reciprocal(total, approx=True)
+        inverse = inverse * (2.0 - total * inverse)
         for i in range(last):
             last_weight[h, :, head_columns(i)] = (weight[:, head_columns(i)] * inverse).astype(jnp.bfloat16)
         attended = acc[h, :, :HEAD_SIZE] * inverse
@@ -117,7 +114,8 @@
             gated(h, g, attended)
             every_total = jnp.where(at == h * group + g, total[g * rows : (g + 1) * rows, :], every_total)
     log_ref[...] = tops[...] + jnp.log(every_total.T[:heads, :])
-    outside = jnp.max(jnp.where(every_total <= LIMIT, 0.0, 1.0))
+    fits = jnp.logical_and(every_total <= LIMIT, every_total >= 1.0 / LIMIT)
+    outside = jnp.max(jnp.where(fits, 0.0, 1.0))
 
     @pl.when(outside > 0.0)
     def _():
@@ -218,7 +216,7 @@
 
     def around(value, distance, turn):
         return send(
-            value, lambda i: i - i % per_span + (i + turn) % per_span if i >= distance * per_span else None
+            value, lambda i: i - i % per_span + (i + turn) % per_span if i >= (distance - 1) * per_span else None
         )
 
     def travel(held, distance, turned_before):
@@ -239,37 +237,36 @@
     held = [onward(x, 1) for x in (keys, values)] if spans > 1 else []
     near_keys, near_values, floor = lax.optimization_barrier((keys, values, floor))
     turned = list(zip(*[[around(x, 0, turn) for turn in range(1, per_span)] for x in (near_keys, near_values)]))
-    def own(*refs):
-        own_kernel(per_span, *refs)
-
-    stacked, tails, gate_row, tops, acc = pl.pallas_call(
-        own,
+    def prepare(*refs):
+        prepare_kernel(per_span, *refs)
+
+    stacked, tails, gate_row, tops = pl.pallas_call(
+        prepare,
         out_shape=(
             jax.ShapeDtypeStruct((kv_heads, width, 2 * HEAD_SIZE), jnp.bfloat16),
             jax.ShapeDtypeStruct((spans, rows, HEAD_SIZE), jnp.bfloat16),
             jax.ShapeDtypeStruct((1, wide), jnp.float32),
             jax.ShapeDtypeStruct((heads, rows), jnp.float32),
-            acc_shape,
         ),
-        in_specs=[pl.BlockSpec(memory_space=pltpu.SMEM)] * 2 + [VMEM] * 2 + [HBM] * 3,
-        out_specs=(VMEM,) * 5,
+        in_specs=[pl.BlockSpec(memory_space=pltpu.SMEM)] * 2 + [VMEM] * 2 + [HBM] * 2,
+        out_specs=(VMEM,) * 4,
         scratch_shapes=[
             pltpu.VMEM(queries.shape, queries.dtype),
             pltpu.VMEM(keys.shape, keys.dtype),
-            pltpu.VMEM(values.shape, values.dtype),
-            pltpu.SemaphoreType.DMA((3,)),
+            pltpu.SemaphoreType.DMA((2,)),
         ],
         compiler_params=params,
         cost_estimate=cost(1, 10),
-        name="own",
-    )(span_mask, section, section_gate, floor, queries, keys, values)
-
-    seen_blocks = [(0, (keys, values))]
+        name="prepare",
+    )(span_mask, section, section_gate, floor, queries, keys)
+
+    token = tops
+    seen_blocks = []
     for distance in range(1, spans):
-        waiting = [(distance - 1, t) for t in turned]
+        waiting = ([(0, (keys, values))] if distance == 1 else []) + [(distance - 1, t) for t in turned]
         forward = []
         for x in held:
-            x, acc = lax.optimization_barrier((x, acc))
+            x, token = lax.optimization_barrier((x, token))
             forward.append(x)
         held = forward
         waiting.append((distance, tuple(held)))
@@ -277,19 +274,24 @@
         distances = [d for d, _ in waiting]
         blocks = [k for _, (k, _) in waiting] + [v for _, (_, v) in waiting]
         seen_blocks += waiting
+        if distance == 1:
+            tops, state = token, []
+        else:
+            state = [token]
 
         def step(*refs, distances=distances):
-            step_kernel(distances, *refs)
+            step_kernel(distances, distances[0] == 0, *refs)
 
         acc = pl.pallas_call(
             step,
             out_shape=acc_shape,
-            in_specs=[VMEM] * (3 + len(blocks)),
+            in_specs=[VMEM] * (2 + len(state) + len(blocks)),
             out_specs=VMEM,
             compiler_params=params,
             cost_estimate=cost(len(waiting)),
             name="step_%d" % distance,
-        )(stacked, tails, acc, *blocks)
+        )(stacked, tails, *state, *blocks)
+        token = acc
 
     distances = [d for d, _ in seen_blocks] + [spans - 1] * len(turned)
 

time: 30.3 us -> 38.8 us (1.28)
  the two profiles are of different devices: /device:TPU:18 before, /device:TPU:12 now
where the time goes in v4:
time: 38.8 us; the launch traced here: 38.1 us
  Pallas kernels  17.1 us (44%)
  starting transfers between devices  13 us (34%)
  waiting for transfers between devices  7.26 us (19%)
  between operations  0.75 us (2%)
    ppermute x14, starting transfers between devices, send(): return lax.ppermute(value, ('tm', 'head'), pairs)  13 us
    pallas_call x1, Pallas kernels, on_device(): pl.pallas_call(close, out_shape=(jax.ShapeDtypeStruct((kv_heads, width, H...  9.95 us
    ppermute x14, waiting for transfers between devices, send(): return lax.ppermute(value, ('tm', 'head'), pairs)  7.26 us
    pallas_call x3, Pallas kernels, on_device(): pl.pallas_call(step, out_shape=acc_shape, in_specs=[VMEM] * (2 + len(stat...  4.5 us
    pallas_call x1, Pallas kernels, on_device(): pl.pallas_call(prepare, out_shape=(jax.ShapeDtypeStruct((kv_heads, width,...  1.45 us
    pallas_call x1, Pallas kernels, on_device(): pl.pallas_call(mix_kernel, out_shape=jax.ShapeDtypeStruct((rows, wide), j...  1.15 us
  transfers between devices with their start and end apart: 14, of which 4 were waited for; matrix products, arithmetic and copies ran while one was open for 0% of the time, Pallas kernels for 42%

profile of v4, /device:TPU:12, one launch (start us, length us, event | category | flops | bytes accessed | tf_op | source)
XLA Modules:
  0.0 38.1 jit_solution(13871214471952821374)
XLA Ops:
  0.6 0.0 copy-start.1
  0.6 0.0 copy-start
  0.7 0.0 copy-start.4
  0.7 0.0 copy-start.5
  0.7 0.0 copy-start.3
  0.7 0.0 copy-start.2
  0.7 1.6 %collective-permute-start = (bf16[128,512]{1,0:T(8,128)(2,1)}, bf16[128,512]{1,0:T(8,128)(2,1)S(1)}, u32[]{:S(2)}, u32[]{:S(2)}) collective-permute-start(bf16[128,512]{1,0:T(8,128)(2,1)} %refs_13_.1), channel_id=1, source_target_pairs={{0,4},{1,5},{2,6},{3,7},{4,8},{5,9},{6,10},{7,11},{8,12},{9,13},{1... | collective-permute-start | bytes 393224 | tf_op jit(solution)/shard_map/ppermute | solution.py:205
  2.3 1.6 %collective-permute-start.1 = (bf16[128,512]{1,0:T(8,128)(2,1)}, bf16[128,512]{1,0:T(8,128)(2,1)S(1)}, u32[]{:S(2)}, u32[]{:S(2)}) collective-permute-start(bf16[128,512]{1,0:T(8,128)(2,1)} %refs_5_.5), channel_id=1, source_target_pairs={{0,4},{1,5},{2,6},{3,7},{4,8},{5,9},{6,10},{7,11},{8,12},{9,13},{1... | collective-permute-start | bytes 393224 | tf_op jit(solution)/shard_map/ppermute | solution.py:205
  3.9 0.0 copy-done
  3.9 0.5 %collective-permute-start.4 = (bf16[128,512]{1,0:T(8,128)(2,1)S(1)}, bf16[128,512]{1,0:T(8,128)(2,1)S(1)}, u32[]{:S(2)}, u32[]{:S(2)}) collective-permute-start(bf16[128,512]{1,0:T(8,128)(2,1)S(1)} %copy-done), channel_id=1, source_target_pairs={{0,2},{1,3},{2,0},{3,1},{4,6},{5,7},{6,4},{7,5},{8,10},{9,11},{10,... | collective-permute-start | bytes 393224 | tf_op jit(solution)/shard_map/ppermute | solution.py:205
  4.4 0.0 copy-done.1
  4.4 1.5 %collective-permute-start.5 = (bf16[128,512]{1,0:T(8,128)(2,1)S(1)}, bf16[128,512]{1,0:T(8,128)(2,1)S(1)}, u32[]{:S(2)}, u32[]{:S(2)}) collective-permute-start(bf16[128,512]{1,0:T(8,128)(2,1)S(1)} %copy-done.1), channel_id=1, source_target_pairs={{0,2},{1,3},{2,0},{3,1},{4,6},{5,7},{6,4},{7,5},{8,10},{9,11},{10,... | collective-permute-start | bytes 393224 | tf_op jit(solution)/shard_map/ppermute | solution.py:205
  5.9 0.0 copy-done.4
  5.9 0.0 copy-done.5
  5.9 0.0 copy-done.3
  5.9 0.0 copy-done.2
  5.9 1.5 %prepare.1 = (bf16[4,768,256]{2,1,0:T(8,128)(2,1)S(1)}, bf16[4,128,128]{2,1,0:T(8,128)(2,1)S(1)}, f32[1,3072]{1,0:T(1,128)S(1)}, f32[24,128]{1,0:T(8,128)S(1)}) custom-call(s32[4,4]{1,0:T(4,128)S(1)} %copy-done.4, s32[4]{0:T(128)S(1)} %copy-done.5, f32[4,3072]{1,0:T(4,128)S(1)} %copy-done.3, f32[8,768]{1,0:T(8,128)S(1)} %floor.1.refs_3_, ...), custom_call_target="tpu_custom_call" | custom-call | flops 2013265920 | bytes 3145728 | tf_op jit(solution)/shard_map/prepare/pallas_call | solution.py:243
  7.4 1.6 %collective-permute-done.1.refs_4_.refs_7_ = bf16[128,512]{1,0:T(8,128)(2,1)S(1)} collective-permute-done((bf16[128,512]{1,0:T(8,128)(2,1)}, bf16[128,512]{1,0:T(8,128)(2,1)S(1)}, u32[]{:S(2)}, u32[]{:S(2)}) %collective-permute-start.1) | collective-permute-done | bytes 131104 | tf_op jit(solution)/shard_map/ppermute | solution.py:205
  9.0 1.6 %collective-permute-start.3 = (bf16[128,512]{1,0:T(8,128)(2,1)S(1)}, bf16[128,512]{1,0:T(8,128)(2,1)S(1)}, u32[]{:S(2)}, u32[]{:S(2)}) collective-permute-start(bf16[128,512]{1,0:T(8,128)(2,1)S(1)} %collective-permute-done.1.refs_4_.refs_7_), channel_id=1, source_target_pairs={{0,1},{1,0},{2,3},{3,2},{4,8},{5,9},{6,10},{7,11},{8,12},{9,13},{1... | collective-permute-start | bytes 393224 | tf_op jit(solution)/shard_map/ppermute | solution.py:205
  10.6 0.5 %collective-permute-start.8 = (bf16[128,512]{1,0:T(8,128)(2,1)S(1)}, bf16[128,512]{1,0:T(8,128)(2,1)S(1)}, u32[]{:S(2)}, u32[]{:S(2)}) collective-permute-start(bf16[128,512]{1,0:T(8,128)(2,1)S(1)} %collective-permute-done.1.refs_4_.refs_7_), channel_id=1, source_target_pairs={{0,2},{1,3},{2,0},{3,1},{4,6},{5,7},{6,4},{7,5},{8,10},{9,11},{10,... | collective-permute-start | bytes 393224 | tf_op jit(solution)/shard_map/ppermute | solution.py:205
  11.1 0.0 collective-permute-done.refs_7_.refs_15_
  11.1 1.6 %collective-permute-start.2 = (bf16[128,512]{1,0:T(8,128)(2,1)S(1)}, bf16[128,512]{1,0:T(8,128)(2,1)S(1)}, u32[]{:S(2)}, u32[]{:S(2)}) collective-permute-start(bf16[128,512]{1,0:T(8,128)(2,1)S(1)} %collective-permute-done.refs_7_.refs_15_), channel_id=1, source_target_pairs={{0,1},{1,0},{2,3},{3,2},{4,8},{5,9},{6,10},{7,11},{8,12},{9,13},{1... | collective-permute-start | bytes 393224 | tf_op jit(solution)/shard_map/ppermute | solution.py:205
  12.7 0.0 collective-permute-done.4.refs_3_.refs_6_
  12.7 1.5 %collective-permute-start.9 = (bf16[128,512]{1,0:T(8,128)(2,1)S(1)}, bf16[128,512]{1,0:T(8,128)(2,1)S(1)}, u32[]{:S(2)}, u32[]{:S(2)}) collective-permute-start(bf16[128,512]{1,0:T(8,128)(2,1)S(1)} %collective-permute-done.refs_7_.refs_15_), channel_id=1, source_target_pairs={{0,2},{1,3},{2,0},{3,1},{4,6},{5,7},{6,4},{7,5},{8,10},{9,11},{10,... | collective-permute-start | bytes 393224 | tf_op jit(solution)/shard_map/ppermute | solution.py:205
  14.2 0.0 collective-permute-done.5.refs_6_.refs_14_
  14.2 2.0 %step_1.1.refs_2_ = f32[4,768,256]{2,1,0:T(8,128)S(1)} custom-call(bf16[4,768,256]{2,1,0:T(8,128)(2,1)S(1)} %get-tuple-element.26.refs_0_, bf16[4,128,128]{2,1,0:T(8,128)(2,1)S(1)} %get-tuple-element.27.refs_1_, bf16[128,512]{1,0:T(8,128)(2,1)S(1)} %copy-done, bf16[128,512]{1,0:T(8,128)(2,1)S(1)} %collective-permute-done.4.refs_3_.refs_6_, ...), custom_call_target="tpu_custom_call" | custom-call | flops 1207959552 | bytes 3145728 | tf_op jit(solution)/shard_map/step_1/pallas_call | solution.py:285
  16.2 0.0 collective-permute-done.3.refs_4_.refs_9_
  16.2 0.1 collective-permute-start.7
  16.2 1.6 %collective-permute-done.2.refs_6_.refs_17_ = bf16[128,512]{1,0:T(8,128)(2,1)S(1)} collective-permute-done((bf16[128,512]{1,0:T(8,128)(2,1)S(1)}, bf16[128,512]{1,0:T(8,128)(2,1)S(1)}, u32[]{:S(2)}, u32[]{:S(2)}) %collective-permute-start.2) | collective-permute-done | bytes 131104 | tf_op jit(solution)/shard_map/ppermute | solution.py:205
  17.9 1.9 %collective-permute-start.11 = (bf16[128,512]{1,0:T(8,128)(2,1)S(1)}, bf16[128,512]{1,0:T(8,128)(2,1)S(1)}, u32[]{:S(2)}, u32[]{:S(2)}) collective-permute-start(bf16[128,512]{1,0:T(8,128)(2,1)S(1)} %collective-permute-done.2.refs_6_.refs_17_), channel_id=1, source_target_pairs={{0,1},{1,0},{2,3},{3,2},{4,6},{5,7},{6,4},{7,5},{8,10},{9,11},{10,... | collective-permute-start | bytes 393224 | tf_op jit(solution)/shard_map/ppermute | solution.py:205
  19.8 0.0 collective-permute-start.6
  19.8 0.0 collective-permute-done.8.refs_3_.refs_8_
  19.8 0.1 collective-permute-start.10
  19.9 0.0 collective-permute-done.9.refs_5_.refs_16_
  19.9 1.3 %step_2.1.refs_2_ = f32[4,768,256]{2,1,0:T(8,128)S(1)} custom-call(bf16[4,768,256]{2,1,0:T(8,128)(2,1)S(1)} %get-tuple-element.26.refs_0_, bf16[4,128,128]{2,1,0:T(8,128)(2,1)S(1)} %get-tuple-element.27.refs_1_, f32[4,768,256]{2,1,0:T(8,128)S(1)} %step_1.1.refs_2_, bf16[128,512]{1,0:T(8,128)(2,1)S(1)} %collective-permute-done.8.refs_3_.refs_8_, ...), custom_call_target="tpu_custom_call" | custom-call | flops 805306368 | bytes 3145728 | tf_op jit(solution)/shard_map/step_2/pallas_call | solution.py:285
  21.2 0.0 collective-permute-done.7.refs_4_.refs_11_
  21.2 0.4 %collective-permute-start.12 = (bf16[128,512]{1,0:T(8,128)(2,1)S(1)}, bf16[128,512]{1,0:T(8,128)(2,1)S(1)}, u32[]{:S(2)}, u32[]{:S(2)}) collective-permute-start(bf16[128,512]{1,0:T(8,128)(2,1)S(1)} %collective-permute-done.7.refs_4_.refs_11_), channel_id=1, source_target_pairs={{0,1},{1,0},{2,3},{3,2},{4,5},{5,4},{6,7},{7,6},{8,10},{9,11},{10,... | collective-permute-start | bytes 393224 | tf_op jit(solution)/shard_map/ppermute | solution.py:205
  21.7 1.8 %collective-permute-done.11.refs_5_.refs_18_ = bf16[128,512]{1,0:T(8,128)(2,1)S(1)} collective-permute-done((bf16[128,512]{1,0:T(8,128)(2,1)S(1)}, bf16[128,512]{1,0:T(8,128)(2,1)S(1)}, u32[]{:S(2)}, u32[]{:S(2)}) %collective-permute-start.11) | collective-permute-done | bytes 131104 | tf_op jit(solution)/shard_map/ppermute | solution.py:205
  23.5 0.0 collective-permute-start.13
  23.5 0.0 collective-permute-done.6.refs_6_.refs_19_
  23.5 2.2 %collective-permute-done.10.refs_3_.refs_10_ = bf16[128,512]{1,0:T(8,128)(2,1)S(1)} collective-permute-done((bf16[128,512]{1,0:T(8,128)(2,1)S(1)}, bf16[128,512]{1,0:T(8,128)(2,1)S(1)}, u32[]{:S(2)}, u32[]{:S(2)}) %collective-permute-start.10) | collective-permute-done | bytes 131104 | tf_op jit(solution)/shard_map/ppermute | solution.py:205
  25.7 1.3 %step_3.1.refs_4_ = f32[4,768,256]{2,1,0:T(8,128)S(1)} custom-call(bf16[4,768,256]{2,1,0:T(8,128)(2,1)S(1)} %get-tuple-element.26.refs_0_, bf16[4,128,128]{2,1,0:T(8,128)(2,1)S(1)} %get-tuple-element.27.refs_1_, f32[4,768,256]{2,1,0:T(8,128)S(1)} %step_2.1.refs_2_, bf16[128,512]{1,0:T(8,128)(2,1)S(1)} %collective-permute-done.10.refs_3_.refs_10_, ...), custom_call_target="tpu_custom_call" | custom-call | flops 805306368 | bytes 3145728 | tf_op jit(solution)/shard_map/step_3/pallas_call | solution.py:285
  26.9 0.0 collective-permute-done.12.refs_12_
  27.0 10.0 %close.1 = (f32[4,768,128]{2,1,0:T(8,128)S(1)}, bf16[4,768,128]{2,1,0:T(8,128)(2,1)S(1)}, f32[24,128]{1,0:T(8,128)}) custom-call(bf16[4,768,256]{2,1,0:T(8,128)(2,1)S(1)} %get-tuple-element.26.refs_0_, bf16[4,128,128]{2,1,0:T(8,128)(2,1)S(1)} %get-tuple-element.27.refs_1_, f32[1,3072]{1,0:T(1,128)S(1)} %get-tuple-element.25.refs_2_.gate_row, ...), custom_call_target="tpu_custom_call" | custom-call | flops 402653184 | bytes 3145728 | tf_op jit(solution)/shard_map/close/pallas_call | solution.py:302
  36.9 0.0 collective-permute-done.13.refs_0_
  36.9 1.2 %mix.1 = bf16[128,3072]{1,0:T(8,128)(2,1)} custom-call(f32[1,3072]{1,0:T(1,128)S(1)} %get-tuple-element.25.refs_2_.gate_row, f32[4,768,128]{2,1,0:T(8,128)S(1)} %get-tuple-element.43.part, bf16[4,768,128]{2,1,0:T(8,128)(2,1)S(1)} %get-tuple-element.44.last_weight, bf16[128,512]{1,0:T(8,128)(2,1)S(1)} %collective-permute-done.13.refs_0_), custom_call_target="tpu_custom_call" | custom-call | flops 402653184 | bytes 3145728 | tf_op jit(solution)/shard_map/mix/pallas_call | solution.py:315
  (1 shorter events, 0.0 us)
Async XLA Ops:
  0.6 3.8 %copy-start.1 = (bf16[128,512]{1,0:T(8,128)(2,1)S(1)}, bf16[128,512]{1,0:T(8,128)(2,1)}, u32[]{:S(2)}) copy-start(bf16[128,512]{1,0:T(8,128)(2,1)} %refs_13_.1) | copy-start | bytes 393220
  0.6 3.3 %copy-start = (bf16[128,512]{1,0:T(8,128)(2,1)S(1)}, bf16[128,512]{1,0:T(8,128)(2,1)}, u32[]{:S(2)}) copy-start(bf16[128,512]{1,0:T(8,128)(2,1)} %refs_5_.5) | copy-start | bytes 393220
  0.7 5.3 %copy-start.4 = (s32[4,4]{1,0:T(4,128)S(1)}, s32[4,4]{1,0:T(4,128)}, u32[]{:S(2)}) copy-start(s32[4,4]{1,0:T(4,128)} %refs_0_.1) | copy-start | bytes 196
  0.7 5.3 %copy-start.5 = (s32[4]{0:T(128)S(1)}, s32[4]{0:T(128)}, u32[]{:S(2)}) copy-start(s32[4]{0:T(128)} %refs_1_.1) | copy-start | bytes 52
  0.7 5.3 %copy-start.3 = (f32[4,3072]{1,0:T(4,128)S(1)}, f32[4,3072]{1,0:T(4,128)}, u32[]{:S(2)}) copy-start(f32[4,3072]{1,0:T(4,128)} %refs_2_.2) | copy-start | bytes 147460
  0.7 5.3 %copy-start.2 = (bf16[128,3072]{1,0:T(8,128)(2,1)S(1)}, bf16[128,3072]{1,0:T(8,128)(2,1)}, u32[]{:S(2)}) copy-start(bf16[128,3072]{1,0:T(8,128)(2,1)} %refs_4_.1) | copy-start | bytes 2359300
  0.7 10.4 %collective-permute-start = (bf16[128,512]{1,0:T(8,128)(2,1)}, bf16[128,512]{1,0:T(8,128)(2,1)S(1)}, u32[]{:S(2)}, u32[]{:S(2)}) collective-permute-start(bf16[128,512]{1,0:T(8,128)(2,1)} %refs_13_.1), channel_id=1, source_target_pairs={{0,4},{1,5},{2,6},{3,7},{4,8},{5,9},{6,10},{7,11},{8,12},{9,13},{1... | collective-permute-start | bytes 393224 | tf_op jit(solution)/shard_map/ppermute | solution.py:205
  2.3 6.7 %collective-permute-start.1 = (bf16[128,512]{1,0:T(8,128)(2,1)}, bf16[128,512]{1,0:T(8,128)(2,1)S(1)}, u32[]{:S(2)}, u32[]{:S(2)}) collective-permute-start(bf16[128,512]{1,0:T(8,128)(2,1)} %refs_5_.5), channel_id=1, source_target_pairs={{0,4},{1,5},{2,6},{3,7},{4,8},{5,9},{6,10},{7,11},{8,12},{9,13},{1... | collective-permute-start | bytes 393224 | tf_op jit(solution)/shard_map/ppermute | solution.py:205
  3.9 8.8 %collective-permute-start.4 = (bf16[128,512]{1,0:T(8,128)(2,1)S(1)}, bf16[128,512]{1,0:T(8,128)(2,1)S(1)}, u32[]{:S(2)}, u32[]{:S(2)}) collective-permute-start(bf16[128,512]{1,0:T(8,128)(2,1)S(1)} %copy-done), channel_id=1, source_target_pairs={{0,2},{1,3},{2,0},{3,1},{4,6},{5,7},{6,4},{7,5},{8,10},{9,11},{10,... | collective-permute-start | bytes 393224 | tf_op jit(solution)/shard_map/ppermute | solution.py:205
  4.4 9.8 %collective-permute-start.5 = (bf16[128,512]{1,0:T(8,128)(2,1)S(1)}, bf16[128,512]{1,0:T(8,128)(2,1)S(1)}, u32[]{:S(2)}, u32[]{:S(2)}) collective-permute-start(bf16[128,512]{1,0:T(8,128)(2,1)S(1)} %copy-done.1), channel_id=1, source_target_pairs={{0,2},{1,3},{2,0},{3,1},{4,6},{5,7},{6,4},{7,5},{8,10},{9,11},{10,... | collective-permute-start | bytes 393224 | tf_op jit(solution)/shard_map/ppermute | solution.py:205
  9.0 7.2 %collective-permute-start.3 = (bf16[128,512]{1,0:T(8,128)(2,1)S(1)}, bf16[128,512]{1,0:T(8,128)(2,1)S(1)}, u32[]{:S(2)}, u32[]{:S(2)}) collective-permute-start(bf16[128,512]{1,0:T(8,128)(2,1)S(1)} %collective-permute-done.1.refs_4_.refs_7_), channel_id=1, source_target_pairs={{0,1},{1,0},{2,3},{3,2},{4,8},{5,9},{6,10},{7,11},{8,12},{9,13},{1... | collective-permute-start | bytes 393224 | tf_op jit(solution)/shard_map/ppermute | solution.py:205
  10.6 9.2 %collective-permute-start.8 = (bf16[128,512]{1,0:T(8,128)(2,1)S(1)}, bf16[128,512]{1,0:T(8,128)(2,1)S(1)}, u32[]{:S(2)}, u32[]{:S(2)}) collective-permute-start(bf16[128,512]{1,0:T(8,128)(2,1)S(1)} %collective-permute-done.1.refs_4_.refs_7_), channel_id=1, source_target_pairs={{0,2},{1,3},{2,0},{3,1},{4,6},{5,7},{6,4},{7,5},{8,10},{9,11},{10,... | collective-permute-start | bytes 393224 | tf_op jit(solution)/shard_map/ppermute | solution.py:205
  11.1 6.8 %collective-permute-start.2 = (bf16[128,512]{1,0:T(8,128)(2,1)S(1)}, bf16[128,512]{1,0:T(8,128)(2,1)S(1)}, u32[]{:S(2)}, u32[]{:S(2)}) collective-permute-start(bf16[128,512]{1,0:T(8,128)(2,1)S(1)} %collective-permute-done.refs_7_.refs_15_), channel_id=1, source_target_pairs={{0,1},{1,0},{2,3},{3,2},{4,8},{5,9},{6,10},{7,11},{8,12},{9,13},{1... | collective-permute-start | bytes 393224 | tf_op jit(solution)/shard_map/ppermute | solution.py:205
  12.7 7.2 %collective-permute-start.9 = (bf16[128,512]{1,0:T(8,128)(2,1)S(1)}, bf16[128,512]{1,0:T(8,128)(2,1)S(1)}, u32[]{:S(2)}, u32[]{:S(2)}) collective-permute-start(bf16[128,512]{1,0:T(8,128)(2,1)S(1)} %collective-permute-done.refs_7_.refs_15_), channel_id=1, source_target_pairs={{0,2},{1,3},{2,0},{3,1},{4,6},{5,7},{6,4},{7,5},{8,10},{9,11},{10,... | collective-permute-start | bytes 393224 | tf_op jit(solution)/shard_map/ppermute | solution.py:205
  16.2 5.0 %collective-permute-start.7 = (bf16[128,512]{1,0:T(8,128)(2,1)S(1)}, bf16[128,512]{1,0:T(8,128)(2,1)S(1)}, u32[]{:S(2)}, u32[]{:S(2)}) collective-permute-start(bf16[128,512]{1,0:T(8,128)(2,1)S(1)} %collective-permute-done.3.refs_4_.refs_9_), channel_id=1, source_target_pairs={{0,1},{1,0},{2,3},{3,2},{4,5},{5,4},{6,7},{7,6},{8,12},{9,13},{10,... | collective-permute-start | bytes 393224 | tf_op jit(solution)/shard_map/ppermute | solution.py:205
  17.9 5.6 %collective-permute-start.11 = (bf16[128,512]{1,0:T(8,128)(2,1)S(1)}, bf16[128,512]{1,0:T(8,128)(2,1)S(1)}, u32[]{:S(2)}, u32[]{:S(2)}) collective-permute-start(bf16[128,512]{1,0:T(8,128)(2,1)S(1)} %collective-permute-done.2.refs_6_.refs_17_), channel_id=1, source_target_pairs={{0,1},{1,0},{2,3},{3,2},{4,6},{5,7},{6,4},{7,5},{8,10},{9,11},{10,... | collective-permute-start | bytes 393224 | tf_op jit(solution)/shard_map/ppermute | solution.py:205
  19.8 3.7 %collective-permute-start.6 = (bf16[128,512]{1,0:T(8,128)(2,1)S(1)}, bf16[128,512]{1,0:T(8,128)(2,1)S(1)}, u32[]{:S(2)}, u32[]{:S(2)}) collective-permute-start(bf16[128,512]{1,0:T(8,128)(2,1)S(1)} %collective-permute-done.2.refs_6_.refs_17_), channel_id=1, source_target_pairs={{0,1},{1,0},{2,3},{3,2},{4,5},{5,4},{6,7},{7,6},{8,12},{9,13},{10,... | collective-permute-start | bytes 393224 | tf_op jit(solution)/shard_map/ppermute | solution.py:205
  19.8 5.9 %collective-permute-start.10 = (bf16[128,512]{1,0:T(8,128)(2,1)S(1)}, bf16[128,512]{1,0:T(8,128)(2,1)S(1)}, u32[]{:S(2)}, u32[]{:S(2)}) collective-permute-start(bf16[128,512]{1,0:T(8,128)(2,1)S(1)} %collective-permute-done.3.refs_4_.refs_9_), channel_id=1, source_target_pairs={{0,1},{1,0},{2,3},{3,2},{4,6},{5,7},{6,4},{7,5},{8,10},{9,11},{10,... | collective-permute-start | bytes 393224 | tf_op jit(solution)/shard_map/ppermute | solution.py:205
  21.2 5.7 %collective-permute-start.12 = (bf16[128,512]{1,0:T(8,128)(2,1)S(1)}, bf16[128,512]{1,0:T(8,128)(2,1)S(1)}, u32[]{:S(2)}, u32[]{:S(2)}) collective-permute-start(bf16[128,512]{1,0:T(8,128)(2,1)S(1)} %collective-permute-done.7.refs_4_.refs_11_), channel_id=1, source_target_pairs={{0,1},{1,0},{2,3},{3,2},{4,5},{5,4},{6,7},{7,6},{8,10},{9,11},{10,... | collective-permute-start | bytes 393224 | tf_op jit(solution)/shard_map/ppermute | solution.py:205
  23.5 13.4 %collective-permute-start.13 = (bf16[128,512]{1,0:T(8,128)(2,1)S(1)}, bf16[128,512]{1,0:T(8,128)(2,1)S(1)}, u32[]{:S(2)}, u32[]{:S(2)}) collective-permute-start(bf16[128,512]{1,0:T(8,128)(2,1)S(1)} %collective-permute-done.11.refs_5_.refs_18_), channel_id=1, source_target_pairs={{0,1},{1,0},{2,3},{3,2},{4,5},{5,4},{6,7},{7,6},{8,12},{9,13},{10,... | collective-permute-start | bytes 393224 | tf_op jit(solution)/shard_map/ppermute | solution.py:205

commit v5 on v2

--- a/solution.py
+++ b/solution.py
@@ -56,24 +56,20 @@
         copy.wait()
     rows, width = q.shape[0], stacked.shape[1]
     group = width // rows
-    every_top = jnp.zeros((rows, HEAD_SIZE), jnp.float32)
-    at, beside = lanes(rows), lanes(width)
+    at = lanes(1)
     for h in range(stacked.shape[0]):
         queries = jnp.concatenate([q[:, head_columns(h * group + g)] for g in range(group)], axis=0)
         score = against(queries, k[:, head_columns(h)])
-        top = jnp.maximum(floor[0:1, 0:1], jnp.max(score, axis=1, keepdims=True))
+        top = jnp.maximum(floor[0:1, 0:1], jnp.max(jnp.max(score, axis=0, keepdims=True), axis=1, keepdims=True))
         weight = jnp.exp2(SCALE * (score - top)).astype(jnp.bfloat16)
         acc[h] = jnp.dot(weight, with_ones(v[:, head_columns(h)]), preferred_element_type=jnp.float32)
         high = top.astype(jnp.bfloat16).astype(jnp.float32)
         middle = (top - high).astype(jnp.bfloat16).astype(jnp.float32)
         low = top - high - middle
-        extra = jnp.where(
-            beside == 0, -high, jnp.where(beside == 1, -middle, jnp.where(beside == 2, -low, jnp.where(beside == 3, 1.0, 0.0)))
-        )
-        stacked[h] = jnp.concatenate([queries, extra.astype(jnp.bfloat16)], axis=1)
-        for g in range(group):
-            every_top = jnp.where(at == h * group + g, top[g * rows : (g + 1) * rows, :], every_top)
-    tops[...] = every_top.T[: tops.shape[0], :] * (1.0 / math.sqrt(HEAD_SIZE))
+        extra = jnp.where(at == 0, -high, jnp.where(at == 1, -middle, jnp.where(at == 2, -low, jnp.where(at == 3, 1.0, 0.0))))
+        extra = jnp.broadcast_to(extra, (width, HEAD_SIZE)).astype(jnp.bfloat16)
+        stacked[h] = jnp.concatenate([queries, extra], axis=1)
+        tops[h * group : (h + 1) * group, :] = jnp.broadcast_to(top * (1.0 / math.sqrt(HEAD_SIZE)), (group, rows))
 
 
 def weights_of(h, distances, stacked, tails, key_refs):
@@ -109,7 +105,8 @@
         weight = weights_of(h, distances[-last:], stacked, tails, key_refs[-last:])
         ones = jnp.ones((weight.shape[1], HEAD_SIZE), jnp.bfloat16)
         total = acc[h, :, HEAD_SIZE:] + jnp.dot(weight.astype(jnp.bfloat16), ones, preferred_element_type=jnp.float32)
-        inverse = 1.0 / total
+        inverse = pl.reciprocal(total, approx=True)
+        inverse = inverse * (2.0 - total * inverse)
         for i in range(last):
             last_weight[h, :, head_columns(i)] = (weight[:, head_columns(i)] * inverse).astype(jnp.bfloat16)
         attended = acc[h, :, :HEAD_SIZE] * inverse
@@ -117,7 +114,8 @@
             gated(h, g, attended)
             every_total = jnp.where(at == h * group + g, total[g * rows : (g + 1) * rows, :], every_total)
     log_ref[...] = tops[...] + jnp.log(every_total.T[:heads, :])
-    outside = jnp.max(jnp.where(every_total <= LIMIT, 0.0, 1.0))
+    fits = jnp.logical_and(every_total <= LIMIT, every_total >= 1.0 / LIMIT)
+    outside = jnp.max(jnp.where(fits, 0.0, 1.0))
 
     @pl.when(outside > 0.0)
     def _():
@@ -188,7 +186,7 @@
     params = pltpu.CompilerParams(vmem_limit_bytes=24 * 1024 * 1024)
     acc_shape = jax.ShapeDtypeStruct((kv_heads, width, 2 * HEAD_SIZE), jnp.float32)
 
-    def cost(blocks, times=2):
+    def cost(blocks, times=3):
         return pl.CostEstimate(
             flops=4 * times * blocks * rows * rows * wide, bytes_accessed=rows * wide * 8, transcendentals=blocks * rows * rows * heads
         )
@@ -260,7 +258,7 @@
             pltpu.SemaphoreType.DMA((3,)),
         ],
         compiler_params=params,
-        cost_estimate=cost(1, 10),
+        cost_estimate=cost(1, 5),
         name="own",
     )(span_mask, section, section_gate, floor, queries, keys, values)
 
@@ -307,7 +305,7 @@
         in_specs=[VMEM] * (5 + len(blocks)),
         out_specs=(VMEM,) * 3,
         compiler_params=params,
-        cost_estimate=cost(1),
+        cost_estimate=cost(2),
         name="close",
     )(stacked, tails, gate_row, tops, acc, *blocks)
     mixed = pl.pallas_call(
@@ -317,7 +315,7 @@
         out_specs=HBM,
         scratch_shapes=[pltpu.VMEM((rows, wide), jnp.bfloat16), pltpu.SemaphoreType.DMA((kv_heads,))],
         compiler_params=params,
-        cost_estimate=cost(1),
+        cost_estimate=cost(2),
         name="mix",
     )(gate_row, part, last_weight, *[v for _, v in turned])
     return mixed, log_total

time: 30.3 us -> 38.3 us (1.26)
  the two profiles are of different devices: /device:TPU:18 before, /device:TPU:16 now
where the time goes in v5:
time: 38.3 us; the launch traced here: 38.1 us
  Pallas kernels  17.9 us (47%)
  starting transfers between devices  15.1 us (39%)
  waiting for transfers between devices  4.41 us (12%)
  between operations  0.75 us (2%)
    ppermute x14, starting transfers between devices, send(): return lax.ppermute(value, ('tm', 'head'), pairs)  15.1 us
    pallas_call x1, Pallas kernels, on_device(): pl.pallas_call(close, out_shape=(jax.ShapeDtypeStruct((kv_heads, width, H...  9.95 us
    ppermute x14, waiting for transfers between devices, send(): return lax.ppermute(value, ('tm', 'head'), pairs)  4.41 us
    pallas_call x3, Pallas kernels, on_device(): pl.pallas_call(step, out_shape=acc_shape, in_specs=[VMEM] * (3 + len(bloc...  3.83 us
    pallas_call x1, Pallas kernels, on_device(): pl.pallas_call(own, out_shape=(jax.ShapeDtypeStruct((kv_heads, width, 2 *...  2.92 us
    pallas_call x1, Pallas kernels, on_device(): pl.pallas_call(mix_kernel, out_shape=jax.ShapeDtypeStruct((rows, wide), j...  1.17 us
  transfers between devices with their start and end apart: 14, of which 4 were waited for; matrix products, arithmetic and copies ran while one was open for 0% of the time, Pallas kernels for 44%

profile of v5, /device:TPU:16, one launch (start us, length us, event | category | flops | bytes accessed | tf_op | source)
XLA Modules:
  0.0 38.1 jit_solution(13063345140664376847)
XLA Ops:
  0.6 0.0 copy-start.1
  0.6 0.0 copy-start
  0.7 0.0 copy-start.4
  0.7 0.0 copy-start.5
  0.7 0.0 copy-start.3
  0.7 0.0 copy-start.2
  0.7 1.6 %collective-permute-start = (bf16[128,512]{1,0:T(8,128)(2,1)}, bf16[128,512]{1,0:T(8,128)(2,1)S(1)}, u32[]{:S(2)}, u32[]{:S(2)}) collective-permute-start(bf16[128,512]{1,0:T(8,128)(2,1)} %refs_13_.1), channel_id=1, source_target_pairs={{0,4},{1,5},{2,6},{3,7},{4,8},{5,9},{6,10},{7,11},{8,12},{9,13},{1... | collective-permute-start | bytes 393224 | tf_op jit(solution)/shard_map/ppermute | solution.py:205
  2.3 0.1 collective-permute-start.1
  2.4 0.0 copy-done
  2.4 1.7 %collective-permute-start.4 = (bf16[128,512]{1,0:T(8,128)(2,1)S(1)}, bf16[128,512]{1,0:T(8,128)(2,1)S(1)}, u32[]{:S(2)}, u32[]{:S(2)}) collective-permute-start(bf16[128,512]{1,0:T(8,128)(2,1)S(1)} %copy-done), channel_id=1, source_target_pairs={{0,2},{1,3},{2,0},{3,1},{4,6},{5,7},{6,4},{7,5},{8,10},{9,11},{10,... | collective-permute-start | bytes 393224 | tf_op jit(solution)/shard_map/ppermute | solution.py:205
  4.1 0.0 copy-done.1
  4.1 0.4 collective-permute-start.5
  4.4 0.0 copy-done.4
  4.4 0.0 copy-done.5
  4.4 0.0 copy-done.3
  4.4 0.0 copy-done.2
  4.4 2.9 %own.1 = (bf16[4,768,256]{2,1,0:T(8,128)(2,1)S(1)}, bf16[4,128,128]{2,1,0:T(8,128)(2,1)S(1)}, f32[1,3072]{1,0:T(1,128)S(1)}, f32[24,128]{1,0:T(8,128)S(1)}, f32[4,768,256]{2,1,0:T(8,128)S(1)}) custom-call(s32[4,4]{1,0:T(4,128)S(1)} %copy-done.4, s32[4]{0:T(128)S(1)} %copy-done.5, f32[4,3072]{1,0:T(4,128)S(1)} %copy-done.3, f32[8,768]{1,0:T(8,128)S(1)} %floor.1.refs_3_, ...), custom_call_target="tpu_custom_call" | custom-call | flops 1006632960 | bytes 3145728 | tf_op jit(solution)/shard_map/own/pallas_call | solution.py:243
  7.4 1.6 %collective-permute-done.1.refs_4_.refs_7_ = bf16[128,512]{1,0:T(8,128)(2,1)S(1)} collective-permute-done((bf16[128,512]{1,0:T(8,128)(2,1)}, bf16[128,512]{1,0:T(8,128)(2,1)S(1)}, u32[]{:S(2)}, u32[]{:S(2)}) %collective-permute-start.1) | collective-permute-done | bytes 131104 | tf_op jit(solution)/shard_map/ppermute | solution.py:205
  9.0 1.6 %collective-permute-start.3 = (bf16[128,512]{1,0:T(8,128)(2,1)S(1)}, bf16[128,512]{1,0:T(8,128)(2,1)S(1)}, u32[]{:S(2)}, u32[]{:S(2)}) collective-permute-start(bf16[128,512]{1,0:T(8,128)(2,1)S(1)} %collective-permute-done.1.refs_4_.refs_7_), channel_id=1, source_target_pairs={{0,1},{1,0},{2,3},{3,2},{4,8},{5,9},{6,10},{7,11},{8,12},{9,13},{1... | collective-permute-start | bytes 393224 | tf_op jit(solution)/shard_map/ppermute | solution.py:205
  10.6 1.5 %collective-permute-start.8 = (bf16[128,512]{1,0:T(8,128)(2,1)S(1)}, bf16[128,512]{1,0:T(8,128)(2,1)S(1)}, u32[]{:S(2)}, u32[]{:S(2)}) collective-permute-start(bf16[128,512]{1,0:T(8,128)(2,1)S(1)} %collective-permute-done.1.refs_4_.refs_7_), channel_id=1, source_target_pairs={{0,1},{1,0},{2,3},{3,2},{4,6},{5,7},{6,4},{7,5},{8,10},{9,11},{10,... | collective-permute-start | bytes 393224 | tf_op jit(solution)/shard_map/ppermute | solution.py:205
  12.1 0.0 collective-permute-done.refs_6_.refs_15_
  12.1 0.3 collective-permute-start.2
  12.4 0.0 collective-permute-done.4.refs_3_.refs_6_
  12.4 0.5 %collective-permute-start.9 = (bf16[128,512]{1,0:T(8,128)(2,1)S(1)}, bf16[128,512]{1,0:T(8,128)(2,1)S(1)}, u32[]{:S(2)}, u32[]{:S(2)}) collective-permute-start(bf16[128,512]{1,0:T(8,128)(2,1)S(1)} %collective-permute-done.refs_6_.refs_15_), channel_id=1, source_target_pairs={{0,1},{1,0},{2,3},{3,2},{4,6},{5,7},{6,4},{7,5},{8,10},{9,11},{10,... | collective-permute-start | bytes 393224 | tf_op jit(solution)/shard_map/ppermute | solution.py:205
  12.9 0.0 collective-permute-done.5.refs_5_.refs_14_
  13.0 1.3 %step_1.1.refs_2_ = f32[4,768,256]{2,1,0:T(8,128)S(1)} custom-call(bf16[4,768,256]{2,1,0:T(8,128)(2,1)S(1)} %get-tuple-element.27.refs_0_, bf16[4,128,128]{2,1,0:T(8,128)(2,1)S(1)} %get-tuple-element.28.refs_1_, f32[4,768,256]{2,1,0:T(8,128)S(1)} %get-tuple-element.34.refs_2_, bf16[128,512]{1,0:T(8,128)(2,1)S(1)} %collective-permute-done.4.refs_3_.refs_6_, ...), custom_call_target="tpu_custom_call" | custom-call | flops 1207959552 | bytes 3145728 | tf_op jit(solution)/shard_map/step_1/pallas_call | solution.py:282
  14.2 0.7 %collective-permute-done.3.refs_4_.refs_9_ = bf16[128,512]{1,0:T(8,128)(2,1)S(1)} collective-permute-done((bf16[128,512]{1,0:T(8,128)(2,1)S(1)}, bf16[128,512]{1,0:T(8,128)(2,1)S(1)}, u32[]{:S(2)}, u32[]{:S(2)}) %collective-permute-start.3) | collective-permute-done | bytes 131104 | tf_op jit(solution)/shard_map/ppermute | solution.py:205
  14.9 1.4 %collective-permute-start.7 = (bf16[128,512]{1,0:T(8,128)(2,1)S(1)}, bf16[128,512]{1,0:T(8,128)(2,1)S(1)}, u32[]{:S(2)}, u32[]{:S(2)}) collective-permute-start(bf16[128,512]{1,0:T(8,128)(2,1)S(1)} %collective-permute-done.3.refs_4_.refs_9_), channel_id=1, source_target_pairs={{0,1},{1,0},{2,3},{3,2},{4,5},{5,4},{6,7},{7,6},{8,12},{9,13},{10,... | collective-permute-start | bytes 393224 | tf_op jit(solution)/shard_map/ppermute | solution.py:205
  16.3 1.5 %collective-permute-start.10 = (bf16[128,512]{1,0:T(8,128)(2,1)S(1)}, bf16[128,512]{1,0:T(8,128)(2,1)S(1)}, u32[]{:S(2)}, u32[]{:S(2)}) collective-permute-start(bf16[128,512]{1,0:T(8,128)(2,1)S(1)} %collective-permute-done.3.refs_4_.refs_9_), channel_id=1, source_target_pairs={{0,1},{1,0},{2,3},{3,2},{4,5},{5,4},{6,7},{7,6},{8,10},{9,11},{10,... | collective-permute-start | bytes 393224 | tf_op jit(solution)/shard_map/ppermute | solution.py:205
  17.9 0.0 collective-permute-done.2.refs_6_.refs_17_
  17.9 1.2 %collective-permute-start.6 = (bf16[128,512]{1,0:T(8,128)(2,1)S(1)}, bf16[128,512]{1,0:T(8,128)(2,1)S(1)}, u32[]{:S(2)}, u32[]{:S(2)}) collective-permute-start(bf16[128,512]{1,0:T(8,128)(2,1)S(1)} %collective-permute-done.2.refs_6_.refs_17_), channel_id=1, source_target_pairs={{0,1},{1,0},{2,3},{3,2},{4,5},{5,4},{6,7},{7,6},{8,12},{9,13},{10,... | collective-permute-start | bytes 393224 | tf_op jit(solution)/shard_map/ppermute | solution.py:205
  19.1 0.0 collective-permute-done.8.refs_3_.refs_8_
  19.1 1.5 %collective-permute-start.11 = (bf16[128,512]{1,0:T(8,128)(2,1)S(1)}, bf16[128,512]{1,0:T(8,128)(2,1)S(1)}, u32[]{:S(2)}, u32[]{:S(2)}) collective-permute-start(bf16[128,512]{1,0:T(8,128)(2,1)S(1)} %collective-permute-done.2.refs_6_.refs_17_), channel_id=1, source_target_pairs={{0,1},{1,0},{2,3},{3,2},{4,5},{5,4},{6,7},{7,6},{8,10},{9,11},{10,... | collective-permute-start | bytes 393224 | tf_op jit(solution)/shard_map/ppermute | solution.py:205
  20.6 0.0 collective-permute-done.9.refs_5_.refs_16_
  20.6 1.3 %step_2.1.refs_2_ = f32[4,768,256]{2,1,0:T(8,128)S(1)} custom-call(bf16[4,768,256]{2,1,0:T(8,128)(2,1)S(1)} %get-tuple-element.27.refs_0_, bf16[4,128,128]{2,1,0:T(8,128)(2,1)S(1)} %get-tuple-element.28.refs_1_, f32[4,768,256]{2,1,0:T(8,128)S(1)} %step_1.1.refs_2_, bf16[128,512]{1,0:T(8,128)(2,1)S(1)} %collective-permute-done.8.refs_3_.refs_8_, ...), custom_call_target="tpu_custom_call" | custom-call | flops 1207959552 | bytes 3145728 | tf_op jit(solution)/shard_map/step_2/pallas_call | solution.py:282
  21.9 0.0 collective-permute-done.7.refs_4_.refs_11_
  21.9 0.1 collective-permute-start.12
  22.0 0.9 %collective-permute-done.6.refs_6_.refs_19_ = bf16[128,512]{1,0:T(8,128)(2,1)S(1)} collective-permute-done((bf16[128,512]{1,0:T(8,128)(2,1)S(1)}, bf16[128,512]{1,0:T(8,128)(2,1)S(1)}, u32[]{:S(2)}, u32[]{:S(2)}) %collective-permute-start.6) | collective-permute-done | bytes 131104 | tf_op jit(solution)/shard_map/ppermute | solution.py:205
  22.8 1.2 %collective-permute-done.11.refs_5_.refs_18_ = bf16[128,512]{1,0:T(8,128)(2,1)S(1)} collective-permute-done((bf16[128,512]{1,0:T(8,128)(2,1)S(1)}, bf16[128,512]{1,0:T(8,128)(2,1)S(1)}, u32[]{:S(2)}, u32[]{:S(2)}) %collective-permute-start.11) | collective-permute-done | bytes 131104 | tf_op jit(solution)/shard_map/ppermute | solution.py:205
  24.1 1.6 %collective-permute-start.13 = (bf16[128,512]{1,0:T(8,128)(2,1)S(1)}, bf16[128,512]{1,0:T(8,128)(2,1)S(1)}, u32[]{:S(2)}, u32[]{:S(2)}) collective-permute-start(bf16[128,512]{1,0:T(8,128)(2,1)S(1)} %collective-permute-done.11.refs_5_.refs_18_), channel_id=1, source_target_pairs={{0,1},{1,0},{2,3},{3,2},{4,5},{5,4},{6,7},{7,6},{8,12},{9,13},{10,... | collective-permute-start | bytes 393224 | tf_op jit(solution)/shard_map/ppermute | solution.py:205
  25.7 0.0 collective-permute-done.10.refs_3_.refs_10_
  25.7 1.3 %step_3.1.refs_4_ = f32[4,768,256]{2,1,0:T(8,128)S(1)} custom-call(bf16[4,768,256]{2,1,0:T(8,128)(2,1)S(1)} %get-tuple-element.27.refs_0_, bf16[4,128,128]{2,1,0:T(8,128)(2,1)S(1)} %get-tuple-element.28.refs_1_, f32[4,768,256]{2,1,0:T(8,128)S(1)} %step_2.1.refs_2_, bf16[128,512]{1,0:T(8,128)(2,1)S(1)} %collective-permute-done.10.refs_3_.refs_10_, ...), custom_call_target="tpu_custom_call" | custom-call | flops 1207959552 | bytes 3145728 | tf_op jit(solution)/shard_map/step_3/pallas_call | solution.py:282
  27.0 0.0 collective-permute-done.12.refs_12_
  27.0 10.0 %close.1 = (f32[4,768,128]{2,1,0:T(8,128)S(1)}, bf16[4,768,128]{2,1,0:T(8,128)(2,1)S(1)}, f32[24,128]{1,0:T(8,128)}) custom-call(bf16[4,768,256]{2,1,0:T(8,128)(2,1)S(1)} %get-tuple-element.27.refs_0_, bf16[4,128,128]{2,1,0:T(8,128)(2,1)S(1)} %get-tuple-element.28.refs_1_, f32[1,3072]{1,0:T(1,128)S(1)} %get-tuple-element.26.refs_2_.gate_row, ...), custom_call_target="tpu_custom_call" | custom-call | flops 1207959552 | bytes 3145728 | tf_op jit(solution)/shard_map/close/pallas_call | solution.py:298
  37.0 0.0 collective-permute-done.13.refs_0_
  37.0 1.2 %mix.1 = bf16[128,3072]{1,0:T(8,128)(2,1)} custom-call(f32[1,3072]{1,0:T(1,128)S(1)} %get-tuple-element.26.refs_2_.gate_row, f32[4,768,128]{2,1,0:T(8,128)S(1)} %get-tuple-element.45.part, bf16[4,768,128]{2,1,0:T(8,128)(2,1)S(1)} %get-tuple-element.46.last_weight, bf16[128,512]{1,0:T(8,128)(2,1)S(1)} %collective-permute-done.13.refs_0_), custom_call_target="tpu_custom_call" | custom-call | flops 1207959552 | bytes 3145728 | tf_op jit(solution)/shard_map/mix/pallas_call | solution.py:311
  (1 shorter events, 0.0 us)
Async XLA Ops:
  0.6 3.4 %copy-start.1 = (bf16[128,512]{1,0:T(8,128)(2,1)S(1)}, bf16[128,512]{1,0:T(8,128)(2,1)}, u32[]{:S(2)}) copy-start(bf16[128,512]{1,0:T(8,128)(2,1)} %refs_13_.1) | copy-start | bytes 393220
  0.6 1.8 %copy-start = (bf16[128,512]{1,0:T(8,128)(2,1)S(1)}, bf16[128,512]{1,0:T(8,128)(2,1)}, u32[]{:S(2)}) copy-start(bf16[128,512]{1,0:T(8,128)(2,1)} %refs_5_.3) | copy-start | bytes 393220
  0.7 3.8 %copy-start.4 = (s32[4,4]{1,0:T(4,128)S(1)}, s32[4,4]{1,0:T(4,128)}, u32[]{:S(2)}) copy-start(s32[4,4]{1,0:T(4,128)} %refs_0_.1) | copy-start | bytes 196
  0.7 3.8 %copy-start.5 = (s32[4]{0:T(128)S(1)}, s32[4]{0:T(128)}, u32[]{:S(2)}) copy-start(s32[4]{0:T(128)} %refs_1_.1) | copy-start | bytes 52
  0.7 3.8 %copy-start.3 = (f32[4,3072]{1,0:T(4,128)S(1)}, f32[4,3072]{1,0:T(4,128)}, u32[]{:S(2)}) copy-start(f32[4,3072]{1,0:T(4,128)} %refs_2_.1) | copy-start | bytes 147460
  0.7 3.8 %copy-start.2 = (bf16[128,3072]{1,0:T(8,128)(2,1)S(1)}, bf16[128,3072]{1,0:T(8,128)(2,1)}, u32[]{:S(2)}) copy-start(bf16[128,3072]{1,0:T(8,128)(2,1)} %refs_4_.1) | copy-start | bytes 2359300
  0.7 11.4 %collective-permute-start = (bf16[128,512]{1,0:T(8,128)(2,1)}, bf16[128,512]{1,0:T(8,128)(2,1)S(1)}, u32[]{:S(2)}, u32[]{:S(2)}) collective-permute-start(bf16[128,512]{1,0:T(8,128)(2,1)} %refs_13_.1), channel_id=1, source_target_pairs={{0,4},{1,5},{2,6},{3,7},{4,8},{5,9},{6,10},{7,11},{8,12},{9,13},{1... | collective-permute-start | bytes 393224 | tf_op jit(solution)/shard_map/ppermute | solution.py:205
  2.3 6.7 %collective-permute-start.1 = (bf16[128,512]{1,0:T(8,128)(2,1)}, bf16[128,512]{1,0:T(8,128)(2,1)S(1)}, u32[]{:S(2)}, u32[]{:S(2)}) collective-permute-start(bf16[128,512]{1,0:T(8,128)(2,1)} %refs_5_.3), channel_id=1, source_target_pairs={{0,4},{1,5},{2,6},{3,7},{4,8},{5,9},{6,10},{7,11},{8,12},{9,13},{1... | collective-permute-start | bytes 393224 | tf_op jit(solution)/shard_map/ppermute | solution.py:205
  2.4 10.0 %collective-permute-start.4 = (bf16[128,512]{1,0:T(8,128)(2,1)S(1)}, bf16[128,512]{1,0:T(8,128)(2,1)S(1)}, u32[]{:S(2)}, u32[]{:S(2)}) collective-permute-start(bf16[128,512]{1,0:T(8,128)(2,1)S(1)} %copy-done), channel_id=1, source_target_pairs={{0,2},{1,3},{2,0},{3,1},{4,6},{5,7},{6,4},{7,5},{8,10},{9,11},{10,... | collective-permute-start | bytes 393224 | tf_op jit(solution)/shard_map/ppermute | solution.py:205
  4.1 8.9 %collective-permute-start.5 = (bf16[128,512]{1,0:T(8,128)(2,1)S(1)}, bf16[128,512]{1,0:T(8,128)(2,1)S(1)}, u32[]{:S(2)}, u32[]{:S(2)}) collective-permute-start(bf16[128,512]{1,0:T(8,128)(2,1)S(1)} %copy-done.1), channel_id=1, source_target_pairs={{0,2},{1,3},{2,0},{3,1},{4,6},{5,7},{6,4},{7,5},{8,10},{9,11},{10,... | collective-permute-start | bytes 393224 | tf_op jit(solution)/shard_map/ppermute | solution.py:205
  9.0 5.9 %collective-permute-start.3 = (bf16[128,512]{1,0:T(8,128)(2,1)S(1)}, bf16[128,512]{1,0:T(8,128)(2,1)S(1)}, u32[]{:S(2)}, u32[]{:S(2)}) collective-permute-start(bf16[128,512]{1,0:T(8,128)(2,1)S(1)} %collective-permute-done.1.refs_4_.refs_7_), channel_id=1, source_target_pairs={{0,1},{1,0},{2,3},{3,2},{4,8},{5,9},{6,10},{7,11},{8,12},{9,13},{1... | collective-permute-start | bytes 393224 | tf_op jit(solution)/shard_map/ppermute | solution.py:205
  10.6 8.5 %collective-permute-start.8 = (bf16[128,512]{1,0:T(8,128)(2,1)S(1)}, bf16[128,512]{1,0:T(8,128)(2,1)S(1)}, u32[]{:S(2)}, u32[]{:S(2)}) collective-permute-start(bf16[128,512]{1,0:T(8,128)(2,1)S(1)} %collective-permute-done.1.refs_4_.refs_7_), channel_id=1, source_target_pairs={{0,1},{1,0},{2,3},{3,2},{4,6},{5,7},{6,4},{7,5},{8,10},{9,11},{10,... | collective-permute-start | bytes 393224 | tf_op jit(solution)/shard_map/ppermute | solution.py:205
  12.1 5.8 %collective-permute-start.2 = (bf16[128,512]{1,0:T(8,128)(2,1)S(1)}, bf16[128,512]{1,0:T(8,128)(2,1)S(1)}, u32[]{:S(2)}, u32[]{:S(2)}) collective-permute-start(bf16[128,512]{1,0:T(8,128)(2,1)S(1)} %collective-permute-done.refs_6_.refs_15_), channel_id=1, source_target_pairs={{0,1},{1,0},{2,3},{3,2},{4,8},{5,9},{6,10},{7,11},{8,12},{9,13},{1... | collective-permute-start | bytes 393224 | tf_op jit(solution)/shard_map/ppermute | solution.py:205
  12.4 8.2 %collective-permute-start.9 = (bf16[128,512]{1,0:T(8,128)(2,1)S(1)}, bf16[128,512]{1,0:T(8,128)(2,1)S(1)}, u32[]{:S(2)}, u32[]{:S(2)}) collective-permute-start(bf16[128,512]{1,0:T(8,128)(2,1)S(1)} %collective-permute-done.refs_6_.refs_15_), channel_id=1, source_target_pairs={{0,1},{1,0},{2,3},{3,2},{4,6},{5,7},{6,4},{7,5},{8,10},{9,11},{10,... | collective-permute-start | bytes 393224 | tf_op jit(solution)/shard_map/ppermute | solution.py:205
  14.9 7.0 %collective-permute-start.7 = (bf16[128,512]{1,0:T(8,128)(2,1)S(1)}, bf16[128,512]{1,0:T(8,128)(2,1)S(1)}, u32[]{:S(2)}, u32[]{:S(2)}) collective-permute-start(bf16[128,512]{1,0:T(8,128)(2,1)S(1)} %collective-permute-done.3.refs_4_.refs_9_), channel_id=1, source_target_pairs={{0,1},{1,0},{2,3},{3,2},{4,5},{5,4},{6,7},{7,6},{8,12},{9,13},{10,... | collective-permute-start | bytes 393224 | tf_op jit(solution)/shard_map/ppermute | solution.py:205
  16.3 9.4 %collective-permute-start.10 = (bf16[128,512]{1,0:T(8,128)(2,1)S(1)}, bf16[128,512]{1,0:T(8,128)(2,1)S(1)}, u32[]{:S(2)}, u32[]{:S(2)}) collective-permute-start(bf16[128,512]{1,0:T(8,128)(2,1)S(1)} %collective-permute-done.3.refs_4_.refs_9_), channel_id=1, source_target_pairs={{0,1},{1,0},{2,3},{3,2},{4,5},{5,4},{6,7},{7,6},{8,10},{9,11},{10,... | collective-permute-start | bytes 393224 | tf_op jit(solution)/shard_map/ppermute | solution.py:205
  17.9 5.0 %collective-permute-start.6 = (bf16[128,512]{1,0:T(8,128)(2,1)S(1)}, bf16[128,512]{1,0:T(8,128)(2,1)S(1)}, u32[]{:S(2)}, u32[]{:S(2)}) collective-permute-start(bf16[128,512]{1,0:T(8,128)(2,1)S(1)} %collective-permute-done.2.refs_6_.refs_17_), channel_id=1, source_target_pairs={{0,1},{1,0},{2,3},{3,2},{4,5},{5,4},{6,7},{7,6},{8,12},{9,13},{10,... | collective-permute-start | bytes 393224 | tf_op jit(solution)/shard_map/ppermute | solution.py:205
  19.1 5.0 %collective-permute-start.11 = (bf16[128,512]{1,0:T(8,128)(2,1)S(1)}, bf16[128,512]{1,0:T(8,128)(2,1)S(1)}, u32[]{:S(2)}, u32[]{:S(2)}) collective-permute-start(bf16[128,512]{1,0:T(8,128)(2,1)S(1)} %collective-permute-done.2.refs_6_.refs_17_), channel_id=1, source_target_pairs={{0,1},{1,0},{2,3},{3,2},{4,5},{5,4},{6,7},{7,6},{8,10},{9,11},{10,... | collective-permute-start | bytes 393224 | tf_op jit(solution)/shard_map/ppermute | solution.py:205
  21.9 5.1 %collective-permute-start.12 = (bf16[128,512]{1,0:T(8,128)(2,1)S(1)}, bf16[128,512]{1,0:T(8,128)(2,1)S(1)}, u32[]{:S(2)}, u32[]{:S(2)}) collective-permute-start(bf16[128,512]{1,0:T(8,128)(2,1)S(1)} %collective-permute-done.7.refs_4_.refs_11_), channel_id=1, source_target_pairs={{0,1},{1,0},{2,3},{3,2},{4,5},{5,4},{6,7},{7,6},{8,9},{9,8},{10,11... | collective-permute-start | bytes 393224 | tf_op jit(solution)/shard_map/ppermute | solution.py:205
  24.1 12.9 %collective-permute-start.13 = (bf16[128,512]{1,0:T(8,128)(2,1)S(1)}, bf16[128,512]{1,0:T(8,128)(2,1)S(1)}, u32[]{:S(2)}, u32[]{:S(2)}) collective-permute-start(bf16[128,512]{1,0:T(8,128)(2,1)S(1)} %collective-permute-done.11.refs_5_.refs_18_), channel_id=1, source_target_pairs={{0,1},{1,0},{2,3},{3,2},{4,5},{5,4},{6,7},{7,6},{8,12},{9,13},{10,... | collective-permute-start | bytes 393224 | tf_op jit(solution)/shard_map/ppermute | solution.py:205

commit v6 on v5

--- a/solution.py
+++ b/solution.py
@@ -219,11 +219,14 @@
             value, lambda i: i - i % per_span + (i + turn) % per_span if i >= distance * per_span else None
         )
 
-    def travel(held, distance, turned_before):
+    def leap(value):
+        return send(value, lambda i: (i - per_span) % count)
+
+    def travel(held, distance, far_values):
         onwards = [onward(x, distance + 1) for x in held] if distance + 1 < spans else []
-        turned = [[around(x, distance, turn) for turn in range(1, per_span)] for x in held]
-        if not onwards and turned_before:
-            turned[1] = [onward(v, distance) for _, v in turned_before]
+        turned = [[around(x, distance, turn) for turn in range(1, per_span)] for x in (held if onwards else held[:1])]
+        if not onwards:
+            turned.append(far_values)
         return list(zip(*turned)), onwards
 
     floor = pl.pallas_call(
@@ -262,6 +265,8 @@
         name="own",
     )(span_mask, section, section_gate, floor, queries, keys, values)
 
+    beside = [v for _, v in turned]
+    far_values = [leap(v) for v in beside] if spans == 2 else None
     seen_blocks = [(0, (keys, values))]
     for distance in range(1, spans):
         waiting = [(distance - 1, t) for t in turned]
@@ -271,7 +276,7 @@
             forward.append(x)
         held = forward
         waiting.append((distance, tuple(held)))
-        turned, held = travel(held, distance, turned)
+        turned, held = travel(held, distance, far_values)
         distances = [d for d, _ in waiting]
         blocks = [k for _, (k, _) in waiting] + [v for _, (_, v) in waiting]
         seen_blocks += waiting
@@ -288,6 +293,11 @@
             cost_estimate=cost(len(waiting)),
             name="step_%d" % distance,
         )(stacked, tails, acc, *blocks)
+        if far_values is None:
+            far_values = []
+            for x in beside:
+                x, acc = lax.optimization_barrier((x, acc))
+                far_values.append(leap(x))
 
     distances = [d for d, _ in seen_blocks] + [spans - 1] * len(turned)
 

time: 38.3 us -> 39.5 us (1.031)
  the two profiles are of different devices: /device:TPU:16 before, /device:TPU:0 now
where the time goes in v6:
time: 39.5 us; the launch traced here: 39.4 us
  starting transfers between devices  18.7 us (47%)
  Pallas kernels  17.9 us (45%)
  waiting for transfers between devices  2.02 us (5%)
  between operations  0.75 us (2%)
    ppermute x14, starting transfers between devices, send(): return lax.ppermute(value, ('tm', 'head'), pairs)  18.7 us
    pallas_call x1, Pallas kernels, on_device(): pl.pallas_call(close, out_shape=(jax.ShapeDtypeStruct((kv_heads, width, H...  9.95 us
    pallas_call x3, Pallas kernels, on_device(): pl.pallas_call(step, out_shape=acc_shape, in_specs=[VMEM] * (3 + len(bloc...  3.83 us
    pallas_call x1, Pallas kernels, on_device(): pl.pallas_call(own, out_shape=(jax.ShapeDtypeStruct((kv_heads, width, 2 *...  2.92 us
    ppermute x14, waiting for transfers between devices, send(): return lax.ppermute(value, ('tm', 'head'), pairs)  2.02 us
    pallas_call x1, Pallas kernels, on_device(): pl.pallas_call(mix_kernel, out_shape=jax.ShapeDtypeStruct((rows, wide), j...  1.16 us
  transfers between devices with their start and end apart: 14, of which 1 were waited for; matrix products, arithmetic and copies ran while one was open for 0% of the time, Pallas kernels for 42%

profile of v6, /device:TPU:0, one launch (start us, length us, event | category | flops | bytes accessed | tf_op | source)
XLA Modules:
  0.0 39.4 jit_solution(15978891446550185298)
XLA Ops:
  0.6 0.0 copy-start.1
  0.6 0.0 copy-start
  0.7 0.0 copy-start.4
  0.7 0.0 copy-start.5
  0.7 0.0 copy-start.3
  0.7 0.0 copy-start.2
  0.7 3.1 %collective-permute-start = (bf16[128,512]{1,0:T(8,128)(2,1)}, bf16[128,512]{1,0:T(8,128)(2,1)S(1)}, u32[]{:S(2)}, u32[]{:S(2)}) collective-permute-start(bf16[128,512]{1,0:T(8,128)(2,1)} %refs_13_.1), channel_id=1, source_target_pairs={{0,4},{1,5},{2,6},{3,7},{4,8},{5,9},{6,10},{7,11},{8,12},{9,13},{1... | collective-permute-start | bytes 393224 | tf_op jit(solution)/shard_map/ppermute | solution.py:205
  3.8 1.6 %collective-permute-start.1 = (bf16[128,512]{1,0:T(8,128)(2,1)}, bf16[128,512]{1,0:T(8,128)(2,1)S(1)}, u32[]{:S(2)}, u32[]{:S(2)}) collective-permute-start(bf16[128,512]{1,0:T(8,128)(2,1)} %refs_5_.3), channel_id=1, source_target_pairs={{0,4},{1,5},{2,6},{3,7},{4,8},{5,9},{6,10},{7,11},{8,12},{9,13},{1... | collective-permute-start | bytes 393224 | tf_op jit(solution)/shard_map/ppermute | solution.py:205
  5.3 0.0 copy-done.1
  5.4 1.5 %collective-permute-start.4 = (bf16[128,512]{1,0:T(8,128)(2,1)S(1)}, bf16[128,512]{1,0:T(8,128)(2,1)S(1)}, u32[]{:S(2)}, u32[]{:S(2)}) collective-permute-start(bf16[128,512]{1,0:T(8,128)(2,1)S(1)} %copy-done.1), channel_id=1, source_target_pairs={{0,2},{1,3},{2,0},{3,1},{4,6},{5,7},{6,4},{7,5},{8,10},{9,11},{10,... | collective-permute-start | bytes 393224 | tf_op jit(solution)/shard_map/ppermute | solution.py:205
  6.9 0.0 copy-done
  6.9 0.5 %collective-permute-start.5 = (bf16[128,512]{1,0:T(8,128)(2,1)S(1)}, bf16[128,512]{1,0:T(8,128)(2,1)S(1)}, u32[]{:S(2)}, u32[]{:S(2)}) collective-permute-start(bf16[128,512]{1,0:T(8,128)(2,1)S(1)} %copy-done), channel_id=1, source_target_pairs={{0,2},{1,3},{2,0},{3,1},{4,6},{5,7},{6,4},{7,5},{8,10},{9,11},{10,... | collective-permute-start | bytes 393224 | tf_op jit(solution)/shard_map/ppermute | solution.py:205
  7.4 0.0 copy-done.4
  7.4 0.0 copy-done.5
  7.4 0.0 copy-done.3
  7.4 0.0 copy-done.2
  7.4 2.9 %own.1 = (bf16[4,768,256]{2,1,0:T(8,128)(2,1)S(1)}, bf16[4,128,128]{2,1,0:T(8,128)(2,1)S(1)}, f32[1,3072]{1,0:T(1,128)S(1)}, f32[24,128]{1,0:T(8,128)S(1)}, f32[4,768,256]{2,1,0:T(8,128)S(1)}) custom-call(s32[4,4]{1,0:T(4,128)S(1)} %copy-done.4, s32[4]{0:T(128)S(1)} %copy-done.5, f32[4,3072]{1,0:T(4,128)S(1)} %copy-done.3, f32[8,768]{1,0:T(8,128)S(1)} %floor.1.refs_3_, ...), custom_call_target="tpu_custom_call" | custom-call | flops 1006632960 | bytes 3145728 | tf_op jit(solution)/shard_map/own/pallas_call | solution.py:246
  10.3 2.0 %collective-permute-done.1.refs_4_.refs_7_ = bf16[128,512]{1,0:T(8,128)(2,1)S(1)} collective-permute-done((bf16[128,512]{1,0:T(8,128)(2,1)}, bf16[128,512]{1,0:T(8,128)(2,1)S(1)}, u32[]{:S(2)}, u32[]{:S(2)}) %collective-permute-start.1) | collective-permute-done | bytes 131104 | tf_op jit(solution)/shard_map/ppermute | solution.py:205
  12.3 0.0 collective-permute-start.3
  12.3 0.5 %collective-permute-start.8 = (bf16[128,512]{1,0:T(8,128)(2,1)S(1)}, bf16[128,512]{1,0:T(8,128)(2,1)S(1)}, u32[]{:S(2)}, u32[]{:S(2)}) collective-permute-start(bf16[128,512]{1,0:T(8,128)(2,1)S(1)} %collective-permute-done.1.refs_4_.refs_7_), channel_id=1, source_target_pairs={{0,1},{1,0},{2,3},{3,2},{4,6},{5,7},{6,4},{7,5},{8,10},{9,11},{10,... | collective-permute-start | bytes 393224 | tf_op jit(solution)/shard_map/ppermute | solution.py:205
  12.8 0.0 collective-permute-done.refs_6_.refs_15_
  12.8 0.0 collective-permute-start.2
  12.8 0.0 collective-permute-done.4.refs_5_.refs_14_
  12.8 0.5 %collective-permute-start.9 = (bf16[128,512]{1,0:T(8,128)(2,1)S(1)}, bf16[128,512]{1,0:T(8,128)(2,1)S(1)}, u32[]{:S(2)}, u32[]{:S(2)}) collective-permute-start(bf16[128,512]{1,0:T(8,128)(2,1)S(1)} %collective-permute-done.refs_6_.refs_15_), channel_id=1, source_target_pairs={{0,1},{1,0},{2,3},{3,2},{4,6},{5,7},{6,4},{7,5},{8,10},{9,11},{10,... | collective-permute-start | bytes 393224 | tf_op jit(solution)/shard_map/ppermute | solution.py:205
  13.3 0.0 collective-permute-done.5.refs_3_.refs_6_
  13.3 1.3 %step_1.1.refs_2_ = f32[4,768,256]{2,1,0:T(8,128)S(1)} custom-call(bf16[4,768,256]{2,1,0:T(8,128)(2,1)S(1)} %get-tuple-element.29.refs_0_, bf16[4,128,128]{2,1,0:T(8,128)(2,1)S(1)} %get-tuple-element.30.refs_1_, f32[4,768,256]{2,1,0:T(8,128)S(1)} %get-tuple-element.37.refs_2_, bf16[128,512]{1,0:T(8,128)(2,1)S(1)} %collective-permute-done.5.refs_3_.refs_6_, ...), custom_call_target="tpu_custom_call" | custom-call | flops 1207959552 | bytes 3145728 | tf_op jit(solution)/shard_map/step_1/pallas_call | solution.py:287
  14.6 0.0 collective-permute-done.3.refs_4_.refs_9_
  14.6 0.1 collective-permute-start.7
  14.8 0.4 %collective-permute-start.10 = (bf16[128,512]{1,0:T(8,128)(2,1)S(1)}, bf16[128,512]{1,0:T(8,128)(2,1)S(1)}, u32[]{:S(2)}, u32[]{:S(2)}) collective-permute-start(bf16[128,512]{1,0:T(8,128)(2,1)S(1)} %collective-permute-done.3.refs_4_.refs_9_), channel_id=1, source_target_pairs={{0,1},{1,0},{2,3},{3,2},{4,5},{5,4},{6,7},{7,6},{8,10},{9,11},{10,... | collective-permute-start | bytes 393224 | tf_op jit(solution)/shard_map/ppermute | solution.py:205
  15.2 0.0 collective-permute-done.2.refs_6_.refs_17_
  15.2 0.1 collective-permute-start.6
  15.3 0.0 collective-permute-done.8.refs_3_.refs_8_
  15.3 0.4 %collective-permute-start.11 = (bf16[128,512]{1,0:T(8,128)(2,1)S(1)}, bf16[128,512]{1,0:T(8,128)(2,1)S(1)}, u32[]{:S(2)}, u32[]{:S(2)}) collective-permute-start(bf16[128,512]{1,0:T(8,128)(2,1)S(1)} %collective-permute-done.2.refs_6_.refs_17_), channel_id=1, source_target_pairs={{0,1},{1,0},{2,3},{3,2},{4,5},{5,4},{6,7},{7,6},{8,10},{9,11},{10,... | collective-permute-start | bytes 393224 | tf_op jit(solution)/shard_map/ppermute | solution.py:205
  15.7 0.0 collective-permute-done.9.refs_5_.refs_16_
  15.7 1.3 %step_2.1.refs_2_ = f32[4,768,256]{2,1,0:T(8,128)S(1)} custom-call(bf16[4,768,256]{2,1,0:T(8,128)(2,1)S(1)} %get-tuple-element.29.refs_0_, bf16[4,128,128]{2,1,0:T(8,128)(2,1)S(1)} %get-tuple-element.30.refs_1_, f32[4,768,256]{2,1,0:T(8,128)S(1)} %step_1.1.refs_2_, bf16[128,512]{1,0:T(8,128)(2,1)S(1)} %collective-permute-done.8.refs_3_.refs_8_, ...), custom_call_target="tpu_custom_call" | custom-call | flops 1207959552 | bytes 3145728 | tf_op jit(solution)/shard_map/step_2/pallas_call | solution.py:287
  17.0 0.0 collective-permute-done.7.refs_4_.refs_11_
  17.0 0.1 collective-permute-start.12
  17.2 9.8 %collective-permute-start.13 = (bf16[128,512]{1,0:T(8,128)(2,1)S(1)}, bf16[128,512]{1,0:T(8,128)(2,1)S(1)}, u32[]{:S(2)}, u32[]{:S(2)}) collective-permute-start(bf16[128,512]{1,0:T(8,128)(2,1)S(1)} %collective-permute-done.4.refs_5_.refs_14_), channel_id=1, source_target_pairs={{0,12},{1,13},{2,14},{3,15},{4,0},{5,1},{6,2},{7,3},{8,4},{9,5},{1... | collective-permute-start | bytes 393224 | tf_op jit(solution)/shard_map/ppermute | solution.py:205
  27.0 0.0 collective-permute-done.6.refs_6_.refs_19_
  27.0 0.0 collective-permute-done.10.refs_3_.refs_10_
  27.0 0.0 collective-permute-done.11.refs_5_.refs_18_
  27.0 1.3 %step_3.1.refs_4_ = f32[4,768,256]{2,1,0:T(8,128)S(1)} custom-call(bf16[4,768,256]{2,1,0:T(8,128)(2,1)S(1)} %get-tuple-element.29.refs_0_, bf16[4,128,128]{2,1,0:T(8,128)(2,1)S(1)} %get-tuple-element.30.refs_1_, f32[4,768,256]{2,1,0:T(8,128)S(1)} %step_2.1.refs_2_, bf16[128,512]{1,0:T(8,128)(2,1)S(1)} %collective-permute-done.10.refs_3_.refs_10_, ...), custom_call_target="tpu_custom_call" | custom-call | flops 1207959552 | bytes 3145728 | tf_op jit(solution)/shard_map/step_3/pallas_call | solution.py:287
  28.3 0.0 collective-permute-done.12.refs_12_
  28.3 10.0 %close.1 = (f32[4,768,128]{2,1,0:T(8,128)S(1)}, bf16[4,768,128]{2,1,0:T(8,128)(2,1)S(1)}, f32[24,128]{1,0:T(8,128)}) custom-call(bf16[4,768,256]{2,1,0:T(8,128)(2,1)S(1)} %get-tuple-element.29.refs_0_, bf16[4,128,128]{2,1,0:T(8,128)(2,1)S(1)} %get-tuple-element.30.refs_1_, f32[1,3072]{1,0:T(1,128)S(1)} %get-tuple-element.28.refs_2_.gate_row, ...), custom_call_target="tpu_custom_call" | custom-call | flops 1207959552 | bytes 3145728 | tf_op jit(solution)/shard_map/close/pallas_call | solution.py:308
  38.2 0.0 collective-permute-done.13.refs_0_
  38.2 1.2 %mix.1 = bf16[128,3072]{1,0:T(8,128)(2,1)} custom-call(f32[1,3072]{1,0:T(1,128)S(1)} %get-tuple-element.28.refs_2_.gate_row, f32[4,768,128]{2,1,0:T(8,128)S(1)} %get-tuple-element.48.part, bf16[4,768,128]{2,1,0:T(8,128)(2,1)S(1)} %get-tuple-element.49.last_weight, bf16[128,512]{1,0:T(8,128)(2,1)S(1)} %collective-permute-done.13.refs_0_), custom_call_target="tpu_custom_call" | custom-call | flops 1207959552 | bytes 3145728 | tf_op jit(solution)/shard_map/mix/pallas_call | solution.py:321
  (1 shorter events, 0.0 us)
Async XLA Ops:
  0.6 4.7 %copy-start.1 = (bf16[128,512]{1,0:T(8,128)(2,1)S(1)}, bf16[128,512]{1,0:T(8,128)(2,1)}, u32[]{:S(2)}) copy-start(bf16[128,512]{1,0:T(8,128)(2,1)} %refs_13_.1) | copy-start | bytes 393220
  0.6 6.2 %copy-start = (bf16[128,512]{1,0:T(8,128)(2,1)S(1)}, bf16[128,512]{1,0:T(8,128)(2,1)}, u32[]{:S(2)}) copy-start(bf16[128,512]{1,0:T(8,128)(2,1)} %refs_5_.3) | copy-start | bytes 393220
  0.7 6.7 %copy-start.4 = (s32[4,4]{1,0:T(4,128)S(1)}, s32[4,4]{1,0:T(4,128)}, u32[]{:S(2)}) copy-start(s32[4,4]{1,0:T(4,128)} %refs_0_.1) | copy-start | bytes 196
  0.7 6.7 %copy-start.5 = (s32[4]{0:T(128)S(1)}, s32[4]{0:T(128)}, u32[]{:S(2)}) copy-start(s32[4]{0:T(128)} %refs_1_.1) | copy-start | bytes 52
  0.7 6.7 %copy-start.3 = (f32[4,3072]{1,0:T(4,128)S(1)}, f32[4,3072]{1,0:T(4,128)}, u32[]{:S(2)}) copy-start(f32[4,3072]{1,0:T(4,128)} %refs_2_.1) | copy-start | bytes 147460
  0.7 6.7 %copy-start.2 = (bf16[128,3072]{1,0:T(8,128)(2,1)S(1)}, bf16[128,3072]{1,0:T(8,128)(2,1)}, u32[]{:S(2)}) copy-start(bf16[128,3072]{1,0:T(8,128)(2,1)} %refs_4_.1) | copy-start | bytes 2359300
  0.7 12.1 %collective-permute-start = (bf16[128,512]{1,0:T(8,128)(2,1)}, bf16[128,512]{1,0:T(8,128)(2,1)S(1)}, u32[]{:S(2)}, u32[]{:S(2)}) collective-permute-start(bf16[128,512]{1,0:T(8,128)(2,1)} %refs_13_.1), channel_id=1, source_target_pairs={{0,4},{1,5},{2,6},{3,7},{4,8},{5,9},{6,10},{7,11},{8,12},{9,13},{1... | collective-permute-start | bytes 393224 | tf_op jit(solution)/shard_map/ppermute | solution.py:205
  3.8 8.5 %collective-permute-start.1 = (bf16[128,512]{1,0:T(8,128)(2,1)}, bf16[128,512]{1,0:T(8,128)(2,1)S(1)}, u32[]{:S(2)}, u32[]{:S(2)}) collective-permute-start(bf16[128,512]{1,0:T(8,128)(2,1)} %refs_5_.3), channel_id=1, source_target_pairs={{0,4},{1,5},{2,6},{3,7},{4,8},{5,9},{6,10},{7,11},{8,12},{9,13},{1... | collective-permute-start | bytes 393224 | tf_op jit(solution)/shard_map/ppermute | solution.py:205
  5.4 7.5 %collective-permute-start.4 = (bf16[128,512]{1,0:T(8,128)(2,1)S(1)}, bf16[128,512]{1,0:T(8,128)(2,1)S(1)}, u32[]{:S(2)}, u32[]{:S(2)}) collective-permute-start(bf16[128,512]{1,0:T(8,128)(2,1)S(1)} %copy-done.1), channel_id=1, source_target_pairs={{0,2},{1,3},{2,0},{3,1},{4,6},{5,7},{6,4},{7,5},{8,10},{9,11},{10,... | collective-permute-start | bytes 393224 | tf_op jit(solution)/shard_map/ppermute | solution.py:205
  6.9 6.5 %collective-permute-start.5 = (bf16[128,512]{1,0:T(8,128)(2,1)S(1)}, bf16[128,512]{1,0:T(8,128)(2,1)S(1)}, u32[]{:S(2)}, u32[]{:S(2)}) collective-permute-start(bf16[128,512]{1,0:T(8,128)(2,1)S(1)} %copy-done), channel_id=1, source_target_pairs={{0,2},{1,3},{2,0},{3,1},{4,6},{5,7},{6,4},{7,5},{8,10},{9,11},{10,... | collective-permute-start | bytes 393224 | tf_op jit(solution)/shard_map/ppermute | solution.py:205
  12.3 2.3 %collective-permute-start.3 = (bf16[128,512]{1,0:T(8,128)(2,1)S(1)}, bf16[128,512]{1,0:T(8,128)(2,1)S(1)}, u32[]{:S(2)}, u32[]{:S(2)}) collective-permute-start(bf16[128,512]{1,0:T(8,128)(2,1)S(1)} %collective-permute-done.1.refs_4_.refs_7_), channel_id=1, source_target_pairs={{0,1},{1,0},{2,3},{3,2},{4,8},{5,9},{6,10},{7,11},{8,12},{9,13},{1... | collective-permute-start | bytes 393224 | tf_op jit(solution)/shard_map/ppermute | solution.py:205
  12.3 3.0 %collective-permute-start.8 = (bf16[128,512]{1,0:T(8,128)(2,1)S(1)}, bf16[128,512]{1,0:T(8,128)(2,1)S(1)}, u32[]{:S(2)}, u32[]{:S(2)}) collective-permute-start(bf16[128,512]{1,0:T(8,128)(2,1)S(1)} %collective-permute-done.1.refs_4_.refs_7_), channel_id=1, source_target_pairs={{0,1},{1,0},{2,3},{3,2},{4,6},{5,7},{6,4},{7,5},{8,10},{9,11},{10,... | collective-permute-start | bytes 393224 | tf_op jit(solution)/shard_map/ppermute | solution.py:205
  12.8 2.4 %collective-permute-start.2 = (bf16[128,512]{1,0:T(8,128)(2,1)S(1)}, bf16[128,512]{1,0:T(8,128)(2,1)S(1)}, u32[]{:S(2)}, u32[]{:S(2)}) collective-permute-start(bf16[128,512]{1,0:T(8,128)(2,1)S(1)} %collective-permute-done.refs_6_.refs_15_), channel_id=1, source_target_pairs={{0,1},{1,0},{2,3},{3,2},{4,8},{5,9},{6,10},{7,11},{8,12},{9,13},{1... | collective-permute-start | bytes 393224 | tf_op jit(solution)/shard_map/ppermute | solution.py:205
  12.8 2.9 %collective-permute-start.9 = (bf16[128,512]{1,0:T(8,128)(2,1)S(1)}, bf16[128,512]{1,0:T(8,128)(2,1)S(1)}, u32[]{:S(2)}, u32[]{:S(2)}) collective-permute-start(bf16[128,512]{1,0:T(8,128)(2,1)S(1)} %collective-permute-done.refs_6_.refs_15_), channel_id=1, source_target_pairs={{0,1},{1,0},{2,3},{3,2},{4,6},{5,7},{6,4},{7,5},{8,10},{9,11},{10,... | collective-permute-start | bytes 393224 | tf_op jit(solution)/shard_map/ppermute | solution.py:205
  14.6 2.4 %collective-permute-start.7 = (bf16[128,512]{1,0:T(8,128)(2,1)S(1)}, bf16[128,512]{1,0:T(8,128)(2,1)S(1)}, u32[]{:S(2)}, u32[]{:S(2)}) collective-permute-start(bf16[128,512]{1,0:T(8,128)(2,1)S(1)} %collective-permute-done.3.refs_4_.refs_9_), channel_id=1, source_target_pairs={{0,1},{1,0},{2,3},{3,2},{4,5},{5,4},{6,7},{7,6},{8,12},{9,13},{10,... | collective-permute-start | bytes 393224 | tf_op jit(solution)/shard_map/ppermute | solution.py:205
  14.8 12.2 %collective-permute-start.10 = (bf16[128,512]{1,0:T(8,128)(2,1)S(1)}, bf16[128,512]{1,0:T(8,128)(2,1)S(1)}, u32[]{:S(2)}, u32[]{:S(2)}) collective-permute-start(bf16[128,512]{1,0:T(8,128)(2,1)S(1)} %collective-permute-done.3.refs_4_.refs_9_), channel_id=1, source_target_pairs={{0,1},{1,0},{2,3},{3,2},{4,5},{5,4},{6,7},{7,6},{8,10},{9,11},{10,... | collective-permute-start | bytes 393224 | tf_op jit(solution)/shard_map/ppermute | solution.py:205
  15.2 11.7 %collective-permute-start.6 = (bf16[128,512]{1,0:T(8,128)(2,1)S(1)}, bf16[128,512]{1,0:T(8,128)(2,1)S(1)}, u32[]{:S(2)}, u32[]{:S(2)}) collective-permute-start(bf16[128,512]{1,0:T(8,128)(2,1)S(1)} %collective-permute-done.2.refs_6_.refs_17_), channel_id=1, source_target_pairs={{0,1},{1,0},{2,3},{3,2},{4,5},{5,4},{6,7},{7,6},{8,12},{9,13},{10,... | collective-permute-start | bytes 393224 | tf_op jit(solution)/shard_map/ppermute | solution.py:205
  15.3 11.7 %collective-permute-start.11 = (bf16[128,512]{1,0:T(8,128)(2,1)S(1)}, bf16[128,512]{1,0:T(8,128)(2,1)S(1)}, u32[]{:S(2)}, u32[]{:S(2)}) collective-permute-start(bf16[128,512]{1,0:T(8,128)(2,1)S(1)} %collective-permute-done.2.refs_6_.refs_17_), channel_id=1, source_target_pairs={{0,1},{1,0},{2,3},{3,2},{4,5},{5,4},{6,7},{7,6},{8,10},{9,11},{10,... | collective-permute-start | bytes 393224 | tf_op jit(solution)/shard_map/ppermute | solution.py:205
  17.0 11.3 %collective-permute-start.12 = (bf16[128,512]{1,0:T(8,128)(2,1)S(1)}, bf16[128,512]{1,0:T(8,128)(2,1)S(1)}, u32[]{:S(2)}, u32[]{:S(2)}) collective-permute-start(bf16[128,512]{1,0:T(8,128)(2,1)S(1)} %collective-permute-done.7.refs_4_.refs_11_), channel_id=1, source_target_pairs={{0,1},{1,0},{2,3},{3,2},{4,5},{5,4},{6,7},{7,6},{8,9},{9,8},{10,11... | collective-permute-start | bytes 393224 | tf_op jit(solution)/shard_map/ppermute | solution.py:205
  17.2 21.1 %collective-permute-start.13 = (bf16[128,512]{1,0:T(8,128)(2,1)S(1)}, bf16[128,512]{1,0:T(8,128)(2,1)S(1)}, u32[]{:S(2)}, u32[]{:S(2)}) collective-permute-start(bf16[128,512]{1,0:T(8,128)(2,1)S(1)} %collective-permute-done.4.refs_5_.refs_14_), channel_id=1, source_target_pairs={{0,12},{1,13},{2,14},{3,15},{4,0},{5,1},{6,2},{7,3},{8,4},{9,5},{1... | collective-permute-start | bytes 393224 | tf_op jit(solution)/shard_map/ppermute | solution.py:205

commit v7 on v6

--- a/solution.py
+++ b/solution.py
@@ -299,6 +299,9 @@
                 x, acc = lax.optimization_barrier((x, acc))
                 far_values.append(leap(x))
 
+    for i, (k, v) in enumerate(turned):
+        v, acc = lax.optimization_barrier((v, acc))
+        turned[i] = (k, v)
     distances = [d for d, _ in seen_blocks] + [spans - 1] * len(turned)
 
     def close(*refs):

time: 39.5 us -> 39.2 us (level)
  the two profiles are of different devices: /device:TPU:0 before, /device:TPU:16 now
where the time goes in v7:
time: 39.2 us; the launch traced here: 39.1 us
  Pallas kernels  17.9 us (46%)
  starting transfers between devices  15.2 us (39%)
  waiting for transfers between devices  5.25 us (13%)
  between operations  0.77 us (2%)
    ppermute x14, starting transfers between devices, send(): return lax.ppermute(value, ('tm', 'head'), pairs)  15.2 us
    pallas_call x1, Pallas kernels, on_device(): pl.pallas_call(close, out_shape=(jax.ShapeDtypeStruct((kv_heads, width, H...  9.95 us
    ppermute x14, waiting for transfers between devices, send(): return lax.ppermute(value, ('tm', 'head'), pairs)  5.25 us
    pallas_call x3, Pallas kernels, on_device(): pl.pallas_call(step, out_shape=acc_shape, in_specs=[VMEM] * (3 + len(bloc...  3.83 us
    pallas_call x1, Pallas kernels, on_device(): pl.pallas_call(own, out_shape=(jax.ShapeDtypeStruct((kv_heads, width, 2 *...  2.92 us
    pallas_call x1, Pallas kernels, on_device(): pl.pallas_call(mix_kernel, out_shape=jax.ShapeDtypeStruct((rows, wide), j...  1.16 us
  transfers between devices with their start and end apart: 14, of which 4 were waited for; matrix products, arithmetic and copies ran while one was open for 0% of the time, Pallas kernels for 17%

profile of v7, /device:TPU:16, one launch (start us, length us, event | category | flops | bytes accessed | tf_op | source)
XLA Modules:
  0.0 39.1 jit_solution(6329969243067454241)
XLA Ops:
  0.6 0.0 copy-start
  0.6 0.0 copy-start.1
  0.7 0.0 copy-start.5
  0.7 0.0 copy-start.3
  0.7 0.0 copy-start.2
  0.7 0.0 copy-start.4
  0.7 1.6 %collective-permute-start.2 = (bf16[128,512]{1,0:T(8,128)(2,1)}, bf16[128,512]{1,0:T(8,128)(2,1)S(1)}, u32[]{:S(2)}, u32[]{:S(2)}) collective-permute-start(bf16[128,512]{1,0:T(8,128)(2,1)} %refs_5_.3), channel_id=1, source_target_pairs={{0,4},{1,5},{2,6},{3,7},{4,8},{5,9},{6,10},{7,11},{8,12},{9,13},{1... | collective-permute-start | bytes 393224 | tf_op jit(solution)/shard_map/ppermute | solution.py:205
  2.3 0.1 collective-permute-start.1
  2.4 0.0 copy-done.1
  2.4 1.7 %collective-permute-start = (bf16[128,512]{1,0:T(8,128)(2,1)S(1)}, bf16[128,512]{1,0:T(8,128)(2,1)S(1)}, u32[]{:S(2)}, u32[]{:S(2)}) collective-permute-start(bf16[128,512]{1,0:T(8,128)(2,1)S(1)} %copy-done.1), channel_id=1, source_target_pairs={{0,2},{1,3},{2,0},{3,1},{4,6},{5,7},{6,4},{7,5},{8,10},{9,11},{10,... | collective-permute-start | bytes 393224 | tf_op jit(solution)/shard_map/ppermute | solution.py:205
  4.1 0.0 copy-done
  4.1 0.4 collective-permute-start.3
  4.4 0.0 copy-done.5
  4.4 0.0 copy-done.3
  4.4 0.0 copy-done.2
  4.4 0.0 copy-done.4
  4.4 2.9 %own.1 = (bf16[4,768,256]{2,1,0:T(8,128)(2,1)S(1)}, bf16[4,128,128]{2,1,0:T(8,128)(2,1)S(1)}, f32[1,3072]{1,0:T(1,128)S(1)}, f32[24,128]{1,0:T(8,128)S(1)}, f32[4,768,256]{2,1,0:T(8,128)S(1)}) custom-call(s32[4,4]{1,0:T(4,128)S(1)} %copy-done.4, s32[4]{0:T(128)S(1)} %copy-done.5, f32[4,3072]{1,0:T(4,128)S(1)} %copy-done.3, f32[8,768]{1,0:T(8,128)S(1)} %floor.1.refs_3_, ...), custom_call_target="tpu_custom_call" | custom-call | flops 1006632960 | bytes 3145728 | tf_op jit(solution)/shard_map/own/pallas_call | solution.py:246
  7.4 0.0 collective-permute-done.2.refs_4_.refs_7_
  7.4 1.8 %collective-permute-start.6 = (bf16[128,512]{1,0:T(8,128)(2,1)S(1)}, bf16[128,512]{1,0:T(8,128)(2,1)S(1)}, u32[]{:S(2)}, u32[]{:S(2)}) collective-permute-start(bf16[128,512]{1,0:T(8,128)(2,1)S(1)} %collective-permute-done.2.refs_4_.refs_7_), channel_id=1, source_target_pairs={{0,1},{1,0},{2,3},{3,2},{4,8},{5,9},{6,10},{7,11},{8,12},{9,13},{1... | collective-permute-start | bytes 393224 | tf_op jit(solution)/shard_map/ppermute | solution.py:205
  9.2 0.0 collective-permute-done.1.refs_6_.refs_15_
  9.2 1.7 %collective-permute-start.5 = (bf16[128,512]{1,0:T(8,128)(2,1)S(1)}, bf16[128,512]{1,0:T(8,128)(2,1)S(1)}, u32[]{:S(2)}, u32[]{:S(2)}) collective-permute-start(bf16[128,512]{1,0:T(8,128)(2,1)S(1)} %collective-permute-done.1.refs_6_.refs_15_), channel_id=1, source_target_pairs={{0,1},{1,0},{2,3},{3,2},{4,8},{5,9},{6,10},{7,11},{8,12},{9,13},{1... | collective-permute-start | bytes 393224 | tf_op jit(solution)/shard_map/ppermute | solution.py:205
  10.9 1.5 %collective-permute-start.10 = (bf16[128,512]{1,0:T(8,128)(2,1)S(1)}, bf16[128,512]{1,0:T(8,128)(2,1)S(1)}, u32[]{:S(2)}, u32[]{:S(2)}) collective-permute-start(bf16[128,512]{1,0:T(8,128)(2,1)S(1)} %collective-permute-done.1.refs_6_.refs_15_), channel_id=1, source_target_pairs={{0,1},{1,0},{2,3},{3,2},{4,6},{5,7},{6,4},{7,5},{8,10},{9,11},{10,... | collective-permute-start | bytes 393224 | tf_op jit(solution)/shard_map/ppermute | solution.py:205
  12.4 0.0 collective-permute-done.refs_5_.refs_14_
  12.4 0.5 %collective-permute-start.9 = (bf16[128,512]{1,0:T(8,128)(2,1)S(1)}, bf16[128,512]{1,0:T(8,128)(2,1)S(1)}, u32[]{:S(2)}, u32[]{:S(2)}) collective-permute-start(bf16[128,512]{1,0:T(8,128)(2,1)S(1)} %collective-permute-done.2.refs_4_.refs_7_), channel_id=1, source_target_pairs={{0,1},{1,0},{2,3},{3,2},{4,6},{5,7},{6,4},{7,5},{8,10},{9,11},{10,... | collective-permute-start | bytes 393224 | tf_op jit(solution)/shard_map/ppermute | solution.py:205
  12.9 0.0 collective-permute-done.3.refs_3_.refs_6_
  12.9 1.3 %step_1.1.refs_2_ = f32[4,768,256]{2,1,0:T(8,128)S(1)} custom-call(bf16[4,768,256]{2,1,0:T(8,128)(2,1)S(1)} %get-tuple-element.31.refs_0_, bf16[4,128,128]{2,1,0:T(8,128)(2,1)S(1)} %get-tuple-element.32.refs_1_, f32[4,768,256]{2,1,0:T(8,128)S(1)} %get-tuple-element.37.refs_2_, bf16[128,512]{1,0:T(8,128)(2,1)S(1)} %collective-permute-done.3.refs_3_.refs_6_, ...), custom_call_target="tpu_custom_call" | custom-call | flops 1207959552 | bytes 3145728 | tf_op jit(solution)/shard_map/step_1/pallas_call | solution.py:287
  14.2 0.0 collective-permute-done.6.refs_4_.refs_9_
  14.2 0.7 %collective-permute-start.8 = (bf16[128,512]{1,0:T(8,128)(2,1)S(1)}, bf16[128,512]{1,0:T(8,128)(2,1)S(1)}, u32[]{:S(2)}, u32[]{:S(2)}) collective-permute-start(bf16[128,512]{1,0:T(8,128)(2,1)S(1)} %collective-permute-done.6.refs_4_.refs_9_), channel_id=1, source_target_pairs={{0,1},{1,0},{2,3},{3,2},{4,5},{5,4},{6,7},{7,6},{8,12},{9,13},{10,... | collective-permute-start | bytes 393224 | tf_op jit(solution)/shard_map/ppermute | solution.py:205
  14.9 0.2 collective-permute-done.5.refs_6_.refs_17_
  15.1 2.5 %collective-permute-start.7 = (bf16[128,512]{1,0:T(8,128)(2,1)S(1)}, bf16[128,512]{1,0:T(8,128)(2,1)S(1)}, u32[]{:S(2)}, u32[]{:S(2)}) collective-permute-start(bf16[128,512]{1,0:T(8,128)(2,1)S(1)} %collective-permute-done.5.refs_6_.refs_17_), channel_id=1, source_target_pairs={{0,1},{1,0},{2,3},{3,2},{4,5},{5,4},{6,7},{7,6},{8,12},{9,13},{10,... | collective-permute-start | bytes 393224 | tf_op jit(solution)/shard_map/ppermute | solution.py:205
  17.6 0.6 %collective-permute-start.4 = (bf16[128,512]{1,0:T(8,128)(2,1)S(1)}, bf16[128,512]{1,0:T(8,128)(2,1)S(1)}, u32[]{:S(2)}, u32[]{:S(2)}) collective-permute-start(bf16[128,512]{1,0:T(8,128)(2,1)S(1)} %collective-permute-done.refs_5_.refs_14_), channel_id=1, source_target_pairs={{0,12},{1,13},{2,14},{3,15},{4,0},{5,1},{6,2},{7,3},{8,4},{9,5},{1... | collective-permute-start | bytes 393224 | tf_op jit(solution)/shard_map/ppermute | solution.py:205
  18.2 0.0 collective-permute-done.10.refs_5_.refs_16_
  18.2 1.5 %collective-permute-start.12 = (bf16[128,512]{1,0:T(8,128)(2,1)S(1)}, bf16[128,512]{1,0:T(8,128)(2,1)S(1)}, u32[]{:S(2)}, u32[]{:S(2)}) collective-permute-start(bf16[128,512]{1,0:T(8,128)(2,1)S(1)} %collective-permute-done.5.refs_6_.refs_17_), channel_id=1, source_target_pairs={{0,1},{1,0},{2,3},{3,2},{4,5},{5,4},{6,7},{7,6},{8,10},{9,11},{10,... | collective-permute-start | bytes 393224 | tf_op jit(solution)/shard_map/ppermute | solution.py:205
  19.7 0.0 collective-permute-done.9.refs_3_.refs_8_
  19.7 0.5 %collective-permute-start.11 = (bf16[128,512]{1,0:T(8,128)(2,1)S(1)}, bf16[128,512]{1,0:T(8,128)(2,1)S(1)}, u32[]{:S(2)}, u32[]{:S(2)}) collective-permute-start(bf16[128,512]{1,0:T(8,128)(2,1)S(1)} %collective-permute-done.6.refs_4_.refs_9_), channel_id=1, source_target_pairs={{0,1},{1,0},{2,3},{3,2},{4,5},{5,4},{6,7},{7,6},{8,10},{9,11},{10,... | collective-permute-start | bytes 393224 | tf_op jit(solution)/shard_map/ppermute | solution.py:205
  20.2 1.3 %step_2.1.refs_2_ = f32[4,768,256]{2,1,0:T(8,128)S(1)} custom-call(bf16[4,768,256]{2,1,0:T(8,128)(2,1)S(1)} %get-tuple-element.31.refs_0_, bf16[4,128,128]{2,1,0:T(8,128)(2,1)S(1)} %get-tuple-element.32.refs_1_, f32[4,768,256]{2,1,0:T(8,128)S(1)} %step_1.1.refs_2_, bf16[128,512]{1,0:T(8,128)(2,1)S(1)} %collective-permute-done.9.refs_3_.refs_8_, ...), custom_call_target="tpu_custom_call" | custom-call | flops 1207959552 | bytes 3145728 | tf_op jit(solution)/shard_map/step_2/pallas_call | solution.py:287
  21.5 0.0 collective-permute-done.8.refs_4_.refs_11_
  21.5 0.1 collective-permute-start.13
  21.6 1.2 %collective-permute-done.7.refs_6_.refs_19_ = bf16[128,512]{1,0:T(8,128)(2,1)S(1)} collective-permute-done((bf16[128,512]{1,0:T(8,128)(2,1)S(1)}, bf16[128,512]{1,0:T(8,128)(2,1)S(1)}, u32[]{:S(2)}, u32[]{:S(2)}) %collective-permute-start.7) | collective-permute-done | bytes 131104 | tf_op jit(solution)/shard_map/ppermute | solution.py:205
  22.8 1.8 %collective-permute-done.12.refs_5_.refs_18_ = bf16[128,512]{1,0:T(8,128)(2,1)S(1)} collective-permute-done((bf16[128,512]{1,0:T(8,128)(2,1)S(1)}, bf16[128,512]{1,0:T(8,128)(2,1)S(1)}, u32[]{:S(2)}, u32[]{:S(2)}) %collective-permute-start.12) | collective-permute-done | bytes 131104 | tf_op jit(solution)/shard_map/ppermute | solution.py:205
  24.5 2.1 %collective-permute-done.11.refs_3_.refs_10_ = bf16[128,512]{1,0:T(8,128)(2,1)S(1)} collective-permute-done((bf16[128,512]{1,0:T(8,128)(2,1)S(1)}, bf16[128,512]{1,0:T(8,128)(2,1)S(1)}, u32[]{:S(2)}, u32[]{:S(2)}) %collective-permute-start.11) | collective-permute-done | bytes 131104 | tf_op jit(solution)/shard_map/ppermute | solution.py:205
  26.6 1.3 %step_3.1.refs_4_ = f32[4,768,256]{2,1,0:T(8,128)S(1)} custom-call(bf16[4,768,256]{2,1,0:T(8,128)(2,1)S(1)} %get-tuple-element.31.refs_0_, bf16[4,128,128]{2,1,0:T(8,128)(2,1)S(1)} %get-tuple-element.32.refs_1_, f32[4,768,256]{2,1,0:T(8,128)S(1)} %step_2.1.refs_2_, bf16[128,512]{1,0:T(8,128)(2,1)S(1)} %collective-permute-done.11.refs_3_.refs_10_, ...), custom_call_target="tpu_custom_call" | custom-call | flops 1207959552 | bytes 3145728 | tf_op jit(solution)/shard_map/step_3/pallas_call | solution.py:287
  27.9 0.0 collective-permute-done.4.refs_0_
  27.9 0.0 collective-permute-done.13.refs_12_
  28.0 10.0 %close.1 = (f32[4,768,128]{2,1,0:T(8,128)S(1)}, bf16[4,768,128]{2,1,0:T(8,128)(2,1)S(1)}, f32[24,128]{1,0:T(8,128)}) custom-call(bf16[4,768,256]{2,1,0:T(8,128)(2,1)S(1)} %get-tuple-element.31.refs_0_, bf16[4,128,128]{2,1,0:T(8,128)(2,1)S(1)} %get-tuple-element.32.refs_1_, f32[1,3072]{1,0:T(1,128)S(1)} %get-tuple-element.30.refs_2_.gate_row, ...), custom_call_target="tpu_custom_call" | custom-call | flops 1207959552 | bytes 3145728 | tf_op jit(solution)/shard_map/close/pallas_call | solution.py:311
  37.9 1.2 %mix.1 = bf16[128,3072]{1,0:T(8,128)(2,1)} custom-call(f32[1,3072]{1,0:T(1,128)S(1)} %get-tuple-element.30.refs_2_.gate_row, f32[4,768,128]{2,1,0:T(8,128)S(1)} %get-tuple-element.52.part, bf16[4,768,128]{2,1,0:T(8,128)(2,1)S(1)} %get-tuple-element.53.last_weight, bf16[128,512]{1,0:T(8,128)(2,1)S(1)} %collective-permute-done.4.refs_0_), custom_call_target="tpu_custom_call" | custom-call | flops 1207959552 | bytes 3145728 | tf_op jit(solution)/shard_map/mix/pallas_call | solution.py:324
  (1 shorter events, 0.0 us)
Async XLA Ops:
  0.6 3.4 %copy-start = (bf16[128,512]{1,0:T(8,128)(2,1)S(1)}, bf16[128,512]{1,0:T(8,128)(2,1)}, u32[]{:S(2)}) copy-start(bf16[128,512]{1,0:T(8,128)(2,1)} %refs_5_.3) | copy-start | bytes 393220
  0.6 1.8 %copy-start.1 = (bf16[128,512]{1,0:T(8,128)(2,1)S(1)}, bf16[128,512]{1,0:T(8,128)(2,1)}, u32[]{:S(2)}) copy-start(bf16[128,512]{1,0:T(8,128)(2,1)} %refs_13_.1) | copy-start | bytes 393220
  0.7 3.8 %copy-start.5 = (s32[4]{0:T(128)S(1)}, s32[4]{0:T(128)}, u32[]{:S(2)}) copy-start(s32[4]{0:T(128)} %refs_1_.1) | copy-start | bytes 52
  0.7 3.8 %copy-start.3 = (f32[4,3072]{1,0:T(4,128)S(1)}, f32[4,3072]{1,0:T(4,128)}, u32[]{:S(2)}) copy-start(f32[4,3072]{1,0:T(4,128)} %refs_2_.1) | copy-start | bytes 147460
  0.7 3.8 %copy-start.2 = (bf16[128,3072]{1,0:T(8,128)(2,1)S(1)}, bf16[128,3072]{1,0:T(8,128)(2,1)}, u32[]{:S(2)}) copy-start(bf16[128,3072]{1,0:T(8,128)(2,1)} %refs_4_.1) | copy-start | bytes 2359300
  0.7 3.8 %copy-start.4 = (s32[4,4]{1,0:T(4,128)S(1)}, s32[4,4]{1,0:T(4,128)}, u32[]{:S(2)}) copy-start(s32[4,4]{1,0:T(4,128)} %refs_0_.1) | copy-start | bytes 196
  0.7 6.7 %collective-permute-start.2 = (bf16[128,512]{1,0:T(8,128)(2,1)}, bf16[128,512]{1,0:T(8,128)(2,1)S(1)}, u32[]{:S(2)}, u32[]{:S(2)}) collective-permute-start(bf16[128,512]{1,0:T(8,128)(2,1)} %refs_5_.3), channel_id=1, source_target_pairs={{0,4},{1,5},{2,6},{3,7},{4,8},{5,9},{6,10},{7,11},{8,12},{9,13},{1... | collective-permute-start | bytes 393224 | tf_op jit(solution)/shard_map/ppermute | solution.py:205
  2.3 6.9 %collective-permute-start.1 = (bf16[128,512]{1,0:T(8,128)(2,1)}, bf16[128,512]{1,0:T(8,128)(2,1)S(1)}, u32[]{:S(2)}, u32[]{:S(2)}) collective-permute-start(bf16[128,512]{1,0:T(8,128)(2,1)} %refs_13_.1), channel_id=1, source_target_pairs={{0,4},{1,5},{2,6},{3,7},{4,8},{5,9},{6,10},{7,11},{8,12},{9,13},{1... | collective-permute-start | bytes 393224 | tf_op jit(solution)/shard_map/ppermute | solution.py:205
  2.4 10.0 %collective-permute-start = (bf16[128,512]{1,0:T(8,128)(2,1)S(1)}, bf16[128,512]{1,0:T(8,128)(2,1)S(1)}, u32[]{:S(2)}, u32[]{:S(2)}) collective-permute-start(bf16[128,512]{1,0:T(8,128)(2,1)S(1)} %copy-done.1), channel_id=1, source_target_pairs={{0,2},{1,3},{2,0},{3,1},{4,6},{5,7},{6,4},{7,5},{8,10},{9,11},{10,... | collective-permute-start | bytes 393224 | tf_op jit(solution)/shard_map/ppermute | solution.py:205
  4.1 8.8 %collective-permute-start.3 = (bf16[128,512]{1,0:T(8,128)(2,1)S(1)}, bf16[128,512]{1,0:T(8,128)(2,1)S(1)}, u32[]{:S(2)}, u32[]{:S(2)}) collective-permute-start(bf16[128,512]{1,0:T(8,128)(2,1)S(1)} %copy-done), channel_id=1, source_target_pairs={{0,2},{1,3},{2,0},{3,1},{4,6},{5,7},{6,4},{7,5},{8,10},{9,11},{10,... | collective-permute-start | bytes 393224 | tf_op jit(solution)/shard_map/ppermute | solution.py:205
  7.4 6.8 %collective-permute-start.6 = (bf16[128,512]{1,0:T(8,128)(2,1)S(1)}, bf16[128,512]{1,0:T(8,128)(2,1)S(1)}, u32[]{:S(2)}, u32[]{:S(2)}) collective-permute-start(bf16[128,512]{1,0:T(8,128)(2,1)S(1)} %collective-permute-done.2.refs_4_.refs_7_), channel_id=1, source_target_pairs={{0,1},{1,0},{2,3},{3,2},{4,8},{5,9},{6,10},{7,11},{8,12},{9,13},{1... | collective-permute-start | bytes 393224 | tf_op jit(solution)/shard_map/ppermute | solution.py:205
  9.2 5.9 %collective-permute-start.5 = (bf16[128,512]{1,0:T(8,128)(2,1)S(1)}, bf16[128,512]{1,0:T(8,128)(2,1)S(1)}, u32[]{:S(2)}, u32[]{:S(2)}) collective-permute-start(bf16[128,512]{1,0:T(8,128)(2,1)S(1)} %collective-permute-done.1.refs_6_.refs_15_), channel_id=1, source_target_pairs={{0,1},{1,0},{2,3},{3,2},{4,8},{5,9},{6,10},{7,11},{8,12},{9,13},{1... | collective-permute-start | bytes 393224 | tf_op jit(solution)/shard_map/ppermute | solution.py:205
  10.9 7.3 %collective-permute-start.10 = (bf16[128,512]{1,0:T(8,128)(2,1)S(1)}, bf16[128,512]{1,0:T(8,128)(2,1)S(1)}, u32[]{:S(2)}, u32[]{:S(2)}) collective-permute-start(bf16[128,512]{1,0:T(8,128)(2,1)S(1)} %collective-permute-done.1.refs_6_.refs_15_), channel_id=1, source_target_pairs={{0,1},{1,0},{2,3},{3,2},{4,6},{5,7},{6,4},{7,5},{8,10},{9,11},{10,... | collective-permute-start | bytes 393224 | tf_op jit(solution)/shard_map/ppermute | solution.py:205
  12.4 7.4 %collective-permute-start.9 = (bf16[128,512]{1,0:T(8,128)(2,1)S(1)}, bf16[128,512]{1,0:T(8,128)(2,1)S(1)}, u32[]{:S(2)}, u32[]{:S(2)}) collective-permute-start(bf16[128,512]{1,0:T(8,128)(2,1)S(1)} %collective-permute-done.2.refs_4_.refs_7_), channel_id=1, source_target_pairs={{0,1},{1,0},{2,3},{3,2},{4,6},{5,7},{6,4},{7,5},{8,10},{9,11},{10,... | collective-permute-start | bytes 393224 | tf_op jit(solution)/shard_map/ppermute | solution.py:205
  14.2 7.3 %collective-permute-start.8 = (bf16[128,512]{1,0:T(8,128)(2,1)S(1)}, bf16[128,512]{1,0:T(8,128)(2,1)S(1)}, u32[]{:S(2)}, u32[]{:S(2)}) collective-permute-start(bf16[128,512]{1,0:T(8,128)(2,1)S(1)} %collective-permute-done.6.refs_4_.refs_9_), channel_id=1, source_target_pairs={{0,1},{1,0},{2,3},{3,2},{4,5},{5,4},{6,7},{7,6},{8,12},{9,13},{10,... | collective-permute-start | bytes 393224 | tf_op jit(solution)/shard_map/ppermute | solution.py:205
  15.1 7.7 %collective-permute-start.7 = (bf16[128,512]{1,0:T(8,128)(2,1)S(1)}, bf16[128,512]{1,0:T(8,128)(2,1)S(1)}, u32[]{:S(2)}, u32[]{:S(2)}) collective-permute-start(bf16[128,512]{1,0:T(8,128)(2,1)S(1)} %collective-permute-done.5.refs_6_.refs_17_), channel_id=1, source_target_pairs={{0,1},{1,0},{2,3},{3,2},{4,5},{5,4},{6,7},{7,6},{8,12},{9,13},{10,... | collective-permute-start | bytes 393224 | tf_op jit(solution)/shard_map/ppermute | solution.py:205
  17.6 10.3 %collective-permute-start.4 = (bf16[128,512]{1,0:T(8,128)(2,1)S(1)}, bf16[128,512]{1,0:T(8,128)(2,1)S(1)}, u32[]{:S(2)}, u32[]{:S(2)}) collective-permute-start(bf16[128,512]{1,0:T(8,128)(2,1)S(1)} %collective-permute-done.refs_5_.refs_14_), channel_id=1, source_target_pairs={{0,12},{1,13},{2,14},{3,15},{4,0},{5,1},{6,2},{7,3},{8,4},{9,5},{1... | collective-permute-start | bytes 393224 | tf_op jit(solution)/shard_map/ppermute | solution.py:205
  18.2 6.3 %collective-permute-start.12 = (bf16[128,512]{1,0:T(8,128)(2,1)S(1)}, bf16[128,512]{1,0:T(8,128)(2,1)S(1)}, u32[]{:S(2)}, u32[]{:S(2)}) collective-permute-start(bf16[128,512]{1,0:T(8,128)(2,1)S(1)} %collective-permute-done.5.refs_6_.refs_17_), channel_id=1, source_target_pairs={{0,1},{1,0},{2,3},{3,2},{4,5},{5,4},{6,7},{7,6},{8,10},{9,11},{10,... | collective-permute-start | bytes 393224 | tf_op jit(solution)/shard_map/ppermute | solution.py:205
  19.7 6.9 %collective-permute-start.11 = (bf16[128,512]{1,0:T(8,128)(2,1)S(1)}, bf16[128,512]{1,0:T(8,128)(2,1)S(1)}, u32[]{:S(2)}, u32[]{:S(2)}) collective-permute-start(bf16[128,512]{1,0:T(8,128)(2,1)S(1)} %collective-permute-done.6.refs_4_.refs_9_), channel_id=1, source_target_pairs={{0,1},{1,0},{2,3},{3,2},{4,5},{5,4},{6,7},{7,6},{8,10},{9,11},{10,... | collective-permute-start | bytes 393224 | tf_op jit(solution)/shard_map/ppermute | solution.py:205
  21.5 6.4 %collective-permute-start.13 = (bf16[128,512]{1,0:T(8,128)(2,1)S(1)}, bf16[128,512]{1,0:T(8,128)(2,1)S(1)}, u32[]{:S(2)}, u32[]{:S(2)}) collective-permute-start(bf16[128,512]{1,0:T(8,128)(2,1)S(1)} %collective-permute-done.8.refs_4_.refs_11_), channel_id=1, source_target_pairs={{0,1},{1,0},{2,3},{3,2},{4,5},{5,4},{6,7},{7,6},{8,9},{9,8},{10,11... | collective-permute-start | bytes 393224 | tf_op jit(solution)/shard_map/ppermute | solution.py:205

commit v8 on v0

--- a/solution.py
+++ b/solution.py
@@ -192,11 +192,19 @@
     held = [onward(x, 1) for x in (keys, values)] if spans > 1 else []
     near_keys, near_values, floor = lax.optimization_barrier((keys, values, floor))
     turned = list(zip(*[[around(x, 0, turn) for turn in range(1, per_span)] for x in (near_keys, near_values)]))
-    stacked, acc, stat = pl.pallas_call(
-        own_kernel,
-        out_shape=(jax.ShapeDtypeStruct((kv_heads, width, HEAD_SIZE), jnp.bfloat16), acc_shape, stat_shape),
-        in_specs=[VMEM] + [HBM] * 3,
-        out_specs=(VMEM,) * 3,
+    def own(mask, section, gate, floor, q, k, v, seen, gate_row, *refs):
+        flag_kernel(per_span, mask, section, gate, seen, gate_row)
+        own_kernel(floor, q, k, v, *refs)
+
+    seen, gate_row, stacked, acc, stat = pl.pallas_call(
+        own,
+        out_shape=(
+            jax.ShapeDtypeStruct((spans, width), jnp.int32),
+            jax.ShapeDtypeStruct((1, wide), jnp.float32),
+            jax.ShapeDtypeStruct((kv_heads, width, HEAD_SIZE), jnp.bfloat16), acc_shape, stat_shape,
+        ),
+        in_specs=[pl.BlockSpec(memory_space=pltpu.SMEM)] * 2 + [VMEM] * 2 + [HBM] * 3,
+        out_specs=(VMEM,) * 5,
         scratch_shapes=[
             pltpu.VMEM(queries.shape, queries.dtype),
             pltpu.VMEM(keys.shape, keys.dtype),
@@ -206,7 +214,7 @@
         compiler_params=params,
         cost_estimate=cost(1, 10),
         name="own",
-    )(floor, queries, keys, values)
+    )(span_mask, section, section_gate, floor, queries, keys, values)
     for distance in range(1, spans):
         waiting = [(distance - 1, t) for t in turned] + [(distance, tuple(held))]
         forward = []
@@ -220,25 +228,7 @@
 
         count_in = 2 * len(waiting)
         blocks = [k for _, (k, _) in waiting] + [v for _, (_, v) in waiting]
-        if distance == 1:
-
-            def first_step(mask, section, gate, stacked, acc, stat, *refs, distances=distances):
-                flag_kernel(per_span, mask, section, gate, *refs[-2:])
-                step_kernel(distances, stacked, refs[-2], acc, stat, *refs[:-2])
-
-            acc, stat, seen, gate_row = pl.pallas_call(
-                first_step,
-                out_shape=(
-                    acc_shape, stat_shape, jax.ShapeDtypeStruct((spans, width), jnp.int32),
-                    jax.ShapeDtypeStruct((1, wide), jnp.float32),
-                ),
-                in_specs=[pl.BlockSpec(memory_space=pltpu.SMEM)] * 2 + [VMEM] * (4 + count_in),
-                out_specs=(VMEM,) * 4,
-                compiler_params=params,
-                cost_estimate=cost(len(waiting)),
-                name="step_1",
-            )(span_mask, section, section_gate, stacked, acc, stat, *blocks)
-        else:
+        if True:
 
             def step(*refs, distances=distances):
                 step_kernel(distances, *refs)

time: 29.6 us -> 28.5 us (0.963)
  the two profiles are of different devices: /device:TPU:16 before, /device:TPU:18 now
where the time goes in v8:
time: 28.5 us; the launch traced here: 28.3 us
  starting transfers between devices  14.9 us (52%)
  Pallas kernels  11 us (39%)
  waiting for transfers between devices  1.68 us (6%)
  between operations  0.77 us (3%)
    ppermute x14, starting transfers between devices, send(): return lax.ppermute(value, ('tm', 'head'), pairs)  14.9 us
    pallas_call x3, Pallas kernels, on_device(): pl.pallas_call(step, out_shape=(acc_shape, stat_shape), in_specs=[VMEM] *...  5.64 us
    pallas_call x1, Pallas kernels, on_device(): pl.pallas_call(own, out_shape=(jax.ShapeDtypeStruct((spans, width), jnp.i...  2.46 us
    pallas_call x1, Pallas kernels, on_device(): pl.pallas_call(close, out_shape=(jax.ShapeDtypeStruct((kv_heads, width, H...  1.69 us
    ppermute x14, waiting for transfers between devices, send(): return lax.ppermute(value, ('tm', 'head'), pairs)  1.68 us
    pallas_call x1, Pallas kernels, on_device(): pl.pallas_call(mix_kernel, out_shape=jax.ShapeDtypeStruct((rows, wide), j...  1.15 us
  transfers between devices with their start and end apart: 14, of which 5 were waited for; matrix products, arithmetic and copies ran while one was open for 0% of the time, Pallas kernels for 35%

profile of v8, /device:TPU:18, one launch (start us, length us, event | category | flops | bytes accessed | tf_op | source)
XLA Modules:
  0.0 28.3 jit_solution(9231318820043753317)
XLA Ops:
  0.6 0.0 copy-start.1
  0.6 0.0 copy-start.2
  0.7 0.0 copy-start.3
  0.7 0.0 copy-start.5
  0.7 0.0 copy-start.4
  0.7 0.0 copy-start
  0.7 1.6 %collective-permute-start.1 = (bf16[128,512]{1,0:T(8,128)(2,1)}, bf16[128,512]{1,0:T(8,128)(2,1)S(1)}, u32[]{:S(2)}, u32[]{:S(2)}) collective-permute-start(bf16[128,512]{1,0:T(8,128)(2,1)} %k.1), channel_id=1, source_target_pairs={{0,4},{1,5},{2,6},{3,7},{4,8},{5,9},{6,10},{7,11},{8,12},{9,13},{1... | collective-permute-start | bytes 393224 | tf_op jit(solution)/shard_map/ppermute | solution.py:160
  2.3 0.2 collective-permute-start
  2.5 0.0 copy-done.1
  2.5 1.5 %collective-permute-start.2 = (bf16[128,512]{1,0:T(8,128)(2,1)S(1)}, bf16[128,512]{1,0:T(8,128)(2,1)S(1)}, u32[]{:S(2)}, u32[]{:S(2)}) collective-permute-start(bf16[128,512]{1,0:T(8,128)(2,1)S(1)} %copy-done.1), channel_id=1, source_target_pairs={{0,2},{1,3},{2,0},{3,1},{4,6},{5,7},{6,4},{7,5},{8,10},{9,11},{10,... | collective-permute-start | bytes 393224 | tf_op jit(solution)/shard_map/ppermute | solution.py:160
  4.1 0.0 copy-done.2
  4.1 0.5 %collective-permute-start.3 = (bf16[128,512]{1,0:T(8,128)(2,1)S(1)}, bf16[128,512]{1,0:T(8,128)(2,1)S(1)}, u32[]{:S(2)}, u32[]{:S(2)}) collective-permute-start(bf16[128,512]{1,0:T(8,128)(2,1)S(1)} %copy-done.2), channel_id=1, source_target_pairs={{0,2},{1,3},{2,0},{3,1},{4,6},{5,7},{6,4},{7,5},{8,10},{9,11},{10,... | collective-permute-start | bytes 393224 | tf_op jit(solution)/shard_map/ppermute | solution.py:160
  4.6 0.0 copy-done.3
  4.6 0.0 copy-done.5
  4.6 0.0 copy-done.4
  4.6 0.0 copy-done
  4.6 2.5 %own.1 = (s32[4,768]{1,0:T(4,128)S(1)}, f32[1,3072]{1,0:T(1,128)S(1)}, bf16[4,768,128]{2,1,0:T(8,128)(2,1)S(1)}, f32[4,128,768]{2,1,0:T(8,128)S(1)}, f32[4,8,768]{2,1,0:T(8,128)S(1)}) custom-call(s32[4,4]{1,0:T(4,128)S(1)} %copy-done.4, s32[4]{0:T(128)S(1)} %copy-done.5, f32[4,3072]{1,0:T(4,128)S(1)} %copy-done.3, f32[8,768]{1,0:T(8,128)S(1)} %floor.1, ...), custom_call_target="tpu_custom_call" | custom-call | flops 2013265920 | bytes 3145728 | tf_op jit(solution)/shard_map/own/pallas_call | solution.py:199
  7.1 0.3 collective-permute-done.1.refs_5_
  7.3 1.6 %collective-permute-start.5 = (bf16[128,512]{1,0:T(8,128)(2,1)S(1)}, bf16[128,512]{1,0:T(8,128)(2,1)S(1)}, u32[]{:S(2)}, u32[]{:S(2)}) collective-permute-start(bf16[128,512]{1,0:T(8,128)(2,1)S(1)} %collective-permute-done.1.refs_5_), channel_id=1, source_target_pairs={{0,1},{1,0},{2,3},{3,2},{4,8},{5,9},{6,10},{7,11},{8,12},{9,13},{1... | collective-permute-start | bytes 393224 | tf_op jit(solution)/shard_map/ppermute | solution.py:160
  8.9 0.4 %collective-permute-done.refs_7_ = bf16[128,512]{1,0:T(8,128)(2,1)S(1)} collective-permute-done((bf16[128,512]{1,0:T(8,128)(2,1)}, bf16[128,512]{1,0:T(8,128)(2,1)S(1)}, u32[]{:S(2)}, u32[]{:S(2)}) %collective-permute-start) | collective-permute-done | bytes 131104 | tf_op jit(solution)/shard_map/ppermute | solution.py:160
  9.4 1.7 %collective-permute-start.4 = (bf16[128,512]{1,0:T(8,128)(2,1)S(1)}, bf16[128,512]{1,0:T(8,128)(2,1)S(1)}, u32[]{:S(2)}, u32[]{:S(2)}) collective-permute-start(bf16[128,512]{1,0:T(8,128)(2,1)S(1)} %collective-permute-done.refs_7_), channel_id=1, source_target_pairs={{0,1},{1,0},{2,3},{3,2},{4,8},{5,9},{6,10},{7,11},{8,12},{9,13},{1... | collective-permute-start | bytes 393224 | tf_op jit(solution)/shard_map/ppermute | solution.py:160
  11.1 1.5 %collective-permute-start.7 = (bf16[128,512]{1,0:T(8,128)(2,1)S(1)}, bf16[128,512]{1,0:T(8,128)(2,1)S(1)}, u32[]{:S(2)}, u32[]{:S(2)}) collective-permute-start(bf16[128,512]{1,0:T(8,128)(2,1)S(1)} %collective-permute-done.refs_7_), channel_id=1, source_target_pairs={{0,1},{1,0},{2,3},{3,2},{4,6},{5,7},{6,4},{7,5},{8,10},{9,11},{10,... | collective-permute-start | bytes 393224 | tf_op jit(solution)/shard_map/ppermute | solution.py:160
  12.6 0.0 collective-permute-done.2.refs_4_
  12.6 0.5 %collective-permute-start.6 = (bf16[128,512]{1,0:T(8,128)(2,1)S(1)}, bf16[128,512]{1,0:T(8,128)(2,1)S(1)}, u32[]{:S(2)}, u32[]{:S(2)}) collective-permute-start(bf16[128,512]{1,0:T(8,128)(2,1)S(1)} %collective-permute-done.1.refs_5_), channel_id=1, source_target_pairs={{0,1},{1,0},{2,3},{3,2},{4,6},{5,7},{6,4},{7,5},{8,10},{9,11},{10,... | collective-permute-start | bytes 393224 | tf_op jit(solution)/shard_map/ppermute | solution.py:160
  13.1 0.0 collective-permute-done.3.refs_6_
  13.1 1.9 %step_1.1 = (f32[4,128,768]{2,1,0:T(8,128)S(1)}, f32[4,8,768]{2,1,0:T(8,128)S(1)}) custom-call(bf16[4,768,128]{2,1,0:T(8,128)(2,1)S(1)} %get-tuple-element.33.refs_0_, s32[4,768]{1,0:T(4,128)S(1)} %get-tuple-element.34.refs_1_, f32[4,128,768]{2,1,0:T(8,128)S(1)} %get-tuple-element.35.refs_2_, f32[4,8,768]{2,1,0:T(8,128)S(1)} %get-tuple-element.38.refs_3_, ...), custom_call_target="tpu_custom_call" | custom-call | flops 805306368 | bytes 3145728 | tf_op jit(solution)/shard_map/step_1/pallas_call | solution.py:236
  15.0 0.0 collective-permute-done.5.refs_5_
  15.0 0.1 collective-permute-start.9
  15.1 0.0 collective-permute-done.4.refs_7_
  15.1 1.6 %collective-permute-start.11 = (bf16[128,512]{1,0:T(8,128)(2,1)S(1)}, bf16[128,512]{1,0:T(8,128)(2,1)S(1)}, u32[]{:S(2)}, u32[]{:S(2)}) collective-permute-start(bf16[128,512]{1,0:T(8,128)(2,1)S(1)} %collective-permute-done.4.refs_7_), channel_id=1, source_target_pairs={{0,1},{1,0},{2,3},{3,2},{4,5},{5,4},{6,7},{7,6},{8,10},{9,11},{10,... | collective-permute-start | bytes 393224 | tf_op jit(solution)/shard_map/ppermute | solution.py:160
  16.7 1.9 %collective-permute-start.8 = (bf16[128,512]{1,0:T(8,128)(2,1)S(1)}, bf16[128,512]{1,0:T(8,128)(2,1)S(1)}, u32[]{:S(2)}, u32[]{:S(2)}) collective-permute-start(bf16[128,512]{1,0:T(8,128)(2,1)S(1)} %collective-permute-done.4.refs_7_), channel_id=1, source_target_pairs={{0,1},{1,0},{2,3},{3,2},{4,5},{5,4},{6,7},{7,6},{8,12},{9,13},{10,... | collective-permute-start | bytes 393224 | tf_op jit(solution)/shard_map/ppermute | solution.py:160
  18.6 0.0 collective-permute-done.7.refs_6_
  18.6 0.5 %collective-permute-start.10 = (bf16[128,512]{1,0:T(8,128)(2,1)S(1)}, bf16[128,512]{1,0:T(8,128)(2,1)S(1)}, u32[]{:S(2)}, u32[]{:S(2)}) collective-permute-start(bf16[128,512]{1,0:T(8,128)(2,1)S(1)} %collective-permute-done.5.refs_5_), channel_id=1, source_target_pairs={{0,1},{1,0},{2,3},{3,2},{4,5},{5,4},{6,7},{7,6},{8,10},{9,11},{10,... | collective-permute-start | bytes 393224 | tf_op jit(solution)/shard_map/ppermute | solution.py:160
  19.1 0.1 collective-permute-done.6.refs_4_
  19.2 1.9 %step_2.1 = (f32[4,128,768]{2,1,0:T(8,128)S(1)}, f32[4,8,768]{2,1,0:T(8,128)S(1)}) custom-call(bf16[4,768,128]{2,1,0:T(8,128)(2,1)S(1)} %get-tuple-element.33.refs_0_, s32[4,768]{1,0:T(4,128)S(1)} %get-tuple-element.34.refs_1_, f32[4,128,768]{2,1,0:T(8,128)S(1)} %get-tuple-element.43.refs_2_, f32[4,8,768]{2,1,0:T(8,128)S(1)} %get-tuple-element.46.refs_3_, ...), custom_call_target="tpu_custom_call" | custom-call | flops 805306368 | bytes 3145728 | tf_op jit(solution)/shard_map/step_2/pallas_call | solution.py:236
  21.1 0.0 collective-permute-done.9.refs_5_
  21.1 0.1 collective-permute-start.12
  21.2 0.5 %collective-permute-done.11.refs_6_ = bf16[128,512]{1,0:T(8,128)(2,1)S(1)} collective-permute-done((bf16[128,512]{1,0:T(8,128)(2,1)S(1)}, bf16[128,512]{1,0:T(8,128)(2,1)S(1)}, u32[]{:S(2)}, u32[]{:S(2)}) %collective-permute-start.11) | collective-permute-done | bytes 131104 | tf_op jit(solution)/shard_map/ppermute | solution.py:160
  21.7 1.5 %collective-permute-start.13 = (bf16[128,512]{1,0:T(8,128)(2,1)S(1)}, bf16[128,512]{1,0:T(8,128)(2,1)S(1)}, u32[]{:S(2)}, u32[]{:S(2)}) collective-permute-start(bf16[128,512]{1,0:T(8,128)(2,1)S(1)} %collective-permute-done.11.refs_6_), channel_id=1, source_target_pairs={{0,1},{1,0},{2,3},{3,2},{4,5},{5,4},{6,7},{7,6},{8,12},{9,13},{10,... | collective-permute-start | bytes 393224 | tf_op jit(solution)/shard_map/ppermute | solution.py:160
  23.2 0.0 collective-permute-done.8.refs_7_
  23.2 0.4 %collective-permute-done.10.refs_4_ = bf16[128,512]{1,0:T(8,128)(2,1)S(1)} collective-permute-done((bf16[128,512]{1,0:T(8,128)(2,1)S(1)}, bf16[128,512]{1,0:T(8,128)(2,1)S(1)}, u32[]{:S(2)}, u32[]{:S(2)}) %collective-permute-start.10) | collective-permute-done | bytes 131104 | tf_op jit(solution)/shard_map/ppermute | solution.py:160
  23.6 1.9 %step_3.1 = (f32[4,128,768]{2,1,0:T(8,128)S(1)}, f32[4,8,768]{2,1,0:T(8,128)S(1)}) custom-call(bf16[4,768,128]{2,1,0:T(8,128)(2,1)S(1)} %get-tuple-element.33.refs_0_, s32[4,768]{1,0:T(4,128)S(1)} %get-tuple-element.34.refs_1_, f32[4,128,768]{2,1,0:T(8,128)S(1)} %get-tuple-element.49.refs_2_, f32[4,8,768]{2,1,0:T(8,128)S(1)} %get-tuple-element.52.refs_3_, ...), custom_call_target="tpu_custom_call" | custom-call | flops 805306368 | bytes 3145728 | tf_op jit(solution)/shard_map/step_3/pallas_call | solution.py:236
  25.5 0.0 collective-permute-done.12.refs_5_
  25.5 1.7 %close.1 = (f32[4,768,128]{2,1,0:T(8,128)S(1)}, bf16[4,768,128]{2,1,0:T(8,128)(2,1)S(1)}, f32[24,128]{1,0:T(8,128)}) custom-call(bf16[4,768,128]{2,1,0:T(8,128)(2,1)S(1)} %get-tuple-element.33.refs_0_, s32[4,768]{1,0:T(4,128)S(1)} %get-tuple-element.34.refs_1_, f32[1,3072]{1,0:T(1,128)S(1)} %get-tuple-element.32.refs_2_.gate_row, ...), custom_call_target="tpu_custom_call" | custom-call | flops 402653184 | bytes 3145728 | tf_op jit(solution)/shard_map/close/pallas_call | solution.py:251
  27.2 0.0 collective-permute-done.13.refs_0_
  27.2 1.2 %mix.1 = bf16[128,3072]{1,0:T(8,128)(2,1)} custom-call(f32[1,3072]{1,0:T(1,128)S(1)} %get-tuple-element.32.refs_2_.gate_row, f32[4,768,128]{2,1,0:T(8,128)S(1)} %get-tuple-element.57.part, bf16[4,768,128]{2,1,0:T(8,128)(2,1)S(1)} %get-tuple-element.58.last_weight, bf16[128,512]{1,0:T(8,128)(2,1)S(1)} %collective-permute-done.13.refs_0_), custom_call_target="tpu_custom_call" | custom-call | flops 402653184 | bytes 3145728 | tf_op jit(solution)/shard_map/mix/pallas_call | solution.py:264
  (1 shorter events, 0.0 us)
Async XLA Ops:
  0.6 1.9 %copy-start.1 = (bf16[128,512]{1,0:T(8,128)(2,1)S(1)}, bf16[128,512]{1,0:T(8,128)(2,1)}, u32[]{:S(2)}) copy-start(bf16[128,512]{1,0:T(8,128)(2,1)} %k.1) | copy-start | bytes 393220
  0.6 3.4 %copy-start.2 = (bf16[128,512]{1,0:T(8,128)(2,1)S(1)}, bf16[128,512]{1,0:T(8,128)(2,1)}, u32[]{:S(2)}) copy-start(bf16[128,512]{1,0:T(8,128)(2,1)} %v.1) | copy-start | bytes 393220
  0.7 3.9 %copy-start.3 = (f32[4,3072]{1,0:T(4,128)S(1)}, f32[4,3072]{1,0:T(4,128)}, u32[]{:S(2)}) copy-start(f32[4,3072]{1,0:T(4,128)} %gate.1) | copy-start | bytes 147460
  0.7 3.9 %copy-start.5 = (s32[4]{0:T(128)S(1)}, s32[4]{0:T(128)}, u32[]{:S(2)}) copy-start(s32[4]{0:T(128)} %section.1) | copy-start | bytes 52
  0.7 3.9 %copy-start.4 = (s32[4,4]{1,0:T(4,128)S(1)}, s32[4,4]{1,0:T(4,128)}, u32[]{:S(2)}) copy-start(s32[4,4]{1,0:T(4,128)} %mask.1) | copy-start | bytes 196
  0.7 3.9 %copy-start = (bf16[128,3072]{1,0:T(8,128)(2,1)S(1)}, bf16[128,3072]{1,0:T(8,128)(2,1)}, u32[]{:S(2)}) copy-start(bf16[128,3072]{1,0:T(8,128)(2,1)} %q.1) | copy-start | bytes 2359300
  0.7 6.6 %collective-permute-start.1 = (bf16[128,512]{1,0:T(8,128)(2,1)}, bf16[128,512]{1,0:T(8,128)(2,1)S(1)}, u32[]{:S(2)}, u32[]{:S(2)}) collective-permute-start(bf16[128,512]{1,0:T(8,128)(2,1)} %k.1), channel_id=1, source_target_pairs={{0,4},{1,5},{2,6},{3,7},{4,8},{5,9},{6,10},{7,11},{8,12},{9,13},{1... | collective-permute-start | bytes 393224 | tf_op jit(solution)/shard_map/ppermute | solution.py:160
  2.3 7.0 %collective-permute-start = (bf16[128,512]{1,0:T(8,128)(2,1)}, bf16[128,512]{1,0:T(8,128)(2,1)S(1)}, u32[]{:S(2)}, u32[]{:S(2)}) collective-permute-start(bf16[128,512]{1,0:T(8,128)(2,1)} %v.1), channel_id=1, source_target_pairs={{0,4},{1,5},{2,6},{3,7},{4,8},{5,9},{6,10},{7,11},{8,12},{9,13},{1... | collective-permute-start | bytes 393224 | tf_op jit(solution)/shard_map/ppermute | solution.py:160
  2.5 10.1 %collective-permute-start.2 = (bf16[128,512]{1,0:T(8,128)(2,1)S(1)}, bf16[128,512]{1,0:T(8,128)(2,1)S(1)}, u32[]{:S(2)}, u32[]{:S(2)}) collective-permute-start(bf16[128,512]{1,0:T(8,128)(2,1)S(1)} %copy-done.1), channel_id=1, source_target_pairs={{0,2},{1,3},{2,0},{3,1},{4,6},{5,7},{6,4},{7,5},{8,10},{9,11},{10,... | collective-permute-start | bytes 393224 | tf_op jit(solution)/shard_map/ppermute | solution.py:160
  4.1 9.0 %collective-permute-start.3 = (bf16[128,512]{1,0:T(8,128)(2,1)S(1)}, bf16[128,512]{1,0:T(8,128)(2,1)S(1)}, u32[]{:S(2)}, u32[]{:S(2)}) collective-permute-start(bf16[128,512]{1,0:T(8,128)(2,1)S(1)} %copy-done.2), channel_id=1, source_target_pairs={{0,2},{1,3},{2,0},{3,1},{4,6},{5,7},{6,4},{7,5},{8,10},{9,11},{10,... | collective-permute-start | bytes 393224 | tf_op jit(solution)/shard_map/ppermute | solution.py:160
  7.3 7.7 %collective-permute-start.5 = (bf16[128,512]{1,0:T(8,128)(2,1)S(1)}, bf16[128,512]{1,0:T(8,128)(2,1)S(1)}, u32[]{:S(2)}, u32[]{:S(2)}) collective-permute-start(bf16[128,512]{1,0:T(8,128)(2,1)S(1)} %collective-permute-done.1.refs_5_), channel_id=1, source_target_pairs={{0,1},{1,0},{2,3},{3,2},{4,8},{5,9},{6,10},{7,11},{8,12},{9,13},{1... | collective-permute-start | bytes 393224 | tf_op jit(solution)/shard_map/ppermute | solution.py:160
  9.4 5.7 %collective-permute-start.4 = (bf16[128,512]{1,0:T(8,128)(2,1)S(1)}, bf16[128,512]{1,0:T(8,128)(2,1)S(1)}, u32[]{:S(2)}, u32[]{:S(2)}) collective-permute-start(bf16[128,512]{1,0:T(8,128)(2,1)S(1)} %collective-permute-done.refs_7_), channel_id=1, source_target_pairs={{0,1},{1,0},{2,3},{3,2},{4,8},{5,9},{6,10},{7,11},{8,12},{9,13},{1... | collective-permute-start | bytes 393224 | tf_op jit(solution)/shard_map/ppermute | solution.py:160
  11.1 7.5 %collective-permute-start.7 = (bf16[128,512]{1,0:T(8,128)(2,1)S(1)}, bf16[128,512]{1,0:T(8,128)(2,1)S(1)}, u32[]{:S(2)}, u32[]{:S(2)}) collective-permute-start(bf16[128,512]{1,0:T(8,128)(2,1)S(1)} %collective-permute-done.refs_7_), channel_id=1, source_target_pairs={{0,1},{1,0},{2,3},{3,2},{4,6},{5,7},{6,4},{7,5},{8,10},{9,11},{10,... | collective-permute-start | bytes 393224 | tf_op jit(solution)/shard_map/ppermute | solution.py:160
  12.6 6.6 %collective-permute-start.6 = (bf16[128,512]{1,0:T(8,128)(2,1)S(1)}, bf16[128,512]{1,0:T(8,128)(2,1)S(1)}, u32[]{:S(2)}, u32[]{:S(2)}) collective-permute-start(bf16[128,512]{1,0:T(8,128)(2,1)S(1)} %collective-permute-done.1.refs_5_), channel_id=1, source_target_pairs={{0,1},{1,0},{2,3},{3,2},{4,6},{5,7},{6,4},{7,5},{8,10},{9,11},{10,... | collective-permute-start | bytes 393224 | tf_op jit(solution)/shard_map/ppermute | solution.py:160
  15.0 6.1 %collective-permute-start.9 = (bf16[128,512]{1,0:T(8,128)(2,1)S(1)}, bf16[128,512]{1,0:T(8,128)(2,1)S(1)}, u32[]{:S(2)}, u32[]{:S(2)}) collective-permute-start(bf16[128,512]{1,0:T(8,128)(2,1)S(1)} %collective-permute-done.5.refs_5_), channel_id=1, source_target_pairs={{0,1},{1,0},{2,3},{3,2},{4,5},{5,4},{6,7},{7,6},{8,12},{9,13},{10,... | collective-permute-start | bytes 393224 | tf_op jit(solution)/shard_map/ppermute | solution.py:160
  15.1 6.6 %collective-permute-start.11 = (bf16[128,512]{1,0:T(8,128)(2,1)S(1)}, bf16[128,512]{1,0:T(8,128)(2,1)S(1)}, u32[]{:S(2)}, u32[]{:S(2)}) collective-permute-start(bf16[128,512]{1,0:T(8,128)(2,1)S(1)} %collective-permute-done.4.refs_7_), channel_id=1, source_target_pairs={{0,1},{1,0},{2,3},{3,2},{4,5},{5,4},{6,7},{7,6},{8,10},{9,11},{10,... | collective-permute-start | bytes 393224 | tf_op jit(solution)/shard_map/ppermute | solution.py:160
  16.7 6.6 %collective-permute-start.8 = (bf16[128,512]{1,0:T(8,128)(2,1)S(1)}, bf16[128,512]{1,0:T(8,128)(2,1)S(1)}, u32[]{:S(2)}, u32[]{:S(2)}) collective-permute-start(bf16[128,512]{1,0:T(8,128)(2,1)S(1)} %collective-permute-done.4.refs_7_), channel_id=1, source_target_pairs={{0,1},{1,0},{2,3},{3,2},{4,5},{5,4},{6,7},{7,6},{8,12},{9,13},{10,... | collective-permute-start | bytes 393224 | tf_op jit(solution)/shard_map/ppermute | solution.py:160
  18.6 5.0 %collective-permute-start.10 = (bf16[128,512]{1,0:T(8,128)(2,1)S(1)}, bf16[128,512]{1,0:T(8,128)(2,1)S(1)}, u32[]{:S(2)}, u32[]{:S(2)}) collective-permute-start(bf16[128,512]{1,0:T(8,128)(2,1)S(1)} %collective-permute-done.5.refs_5_), channel_id=1, source_target_pairs={{0,1},{1,0},{2,3},{3,2},{4,5},{5,4},{6,7},{7,6},{8,10},{9,11},{10,... | collective-permute-start | bytes 393224 | tf_op jit(solution)/shard_map/ppermute | solution.py:160
  21.1 4.4 %collective-permute-start.12 = (bf16[128,512]{1,0:T(8,128)(2,1)S(1)}, bf16[128,512]{1,0:T(8,128)(2,1)S(1)}, u32[]{:S(2)}, u32[]{:S(2)}) collective-permute-start(bf16[128,512]{1,0:T(8,128)(2,1)S(1)} %collective-permute-done.9.refs_5_), channel_id=1, source_target_pairs={{0,1},{1,0},{2,3},{3,2},{4,5},{5,4},{6,7},{7,6},{8,9},{9,8},{10,11... | collective-permute-start | bytes 393224 | tf_op jit(solution)/shard_map/ppermute | solution.py:160
  21.7 5.5 %collective-permute-start.13 = (bf16[128,512]{1,0:T(8,128)(2,1)S(1)}, bf16[128,512]{1,0:T(8,128)(2,1)S(1)}, u32[]{:S(2)}, u32[]{:S(2)}) collective-permute-start(bf16[128,512]{1,0:T(8,128)(2,1)S(1)} %collective-permute-done.11.refs_6_), channel_id=1, source_target_pairs={{0,1},{1,0},{2,3},{3,2},{4,5},{5,4},{6,7},{7,6},{8,12},{9,13},{10,... | collective-permute-start | bytes 393224 | tf_op jit(solution)/shard_map/ppermute | solution.py:160
